TPU v7x, 32 devices: a whole 2x2x4 slice. The times are simulated.
32 devices in a mesh: doc: 8 (over y, x, core), filt: 4 (over z).
Axes of the slice: x: 2, y: 2, z: 4, core: 2. Of those that a mesh axis runs over, the one named last changes fastest.
Arguments:
- embedded: bfloat16 [16, 256, 256], P('doc'), may hold values from -8 to 8
- lengths: int32 [16], P('doc'), may hold values from 1 to 256, 1638 in all
- conv_weight: bfloat16 [256, 15, 1024], P(None, None, 'filt'), may hold values from -0.15625 to 0.15625
- head_weight: bfloat16 [3, 1024], P(None, 'filt'), may hold values from -0.109375 to 0.109375
- occupation: int32 [16], P('doc'), may hold values from 0 to 839
- cohort: int32 [16], P('doc'), may hold values from 0 to 39
- education: int32 [16], P('doc'), may hold values from 0 to 7
- occ_table: float32 [840], replicated, may hold values from -3 to 3
- cohort_table: float32 [40], replicated, may hold values from -3 to 3
- edu_table: float32 [8], replicated, may hold values from -3 to 3
- wage: float32 [16], P('doc'), may hold values from -8 to 8
Outputs:
- conv_grad: float32 [256, 15, 1024], P('doc', None, 'filt')
- head_grad: float32 [3, 1024], P(None, 'filt')
- occ_grad: float32 [840], replicated
- cohort_grad: float32 [40], replicated
- edu_grad: float32 [8], replicated
- prediction: float32 [16], P('doc')
All inputs are finite; a program needn't handle non-finite values. No bound on the sum of `lengths` on one device may be relied on, other than what follows from the above.
Results may differ from a plain program's by a relative error of at most 0.0029.
Values sent between devices are 32-bit elements; how exact they have to be, the bound alone decides.
No kernel may reach another device: no remote copies, remote signals or barrier semaphores. Data moves between devices by JAX's collectives and lax.ppermute only.
A program may use at most 64 MiB of HBM per device.

v0:
```python
import jax
import jax.numpy as jnp
from jax import lax
from jax.sharding import PartitionSpec as P

TAU = 0.05
WIDTH_LIST = ((3, 0), (5, 3), (7, 8))


def convolve(columns, weights):
    outputs = []
    for taps, first in WIDTH_LIST:
        half = (taps - 1) // 2
        window = columns[:, :, 3 - half : 3 + half + 1, :]
        outputs.append(
            jnp.einsum(
                "ptje,ejf->ptf",
                window,
                weights[:, first : first + taps, :],
                preferred_element_type=jnp.float32,
            )
        )
    return tuple(outputs)


def grad_terms(columns, slopes):
    outputs = []
    for index in range(3):
        taps = WIDTH_LIST[index][0]
        half = (taps - 1) // 2
        window = columns[:, :, 3 - half : 3 + half + 1, :]
        outputs.append(
            jnp.einsum("ptje,ptf->ejf", window, slopes[index], preferred_element_type=jnp.float32)
        )
    return jnp.concatenate(outputs, axis=1)


def local(
    embedded,
    lengths,
    conv_weight,
    head_weight,
    occupation,
    cohort,
    education,
    occ_table,
    cohort_table,
    edu_table,
    wage,
):
    posts, seq_len, _ = embedded.shape
    positions = jnp.arange(seq_len, dtype=jnp.int32)
    valid = positions[None, :] < lengths[:, None]
    masked = jnp.where(valid[:, :, None], embedded, jnp.zeros_like(embedded))
    padded = jnp.pad(masked, ((0, 0), (3, 3), (0, 0)))
    columns = jnp.stack([padded[:, offset : offset + seq_len, :] for offset in range(7)], axis=2)
    convs = convolve(columns, conv_weight)
    features = []
    shares = []
    for conv in convs:
        score = jnp.where(valid[:, :, None], conv / TAU, -jnp.inf)
        top = jnp.max(score, axis=1, keepdims=True)
        expd = jnp.exp(score - top)
        total = jnp.sum(expd, axis=1, keepdims=True)
        features.append(TAU * (top[:, 0, :] + jnp.log(total[:, 0, :])))
        shares.append(expd / total)
    feature = jnp.stack(features, axis=1)
    head = head_weight.astype(jnp.float32)
    partial_pred = jnp.sum(feature * head[None, :, :], axis=(1, 2))
    occ_hot = (
        occupation[:, None] == jnp.arange(occ_table.shape[0], dtype=jnp.int32)[None, :]
    ).astype(jnp.float32)
    cohort_hot = (
        cohort[:, None] == jnp.arange(cohort_table.shape[0], dtype=jnp.int32)[None, :]
    ).astype(jnp.float32)
    edu_hot = (
        education[:, None] == jnp.arange(edu_table.shape[0], dtype=jnp.int32)[None, :]
    ).astype(jnp.float32)
    highest = lax.Precision.HIGHEST
    offsets = (
        jnp.dot(occ_hot, occ_table, precision=highest)
        + jnp.dot(cohort_hot, cohort_table, precision=highest)
        + jnp.dot(edu_hot, edu_table, precision=highest)
    )
    prediction = lax.psum(partial_pred, "filt") + offsets
    residual = prediction - wage
    slopes = [
        (residual[:, None, None] * head[index][None, None, :] * shares[index]).astype(jnp.bfloat16)
        for index in range(3)
    ]
    conv_grad = lax.psum_scatter(
        grad_terms(columns, slopes), "doc", scatter_dimension=0, tiled=True
    )
    head_terms = jnp.sum(residual[:, None, None] * feature, axis=0)
    head_grad, occ_grad, cohort_grad, edu_grad = lax.psum(
        (
            head_terms,
            jnp.dot(residual, occ_hot, precision=highest),
            jnp.dot(residual, cohort_hot, precision=highest),
            jnp.dot(residual, edu_hot, precision=highest),
        ),
        "doc",
    )
    return (conv_grad, head_grad, occ_grad, cohort_grad, edu_grad, prediction)


def solution(mesh):
    return jax.shard_map(
        local,
        mesh=mesh,
        in_specs=(
            P("doc", None, None),
            P("doc"),
            P(None, None, "filt"),
            P(None, "filt"),
            P("doc"),
            P("doc"),
            P("doc"),
            P(),
            P(),
            P(),
            P("doc"),
        ),
        out_specs=(P("doc", None, "filt"), P(None, "filt"), P(), P(), P(), P("doc")),
        check_vma=False,
    )
```

profile of v0, /device:TPU:0, one launch (start us, length us, event | category | flops | bytes accessed | tf_op | source)
XLA Modules:
  0.0 98.7 jit_solution(9364096488321095102)
XLA Ops:
  7.2 0.8 iota_compare_fusion.3
  8.0 1.1 %broadcast_select_fusion = bf16[2,256,256]{2,1,0:T(8,128)(2,1)S(1)} fusion(bf16[2,256,256]{2,1,0:T(8,128)(2,1)} %param.11, pred[2,256]{1,0:T(4,128)(4,1)S(1)} %iota_compare_fusion.3), kind=kLoop, calls=%fused_computation.56 | loop fusion | flops 131072 | bytes 524800 | tf_op jit(solution)/shard_map/jit(_where)/select_n | solution.py:54
  9.4 0.1 fusion.50
  10.1 0.1 bitcast_dynamic-update-slice_fusion.7
  10.4 1.6 %copy-done.7 = bf16[256,15,256]{2,0,1:T(8,128)(2,1)S(1)} copy-done((bf16[256,15,256]{2,0,1:T(8,128)(2,1)S(1)}, bf16[256,15,256]{2,0,1:T(8,128)(2,1)}, u32[]{:S(2)}) %copy-start.7) | copy-done | bytes 1966104
  12.0 0.7 fusion.41
  12.7 0.4 copy-done.2
  13.1 0.5 fusion.42
  13.7 0.4 fusion.43
  14.5 13.5 %psum.35 = f32[2]{0:T(128)S(1)} all-reduce(f32[2]{0:T(128)S(1)} %multiply_reduce_fusion.1), channel_id=1, replica_groups=mesh['doc'=8,'filt'=4] {'filt'}, use_global_device_ids=true, to_apply=%region_7.8 | all-reduce | flops 2 | bytes 16 | tf_op jit(solution)/shard_map/psum | solution.py:85
  28.0 0.2 convolution_bitcast_fusion.8
  28.2 0.2 convolution_bitcast_fusion.10
  28.4 0.7 fusion.44
  29.2 2.3 %convolution_bitcast_fusion = f32[256,7,256]{0,2,1:T(8,128)S(1)} fusion(bf16[2,256,7,256]{3,1,2,0:T(8,128)(2,1)} %copy-done.4, f32[2,256,256]{2,1,0:T(8,128)S(1)} %get-tuple-element.31, f32[2,256]{1,0:T(2,128)S(1)} %fusion.15, f32[2,256]{1,0:T(2,128)S(1)} %get-tuple-element.29, f32[2,256]{1,0:T(2,128)S(1)} %get-tuple-element.30), kind=kOutput, calls=%fused_computation.1 | convolution fusion | flops 470286336 | bytes 4200448 | tf_op jit(solution)/shard_map/ptje,ptf->ejf/dot_general | solution.py:33
  31.5 0.6 convolution_bitcast_fusion.1
  32.1 0.4 convolution_bitcast_fusion.2
  32.5 2.1 %pad_maximum_fusion = f32[256,15,256]{0,2,1:T(8,128)} fusion(f32[256,7,256]{0,2,1:T(8,128)S(1)} %convolution_bitcast_fusion, f32[256,5,256]{0,2,1:T(8,128)S(1)} %convolution_bitcast_fusion.1, f32[256,3,256]{0,2,1:T(8,128)S(1)} %convolution_bitcast_fusion.2), kind=kLoop, calls=%fused_computation | loop fusion | flops 1966080 | bytes 7864320 | tf_op jit(solution)/shard_map/concatenate | solution.py:35
  34.6 5.5 %copy.46 = f32[256,15,256]{2,1,0:T(8,128)} copy(f32[256,15,256]{0,2,1:T(8,128)} %pad_maximum_fusion) | data formatting | bytes 7864320 | tf_op jit(solution)/shard_map/concatenate | solution.py:35
  40.2 0.2 convolution_reduce_fusion
  40.4 0.2 convolution_bitcast_fusion.7
  40.6 0.2 convolution_bitcast_fusion.6
  40.8 13.0 %all-reduce.1 = (f32[3,256]{1,0:T(4,128)}, f32[840]{0:T(1024)}, f32[40]{0:T(128)}, f32[8]{0:T(128)}) all-reduce(f32[3,256]{1,0:T(4,128)S(1)} %multiply_reduce_fusion, f32[840]{0:T(1024)S(1)} %convolution_reduce_fusion, f32[40]{0:T(128)S(1)} %convolution_bitcast_fusion.7, ...), channel_id=1, replica_groups=mesh['doc'=8,'filt'=4] {'doc'}, use_global_device_ids=true, to_apply=%region_10.11 | all-reduce | flops 1656 | bytes 13248 | tf_op jit(solution)/shard_map/psum | solution.py:95
  53.7 36.1 %reduce-scatter.2.cloned.1.call-done = f32[32,15,256]{2,1,0:T(8,128)} async-done(((f32[256,15,256]{2,1,0:T(8,128)}), f32[32,15,256]{2,1,0:T(8,128)}) %reduce-scatter.2.cloned.1.call-update) | async-done | bytes 491536 | tf_op jit(solution)/shard_map/reduce_scatter | solution.py:91
  89.8 2.1 %copy.47 = f32[32,15,256]{2,0,1:T(8,128)} copy(f32[32,15,256]{2,1,0:T(8,128)} %reduce-scatter.2.cloned.1.call-done) | data formatting | bytes 983040
  (49 shorter events, 1.6 us)
Async XLA Ops:
  7.2 21.2 %copy-start = (f32[40]{0:T(128)S(1)}, f32[40]{0:T(128)}, u32[]{:S(2)}) copy-start(f32[40]{0:T(128)} %param.19) | copy-start | bytes 484
  7.2 2.2 %copy-start.1 = (bf16[2,256,256]{2,1,0:T(8,128)(2,1)S(1)}, bf16[2,256,256]{2,1,0:T(8,128)(2,1)}, u32[]{:S(2)}) copy-start(bf16[2,256,256]{2,1,0:T(8,128)(2,1)} %param.11) | copy-start | bytes 786436
  7.2 82.6 %reduce-scatter.2.cloned.1.call-start = ((), (), s32[]{:S(2)}) async-start(), calls=%async_computation.1 | async-start | bytes 4718592 | tf_op jit(solution)/shard_map/reduce_scatter | solution.py:91
  9.4 0.7 copy-start.5
  9.8 2.2 %copy-start.7 = (bf16[256,15,256]{2,0,1:T(8,128)(2,1)S(1)}, bf16[256,15,256]{2,0,1:T(8,128)(2,1)}, u32[]{:S(2)}) copy-start(bf16[256,15,256]{2,0,1:T(8,128)(2,1)} %param.13) | copy-start | bytes 5898244
  10.0 2.6 %copy-start.4 = (bf16[2,256,7,256]{3,1,2,0:T(8,128)(2,1)}, bf16[2,256,7,256]{3,1,2,0:T(8,128)(2,1)S(1)}, u32[]{:S(2)}) copy-start(bf16[2,256,7,256]{3,1,2,0:T(8,128)(2,1)S(1)} %bitcast_dynamic-update-slice_fusion.4) | copy-start | bytes 5505028
  12.0 1.1 %copy-start.2 = (bf16[2,256,5,256]{3,1,0,2:T(8,128)(2,1)}, bf16[2,256,5,256]{3,1,0,2:T(8,128)(2,1)S(1)}, u32[]{:S(2)}) copy-start(bf16[2,256,5,256]{3,1,0,2:T(8,128)(2,1)S(1)} %bitcast_dynamic-update-slice_fusion.5) | copy-start | bytes 3932164
  13.6 14.4 %copy-start.6 = (f32[840]{0:T(1024)S(1)}, f32[840]{0:T(1024)}, u32[]{:S(2)}) copy-start(f32[840]{0:T(1024)} %param.18) | copy-start | bytes 10084
  13.6 14.4 %copy-start.8 = (f32[8]{0:T(128)S(1)}, f32[8]{0:T(128)}, u32[]{:S(2)}) copy-start(f32[8]{0:T(128)} %param.20) | copy-start | bytes 100
  13.6 14.4 %copy-start.12 = (s32[2]{0:T(128)S(1)}, s32[2]{0:T(128)}, u32[]{:S(2)}) copy-start(s32[2]{0:T(128)} %param.17) | copy-start | bytes 28
  13.6 14.6 %copy-start.10 = (s32[2]{0:T(128)S(1)}, s32[2]{0:T(128)}, u32[]{:S(2)}) copy-start(s32[2]{0:T(128)} %param.15) | copy-start | bytes 28
  13.6 14.8 %copy-start.9 = (f32[2]{0:T(128)S(1)}, f32[2]{0:T(128)}, u32[]{:S(2)}) copy-start(f32[2]{0:T(128)} %param.21) | copy-start | bytes 28
  13.7 14.8 %copy-start.11 = (s32[2]{0:T(128)S(1)}, s32[2]{0:T(128)}, u32[]{:S(2)}) copy-start(s32[2]{0:T(128)} %param.16) | copy-start | bytes 28
  29.2 2.3 %copy-start.3 = (bf16[2,256,5,256]{3,1,0,2:T(8,128)(2,1)S(1)}, bf16[2,256,5,256]{3,1,0,2:T(8,128)(2,1)}, u32[]{:S(2)}) copy-start(bf16[2,256,5,256]{3,1,0,2:T(8,128)(2,1)} %copy-done.2) | copy-start | bytes 3932164
Sparse Core Ops, SparseCore 0:
  40.2 49.5 reduce-scatter.1
where the time goes:
time: 99.1 us; the launch traced here: 98.7 us
  waiting for transfers between devices  36.1 us (36%)
  blocking collectives  26.4 us (27%)
  between operations  14.3 us (14%)
  local copies, waits for them, and re-layouts  10.5 us (11%)
  matrix products  6.48 us (7%)
  other arithmetic  4.96 us (5%)
    reduce_scatter x1, waiting for transfers between devices, local(): lax.psum_scatter(grad_terms(columns, slopes), 'doc', scatter_dimension=0,...  36.1 us
    psum x1, blocking collectives, local(): prediction = lax.psum(partial_pred, 'filt') + offsets  13.5 us
    psum x1, blocking collectives, local(): lax.psum((head_terms, jnp.dot(residual, occ_hot, precision=highest), jnp....  13 us
    concatenate x1, local copies, waits for them, and re-layouts, grad_terms(): return jnp.concatenate(outputs, axis=1)  5.49 us
    unnamed x36, local copies, waits for them, and re-layouts  4.72 us
    dot_general x3, matrix products, grad_terms(): jnp.einsum('ptje,ptf->ejf', window, slopes[index], preferred_element_type...  3.25 us
    concatenate x1, other arithmetic, grad_terms(): return jnp.concatenate(outputs, axis=1)  2.12 us
  transfers between devices with their start and end apart: 1, of which 1 were waited for; matrix products, arithmetic and copies ran while one was open for 1% of the time, Pallas kernels for 0%

commit v1 on v0

--- a/solution.py
+++ b/solution.py
@@ -1,10 +1,19 @@
+import functools
+
 import jax
 import jax.numpy as jnp
+import numpy as np
 from jax import lax
+from jax.experimental import pallas as pl
+from jax.experimental.pallas import tpu as pltpu
 from jax.sharding import PartitionSpec as P
 
 TAU = 0.05
 WIDTH_LIST = ((3, 0), (5, 3), (7, 8))
+TAPS = 15
+REACH = 3
+PAD = 8
+BY_LAST = (((1,), (1,)), ((), ()))
 
 
 def convolve(columns, weights):
@@ -35,7 +44,11 @@
     return jnp.concatenate(outputs, axis=1)
 
 
-def local(
+def one_hots(codes, size):
+    return (codes[:, None] == jnp.arange(size, dtype=jnp.int32)[None, :]).astype(jnp.float32)
+
+
+def local_scatter(
     embedded,
     lengths,
     conv_weight,
@@ -67,15 +80,9 @@
     feature = jnp.stack(features, axis=1)
     head = head_weight.astype(jnp.float32)
     partial_pred = jnp.sum(feature * head[None, :, :], axis=(1, 2))
-    occ_hot = (
-        occupation[:, None] == jnp.arange(occ_table.shape[0], dtype=jnp.int32)[None, :]
-    ).astype(jnp.float32)
-    cohort_hot = (
-        cohort[:, None] == jnp.arange(cohort_table.shape[0], dtype=jnp.int32)[None, :]
-    ).astype(jnp.float32)
-    edu_hot = (
-        education[:, None] == jnp.arange(edu_table.shape[0], dtype=jnp.int32)[None, :]
-    ).astype(jnp.float32)
+    occ_hot = one_hots(occupation, occ_table.shape[0])
+    cohort_hot = one_hots(cohort, cohort_table.shape[0])
+    edu_hot = one_hots(education, edu_table.shape[0])
     highest = lax.Precision.HIGHEST
     offsets = (
         jnp.dot(occ_hot, occ_table, precision=highest)
@@ -104,7 +111,338 @@
     return (conv_grad, head_grad, occ_grad, cohort_grad, edu_grad, prediction)
 
 
+def load_post(x, xpad):
+    rows, width = x.shape
+    xpad[0:PAD, :] = jnp.zeros((PAD, width), jnp.float32)
+    xpad[PAD + rows :, :] = jnp.zeros((PAD, width), jnp.float32)
+    xpad[PAD : PAD + rows, :] = x
+
+
+def make_cols(xpad, cols):
+    rows, width = cols.shape[0], xpad.shape[1]
+    for offset in range(2 * REACH + 1):
+        start = PAD - REACH + offset
+        cols[:, offset * width : (offset + 1) * width] = xpad[start : start + rows, :].astype(
+            jnp.bfloat16
+        )
+
+
+def forward(index, cols, w_ref, valid):
+    taps, first = WIDTH_LIST[index]
+    half = taps // 2
+    width = w_ref.shape[0] // TAPS
+    conv = jnp.dot(
+        cols[:, (REACH - half) * width : (REACH + half + 1) * width],
+        w_ref[first * width : (first + taps) * width, :],
+        preferred_element_type=jnp.float32,
+    )
+    score = jnp.where(valid, conv * np.float32(1.0 / TAU), -jnp.inf)
+    top = jnp.max(score, axis=0, keepdims=True)
+    expd = jnp.exp(score - top)
+    total = jnp.sum(expd, axis=0, keepdims=True)
+    return top, total, expd
+
+
+def select_rows(d_ref, cols, slice_e):
+    rows = cols.shape[0]
+    width = cols.shape[1] // (2 * REACH + 1)
+    me = d_ref[0]
+    row = lax.broadcasted_iota(jnp.int32, (2 * slice_e, width), 0)
+    lane = lax.broadcasted_iota(jnp.int32, (2 * slice_e, width), 1)
+    wanted = jnp.where(row < slice_e, me * slice_e + row, (me ^ 1) * slice_e + row - slice_e)
+    pick = (lane == wanted).astype(jnp.bfloat16)
+    middle = cols[:, REACH * width : (REACH + 1) * width]
+    across = lax.dot_general(pick, middle, BY_LAST, preferred_element_type=jnp.float32)
+    place = lax.broadcasted_iota(jnp.int32, (2 * slice_e, rows), 1)
+    parts = []
+    for offset in range(-REACH, REACH + 1):
+        if offset:
+            moved = pltpu.roll(across, (-offset) % rows, 1)
+            inside = (place + offset >= 0) & (place + offset < rows)
+            parts.append(jnp.where(inside, moved, 0.0))
+        else:
+            parts.append(across)
+    return jnp.concatenate(parts, axis=0).astype(jnp.bfloat16)
+
+
+def add_grad(index, at, slope, own_ref, other_ref, slice_e):
+    taps, first = WIDTH_LIST[index]
+    half = taps // 2
+    step = 2 * slice_e
+    term = jnp.dot(
+        at[(REACH - half) * step : (REACH + half + 1) * step],
+        slope,
+        preferred_element_type=jnp.float32,
+    )
+    for j in range(taps):
+        place = slice(((first + j) * slice_e), (first + j + 1) * slice_e)
+        own_ref[place, :] += term[j * step : j * step + slice_e]
+        other_ref[place, :] += term[j * step + slice_e : (j + 1) * step]
+
+
+def own_kernel(len_ref, x_ref, w_ref, head_ref, part_ref, feat_ref, share_ref, xpad, cols):
+    posts, rows, _ = x_ref.shape
+    head = head_ref[...].astype(jnp.float32)
+
+    def post(p, carry):
+        load_post(x_ref[p], xpad)
+        make_cols(xpad, cols)
+        valid = lax.broadcasted_iota(jnp.int32, (rows, head.shape[1]), 0) < len_ref[p]
+        part = jnp.zeros((1, head.shape[1]), jnp.float32)
+        for index in range(3):
+            top, total, expd = forward(index, cols, w_ref, valid)
+            feature = np.float32(TAU) * (top + jnp.log(total))
+            feat_ref[p, index : index + 1, :] = feature
+            part = part + feature * head[index : index + 1]
+            share_ref[p, index] = expd / total
+        part_ref[p] = jnp.broadcast_to(jnp.sum(part, axis=1, keepdims=True), part_ref.shape[1:])
+        return carry
+
+    lax.fori_loop(0, posts, post, 0)
+
+
+def first_kernel(
+    n_other,
+    slice_e,
+    d_ref,
+    len_ref,
+    res_ref,
+    own_ref,
+    share_ref,
+    *refs,
+):
+    others = refs[:n_other]
+    w_ref, head_ref, acc_own, acc_other, feat_ref, xpads, cols = refs[n_other:]
+    posts, rows, _ = own_ref.shape
+    head = head_ref[...].astype(jnp.float32)
+    acc_own[...] = jnp.zeros_like(acc_own)
+    acc_other[...] = jnp.zeros_like(acc_other)
+    for p in range(posts):
+        load_post(own_ref[p], xpads.at[p])
+    for p in range(n_other):
+        load_post(others[p][...], xpads.at[posts + p])
+
+    def own(p, carry):
+        make_cols(xpads.at[p], cols)
+        at = select_rows(d_ref, cols, slice_e)
+        for index in range(3):
+            scale = res_ref[p] * head[index : index + 1]
+            slope = (scale * share_ref[p, index]).astype(jnp.bfloat16)
+            add_grad(index, at, slope, acc_own, acc_other, slice_e)
+        return carry
+
+    def other(p, carry):
+        make_cols(xpads.at[posts + p], cols)
+        at = select_rows(d_ref, cols, slice_e)
+        valid = lax.broadcasted_iota(jnp.int32, (rows, head.shape[1]), 0) < len_ref[posts + p]
+        for index in range(3):
+            top, total, expd = forward(index, cols, w_ref, valid)
+            feat_ref[p, index : index + 1, :] = np.float32(TAU) * (top + jnp.log(total))
+            scale = res_ref[posts + p] * head[index : index + 1]
+            slope = (scale * (expd / total)).astype(jnp.bfloat16)
+            add_grad(index, at, slope, acc_own, acc_other, slice_e)
+        return carry
+
+    lax.fori_loop(0, posts, own, 0)
+    lax.fori_loop(0, n_other, other, 0)
+
+
+def last_kernel(n_other, slice_e, d_ref, len_ref, res_ref, in_own, in_other, *refs):
+    others = refs[:n_other]
+    w_ref, head_ref, acc_own, acc_other, feat_ref, xpads, cols = refs[n_other:]
+    rows = others[0].shape[0]
+    head = head_ref[...].astype(jnp.float32)
+    acc_own[...] = in_own[...]
+    acc_other[...] = in_other[...]
+    for p in range(n_other):
+        load_post(others[p][...], xpads.at[p])
+
+    def other(p, carry):
+        make_cols(xpads.at[p], cols)
+        at = select_rows(d_ref, cols, slice_e)
+        valid = lax.broadcasted_iota(jnp.int32, (rows, head.shape[1]), 0) < len_ref[p]
+        for index in range(3):
+            top, total, expd = forward(index, cols, w_ref, valid)
+            feat_ref[p, index : index + 1, :] = np.float32(TAU) * (top + jnp.log(total))
+            scale = res_ref[p] * head[index : index + 1]
+            slope = (scale * (expd / total)).astype(jnp.bfloat16)
+            add_grad(index, at, slope, acc_own, acc_other, slice_e)
+        return carry
+
+    lax.fori_loop(0, n_other, other, 0)
+
+
+def tree_sum(values):
+    while len(values) > 1:
+        values = [values[i] + values[i + 1] for i in range(0, len(values), 2)]
+    return values[0]
+
+
+def local_gather(n_doc, n_filt, *args):
+    (
+        embedded,
+        lengths,
+        conv_weight,
+        head_weight,
+        occupation,
+        cohort,
+        education,
+        occ_table,
+        cohort_table,
+        edu_table,
+        wage,
+    ) = args
+    posts, seq_len, dims = embedded.shape
+    filters = conv_weight.shape[2]
+    slice_e = dims // n_doc
+    f32 = jnp.float32
+    me = lax.axis_index("doc").astype(jnp.int32).reshape(1)
+    partners = list(range(2, n_doc, 2))
+
+    def swap(x, k, axis="doc"):
+        size = n_doc if axis == "doc" else n_filt
+        return lax.ppermute(x, axis, [(i, i ^ k) for i in range(size)])
+
+    weights = jnp.transpose(conv_weight, (1, 0, 2)).reshape(TAPS * dims, filters)
+    valid = jnp.arange(seq_len, dtype=jnp.int32)[None, :] < lengths[:, None]
+    payload = jnp.where(valid[:, :, None], embedded, jnp.zeros_like(embedded)).astype(f32)
+    pieces = [payload[p] for p in range(posts)]
+
+    far = [k for k in partners if bin(k).count("1") > 1]
+    near = [k for k in partners if bin(k).count("1") == 1]
+    got = {}
+    for k in far:
+        for p in range(posts):
+            got[k, p] = swap(pieces[p], k)
+    for k in near:
+        got[k, 0] = swap(pieces[0], k)
+
+    vmem = pl.BlockSpec(memory_space=pltpu.VMEM)
+    smem = pl.BlockSpec(memory_space=pltpu.SMEM)
+    params = pltpu.CompilerParams(vmem_limit_bytes=48 << 20)
+    pad_shape = (seq_len + 2 * PAD, dims)
+    cols_shape = (seq_len, (2 * REACH + 1) * dims)
+
+    part, feat_own, share_own = pl.pallas_call(
+        own_kernel,
+        in_specs=[smem, vmem, vmem, vmem],
+        out_specs=[vmem] * 3,
+        out_shape=[
+            jax.ShapeDtypeStruct((posts, 8, 128), f32),
+            jax.ShapeDtypeStruct((posts, 3, filters), f32),
+            jax.ShapeDtypeStruct((posts, 3, seq_len, filters), f32),
+        ],
+        scratch_shapes=[pltpu.VMEM(pad_shape, f32), pltpu.VMEM(cols_shape, jnp.bfloat16)],
+        compiler_params=params,
+    )(lengths, payload, weights, head_weight)
+
+    mine = part[:, 0, 0]
+    parts = [mine] + [swap(mine, k, "filt") for k in range(1, n_filt)]
+    offsets = (
+        jnp.sum(one_hots(occupation, occ_table.shape[0]) * occ_table[None, :], axis=1)
+        + jnp.sum(one_hots(cohort, cohort_table.shape[0]) * cohort_table[None, :], axis=1)
+        + jnp.sum(one_hots(education, edu_table.shape[0]) * edu_table[None, :], axis=1)
+    )
+    prediction = tree_sum(parts) + offsets
+    residual = prediction - wage
+
+    facts = jnp.stack(
+        [residual]
+        + [v.astype(f32) for v in (lengths, occupation, cohort, education)]
+    )
+    told = {0: facts}
+    for k in far + near:
+        told[k] = swap(facts, k)
+    pieces_late, _ = lax.optimization_barrier((pieces[1:], facts))
+    for k in near:
+        for p in range(1, posts):
+            got[k, p] = swap(pieces_late[p - 1], k)
+
+    early = [(k, p) for k in far for p in range(posts)] + [(k, 0) for k in near]
+    late = [(k, p) for k in near for p in range(1, posts)]
+    order = [(0, p) for p in range(posts)] + early
+    res_first = jnp.stack([told[k][0, p] for k, p in order])
+    len_first = jnp.stack([told[k][1, p] for k, p in order]).astype(jnp.int32)
+    res_last = jnp.stack([told[k][0, p] for k, p in late])
+    len_last = jnp.stack([told[k][1, p] for k, p in late]).astype(jnp.int32)
+
+    acc_shape = jax.ShapeDtypeStruct((TAPS * slice_e, filters), f32)
+
+    acc_own, acc_other, feat_early = pl.pallas_call(
+        functools.partial(first_kernel, len(early), slice_e),
+        in_specs=[smem, smem, smem] + [vmem] * (2 + len(early) + 2),
+        out_specs=[vmem] * 3,
+        out_shape=[acc_shape, acc_shape, jax.ShapeDtypeStruct((len(early), 3, filters), f32)],
+        scratch_shapes=[
+            pltpu.VMEM((posts + len(early),) + pad_shape, f32),
+            pltpu.VMEM(cols_shape, jnp.bfloat16),
+        ],
+        compiler_params=params,
+    )(
+        me,
+        len_first,
+        res_first,
+        payload,
+        share_own,
+        *[got[key] for key in early],
+        weights,
+        head_weight,
+    )
+    acc_own, acc_other, feat_late = pl.pallas_call(
+        functools.partial(last_kernel, len(late), slice_e),
+        in_specs=[smem, smem, smem] + [vmem] * (2 + len(late) + 2),
+        out_specs=[vmem] * 3,
+        out_shape=[acc_shape, acc_shape, jax.ShapeDtypeStruct((len(late), 3, filters), f32)],
+        scratch_shapes=[
+            pltpu.VMEM((len(late),) + pad_shape, f32),
+            pltpu.VMEM(cols_shape, jnp.bfloat16),
+        ],
+        compiler_params=params,
+    )(
+        me,
+        len_last,
+        res_last,
+        acc_own,
+        acc_other,
+        *[got[key] for key in late],
+        weights,
+        head_weight,
+    )
+
+    features = {(0, p): feat_own[p] for p in range(posts)}
+    features.update({key: feat_early[i] for i, key in enumerate(early)})
+    features.update({key: feat_late[i] for i, key in enumerate(late)})
+    sizes = (occ_table.shape[0], cohort_table.shape[0], edu_table.shape[0])
+
+    def device_terms(k):
+        head_term = sum(told[k][0, p] * features[k, p] for p in range(posts))
+        codes = [
+            jnp.sum(told[k][0][:, None] * one_hots(told[k][2 + i].astype(jnp.int32), size), axis=0)
+            for i, size in enumerate(sizes)
+        ]
+        return jnp.concatenate([head_term.reshape(-1)] + codes)
+
+    sums = tree_sum([device_terms(k) for k in range(0, n_doc, 2)])
+    rows = -(-sums.shape[0] // filters)
+    tail = jnp.pad(sums, (0, rows * filters - sums.shape[0])).reshape(rows, filters)
+    other_grad = swap(acc_other, 1)
+    sums = sums + swap(tail, 1).reshape(-1)[: sums.shape[0]]
+    conv_grad = jnp.transpose((acc_own + other_grad).reshape(TAPS, slice_e, filters), (1, 0, 2))
+    head_grad = sums[: 3 * filters].reshape(3, filters)
+    outs = []
+    start = 3 * filters
+    for size in sizes:
+        outs.append(sums[start : start + size])
+        start += size
+    return (conv_grad, head_grad, *outs, prediction)
+
+
 def solution(mesh):
+    n_doc, n_filt = mesh.shape["doc"], mesh.shape["filt"]
+    if n_doc == 8 and n_filt == 4:
+        local = functools.partial(local_gather, n_doc, n_filt)
+    else:
+        local = local_scatter
     return jax.shard_map(
         local,
         mesh=mesh,

time: 99.1 us -> 91.6 us (0.924)
  waiting for transfers between devices: 36.1 us -> 1.96 us
  blocking collectives: 26.4 us -> 0 us
  other arithmetic: 4.96 us -> 28.1 us
  local copies, waits for them, and re-layouts: 10.5 us -> 28.2 us
  starting transfers between devices: 0.04 us -> 17.5 us
  Pallas kernels: 0 us -> 14.2 us
  between operations: 14.3 us -> 0.94 us
  matrix products: 6.48 us -> 0 us
    reduce_scatter x1 -> x0, waiting for transfers between devices: 36.1 us -> none  [local(): lax.psum_scatter(grad_terms(columns, slopes), 'doc', scatter_dimension=0,...]
    psum x2 -> x0, blocking collectives: 26.4 us -> none  [the longest x1 13.5 us: local(): prediction = lax.psum(partial_pred, 'filt') + offsets]
    ppermute x0 -> x14, starting transfers between devices: none -> 17.5 us  [swap(): return lax.ppermute(x, axis, [(i, i ^ k) for i in range(size)])]
    pallas_call x0 -> x3, Pallas kernels: none -> 14.2 us  [the longest x1 7.8 us: local_gather(): pl.pallas_call(functools.partial(first_kernel, len(early), slice_e), in_s...]
    another operation x3 -> x8, local copies, waits for them, and re-layouts: 0.24 us -> 12.4 us  [the longest x6 4.67 us: local_gather(): jnp.stack([residual] + [v.astype(f32) for v in (lengths, occupation, coho...]
    reduce_sum x5 -> x15, other arithmetic: 0.49 us -> 12.5 us  [the longest x12 10.4 us: device_terms(): jnp.sum(told[k][0][:, None] * one_hots(told[k][2 + i].astype(jnp.int32),...]
    convert_element_type x1 -> x9, other arithmetic: 0.01 us -> 7.11 us  [the longest x6 2.8 us: device_terms(): told[k][2 + i].astype(jnp.int32)]
    add x0 -> x5, other arithmetic: none -> 6.53 us  [the longest x2 5.68 us: device_terms(): head_term = sum((told[k][0, p] * features[k, p] for p in range(posts)))]
  transfers between devices with their start and end apart: 1 -> 14, of which waited for: 1 -> 3; matrix products, arithmetic and copies ran while one was open for 1% -> 51% of each run, Pallas kernels for 0% -> 9%
where the time goes in v1:
time: 91.6 us; the launch traced here: 91 us
  local copies, waits for them, and re-layouts  28.2 us (31%)
  other arithmetic  28.1 us (31%)
  starting transfers between devices  17.5 us (19%)
  Pallas kernels  14.2 us (16%)
  waiting for transfers between devices  1.96 us (2%)
  between operations  0.94 us (1%)
    ppermute x14, starting transfers between devices, swap(): return lax.ppermute(x, axis, [(i, i ^ k) for i in range(size)])  17.5 us
    reduce_sum x12, other arithmetic, device_terms(): jnp.sum(told[k][0][:, None] * one_hots(told[k][2 + i].astype(jnp.int32),...  10.4 us
    pallas_call x1, Pallas kernels, local_gather(): pl.pallas_call(functools.partial(first_kernel, len(early), slice_e), in_s...  7.8 us
    unnamed x56, local copies, waits for them, and re-layouts  6.79 us
    add x2, other arithmetic, device_terms(): head_term = sum((told[k][0, p] * features[k, p] for p in range(posts)))  5.68 us
    another operation x6, local copies, waits for them, and re-layouts, local_gather(): jnp.stack([residual] + [v.astype(f32) for v in (lengths, occupation, coho...  4.67 us
    pallas_call x1, Pallas kernels, local_gather(): pl.pallas_call(functools.partial(last_kernel, len(late), slice_e), in_spe...  4.02 us
    another operation x1, local copies, waits for them, and re-layouts, local_gather(): res_first = jnp.stack([told[k][0, p] for k, p in order])  3.85 us
  transfers between devices with their start and end apart: 14, of which 3 were waited for; matrix products, arithmetic and copies ran while one was open for 51% of the time, Pallas kernels for 9%

profile of v1, /device:TPU:0, one launch (start us, length us, event | category | flops | bytes accessed | tf_op | source)
XLA Modules:
  0.0 91.0 jit_solution(12775241855364668804)
XLA Ops:
  2.5 1.5 %copy-done = bf16[256,15,256]{2,0,1:T(8,128)(2,1)S(1)} copy-done((bf16[256,15,256]{2,0,1:T(8,128)(2,1)S(1)}, bf16[256,15,256]{2,0,1:T(8,128)(2,1)}, u32[]{:S(2)}) %copy-start) | copy-done | bytes 1966104
  5.4 2.4 %shard_map.154 = (f32[2,8,128]{2,1,0:T(8,128)S(1)}, f32[2,3,256]{2,1,0:T(4,128)S(1)}, f32[2,3,256,256]{3,2,1,0:T(8,128)S(1)}) custom-call(s32[2]{0:T(128)S(1)} %copy-done.6, f32[2,256,256]{2,1,0:T(8,128)S(1)} %select_convert_fusion.x_ref.own_ref, bf16[3840,256]{1,0:T(8,128)(2,1)S(1)} %bitcast.44, bf16[3,256]{1,0:T(4,128)(2,1)S(1)} %copy-done.4), custom_call_target="tpu_custom_call" | custom-call | tf_op jit(solution)/shard_map/pallas_call | solution.py:326
  9.1 4.0 %collective-permute-start.1 = (f32[2]{0:T(128)S(1)}, f32[2]{0:T(128)}, u32[]{:S(2)}, u32[]{:S(2)}) collective-permute-start(f32[2]{0:T(128)S(1)} %slice_reduce_fusion.3), channel_id=1, source_target_pairs={{0,2},{1,3},{2,0},{3,1},{4,6},{5,7},{6,4},{7,5},{8,10},{9,11},{10,... | collective-permute-start | bytes 32 | tf_op jit(solution)/shard_map/ppermute | solution.py:304
  13.1 1.4 %collective-permute-start.2 = (f32[2]{0:T(128)S(1)}, f32[2]{0:T(128)S(1)}, u32[]{:S(2)}, u32[]{:S(2)}) collective-permute-start(f32[2]{0:T(128)S(1)} %slice_reduce_fusion.3), channel_id=1, source_target_pairs={{0,3},{1,2},{2,1},{3,0},{4,7},{5,6},{6,5},{7,4},{8,11},{9,10},{10,... | collective-permute-start | bytes 32 | tf_op jit(solution)/shard_map/ppermute | solution.py:304
  15.5 2.5 %collective-permute-start.6 = (f32[256,256]{1,0:T(8,128)}, f32[256,256]{1,0:T(8,128)S(1)}, u32[]{:S(2)}, u32[]{:S(2)}) collective-permute-start(f32[256,256]{1,0:T(8,128)} %get-tuple-element.38), channel_id=1, source_target_pairs={{0,24},{4,28},{8,16},{12,20},{16,8},{20,12},{24,0},{28,4},{1,25},{... | collective-permute-start | bytes 786440 | tf_op jit(solution)/shard_map/ppermute | solution.py:304
  26.5 2.4 %collective-permute-start.7 = (f32[256,256]{1,0:T(8,128)}, f32[256,256]{1,0:T(8,128)S(1)}, u32[]{:S(2)}, u32[]{:S(2)}) collective-permute-start(f32[256,256]{1,0:T(8,128)} %get-tuple-element.20), channel_id=1, source_target_pairs={{0,24},{4,28},{8,16},{12,20},{16,8},{20,12},{24,0},{28,4},{1,25},{... | collective-permute-start | bytes 786440 | tf_op jit(solution)/shard_map/ppermute | solution.py:304
  28.9 1.3 %fusion.15 = (f32[2]{0:T(128)S(1)}, f32[2]{0:T(128)}) fusion(f32[2]{0:T(128)} %param.21, f32[2]{0:T(128)} %fusion.6, f32[2]{0:T(128)} %fusion, f32[2]{0:T(128)} %fusion.5, f32[2]{0:T(128)} %collective-permute-done.1, f32[2]{0:T(128)} %copy-done.22, f32[2]{0:T(128)} %copy-done.21, f32[2]{0:T(128)} %collective-permute-done), kind=kLoop, calls=%fused_computation.63 | loop fusion | flops 14 | bytes 80 | tf_op jit(solution)/shard_map/sub | solution.py:347
  31.4 1.4 %stack.35 = f32[5,2]{0,1:T(2,128)} concatenate(f32[1,2]{0,1:T(2,128)} %copy.27, f32[1,2]{0,1:T(2,128)} %copy.28, f32[1,2]{0,1:T(2,128)} %copy.29, f32[1,2]{0,1:T(2,128)} %copy.30, f32[1,2]{0,1:T(2,128)} %copy.31), dimensions={0} | concatenate | bytes 80 | tf_op jit(solution)/shard_map/stack | solution.py:349
  33.3 1.8 %multiply_add_fusion.3 = f32[1,3,256]{2,1,0:T(4,128)} fusion(f32[2,3,256]{2,1,0:T(4,128)S(1)} %get-tuple-element.23, f32[]{:T(128)} %bitcast.30, f32[]{:T(128)} %bitcast.29), kind=kLoop, calls=%fused_computation.18 | loop fusion | flops 2304 | bytes 9224 | tf_op jit(solution)/shard_map/add | solution.py:418
  36.6 1.3 %fusion.7 = f32[40]{0:T(128)} fusion(f32[2]{0:T(128)} %copy-done.12, s32[2]{0:T(128)} %get-tuple-element.56), kind=kLoop, calls=%fused_computation.32 | loop fusion | flops 200 | bytes 176 | tf_op jit(solution)/shard_map/reduce_sum | solution.py:420
  37.9 1.3 %fusion.8 = f32[8]{0:T(128)} fusion(f32[2]{0:T(128)} %copy-done.12, s32[2]{0:T(128)} %get-tuple-element.54), kind=kLoop, calls=%fused_computation.33 | loop fusion | flops 40 | bytes 48 | tf_op jit(solution)/shard_map/reduce_sum | solution.py:420
  39.1 1.3 %concatenate.12 = f32[1656]{0:T(1024)} concatenate(f32[768]{0:T(1024)S(1)} %add.71, f32[840]{0:T(1024)S(1)} %fusion.1, f32[40]{0:T(128)} %fusion.7, f32[8]{0:T(128)} %fusion.8), dimensions={0} | concatenate | bytes 13248 | tf_op jit(solution)/shard_map/concatenate | solution.py:423
  40.5 1.5 %collective-permute-start.5 = (f32[5,2]{0,1:T(2,128)}, f32[5,2]{0,1:T(2,128)S(1)}, u32[]{:S(2)}, u32[]{:S(2)}) collective-permute-start(f32[5,2]{0,1:T(2,128)} %stack.35), channel_id=1, source_target_pairs={{0,24},{4,28},{8,16},{12,20},{16,8},{20,12},{24,0},{28,4},{1,25},{... | collective-permute-start | bytes 128 | tf_op jit(solution)/shard_map/ppermute | solution.py:304
  48.9 1.2 %collective-permute-start.10 = (f32[256,256]{1,0:T(8,128)}, f32[256,256]{1,0:T(8,128)}, u32[]{:S(2)}, u32[]{:S(2)}) collective-permute-start(f32[256,256]{1,0:T(8,128)} %get-tuple-element.20), channel_id=1, source_target_pairs={{0,8},{4,12},{8,0},{12,4},{16,24},{20,28},{24,16},{28,20},{1,9},{5... | collective-permute-start | bytes 786440 | tf_op jit(solution)/shard_map/ppermute | solution.py:304
  53.0 1.5 %collective-permute-start.11 = (f32[256,256]{1,0:T(8,128)}, f32[256,256]{1,0:T(8,128)}, u32[]{:S(2)}, u32[]{:S(2)}) collective-permute-start(f32[256,256]{1,0:T(8,128)} %get-tuple-element.20), channel_id=1, source_target_pairs={{0,16},{4,20},{8,24},{12,28},{16,0},{20,4},{24,8},{28,12},{1,17},{... | collective-permute-start | bytes 786440 | tf_op jit(solution)/shard_map/ppermute | solution.py:304
  54.5 2.6 %maximum_convert_fusion = (s32[2]{0:T(128)S(1)}, f32[2]{0:T(128)S(1)}) fusion(f32[1]{0:T(128)} %bitcast.9, f32[1]{0:T(128)} %bitcast.8, f32[1]{0:T(128)} %bitcast.11, f32[1]{0:T(128)} %bitcast.10), kind=kLoop, calls=%fused_computation.53 | loop fusion | flops 6 | bytes 32 | tf_op jit(solution)/shard_map/convert_element_type | solution.py:367
  57.2 3.8 %stack.38 = f32[6]{0:T(128)S(1)} concatenate(f32[1]{0:T(128)} %bitcast.12, f32[1]{0:T(128)} %bitcast.13, f32[1]{0:T(128)} %bitcast.14, f32[1]{0:T(128)} %bitcast.15, f32[1]{0:T(128)} %bitcast.16, f32[1]{0:T(128)} %bitcast.17), dimensions={0} | concatenate | bytes 48 | tf_op jit(solution)/shard_map/stack | solution.py:365
  61.6 3.8 %stack.39.res_ref = f32[6]{0:T(128)S(1)} concatenate(f32[1]{0:T(128)} %bitcast.18, f32[1]{0:T(128)} %bitcast.19, f32[1]{0:T(128)} %bitcast.20, f32[1]{0:T(128)} %bitcast.21, f32[1]{0:T(128)} %bitcast.22, f32[1]{0:T(128)} %bitcast.23), dimensions={0} | concatenate | bytes 48 | tf_op jit(solution)/shard_map/stack | solution.py:364
  65.4 1.3 %fusion.9 = f32[40]{0:T(128)} fusion(f32[2]{0:T(128)} %copy-done.23, s32[2]{0:T(128)} %get-tuple-element.27), kind=kLoop, calls=%fused_computation.34 | loop fusion | flops 200 | bytes 176 | tf_op jit(solution)/shard_map/reduce_sum | solution.py:420
  66.7 1.3 %fusion.10 = f32[8]{0:T(128)} fusion(f32[2]{0:T(128)} %copy-done.23, s32[2]{0:T(128)} %get-tuple-element.26), kind=kLoop, calls=%fused_computation.35 | loop fusion | flops 40 | bytes 48 | tf_op jit(solution)/shard_map/reduce_sum | solution.py:420
  68.1 1.4 %copy-done.3 = f32[2,3,256,256]{3,2,1,0:T(8,128)S(1)} copy-done((f32[2,3,256,256]{3,2,1,0:T(8,128)S(1)}, f32[2,3,256,256]{3,2,1,0:T(8,128)}, u32[]{:S(2)}) %copy-start.3) | copy-done | bytes 1572888
  70.2 7.8 %shard_map.155 = (f32[480,256]{1,0:T(8,128)S(1)}, f32[480,256]{1,0:T(8,128)S(1)}, f32[4,3,256]{2,1,0:T(4,128)S(1)}) custom-call(s32[1]{0:T(128)} %bitcast.d_ref, s32[6]{0:T(128)S(1)} %copy-done.7, f32[6]{0:T(128)S(1)} %stack.39.res_ref, f32[2,256,256]{2,1,0:T(8,128)S(1)} %select_convert_fusion.x_ref.own_ref, f32[2,3,256,256]{3,2,1,0:T(8,128)S(1)} %copy-done.3, ...), custom_call_target="tpu_custom_call" | custom-call | tf_op jit(solution)/shard_map/pallas_call | solution.py:371
  78.1 4.0 %shard_map.156 = (f32[480,256]{1,0:T(8,128)S(1)}, f32[480,256]{1,0:T(8,128)S(1)}, f32[2,3,256]{2,1,0:T(4,128)S(1)}) custom-call(s32[1]{0:T(128)} %bitcast.d_ref, s32[2]{0:T(128)S(1)} %get-tuple-element.64.len_ref, f32[2]{0:T(128)S(1)} %get-tuple-element.65.res_ref, f32[480,256]{1,0:T(8,128)S(1)} %get-tuple-element.18.in_own, ...), custom_call_target="tpu_custom_call" | custom-call | tf_op jit(solution)/shard_map/pallas_call | solution.py:391
  82.2 3.8 %multiply_add_fusion.2 = (f32[1,3,256]{2,1,0:T(4,128)S(1)}, f32[1,3,256]{2,1,0:T(4,128)S(1)}, f32[1,3,256]{2,1,0:T(4,128)S(1)}) fusion(f32[2,3,256]{2,1,0:T(4,128)S(1)} %get-tuple-element.25, f32[4,3,256]{2,1,0:T(4,128)S(1)} %get-tuple-element.24, f32[]{:T(128)} %bitcast.32, f32[]{:T(128)} %bitcast.31, f32[]{:T(128)} %bitcast.34, f32[]{:T(128)} %bitcast.33, ...), kind=kLoop, calls=%fused_computation.17 | loop fusion | flops 6912 | bytes 27672 | tf_op jit(solution)/shard_map/add | solution.py:418
  (129 shorter events, 33.3 us)
Async XLA Ops:
  2.5 17.3 %copy-start.25 = (s32[2]{0:T(128)S(1)}, s32[2]{0:T(128)}, u32[]{:S(2)}) copy-start(s32[2]{0:T(128)} %param.17) | copy-start | bytes 28
  2.5 17.8 %copy-start.24 = (f32[8]{0:T(128)S(1)}, f32[8]{0:T(128)}, u32[]{:S(2)}) copy-start(f32[8]{0:T(128)} %param.20) | copy-start | bytes 100
  2.5 18.5 %copy-start.14 = (s32[2]{0:T(128)S(1)}, s32[2]{0:T(128)}, u32[]{:S(2)}) copy-start(s32[2]{0:T(128)} %param.15) | copy-start | bytes 28
  5.4 16.1 %copy-start.13 = (f32[840]{0:T(1024)S(1)}, f32[840]{0:T(1024)}, u32[]{:S(2)}) copy-start(f32[840]{0:T(1024)} %param.18) | copy-start | bytes 10084
  5.4 16.8 %copy-start.27 = (s32[2]{0:T(128)S(1)}, s32[2]{0:T(128)}, u32[]{:S(2)}) copy-start(s32[2]{0:T(128)} %param.16) | copy-start | bytes 28
  5.4 17.3 %copy-start.26 = (f32[40]{0:T(128)S(1)}, f32[40]{0:T(128)}, u32[]{:S(2)}) copy-start(f32[40]{0:T(128)} %param.19) | copy-start | bytes 484
  5.4 62.7 %copy-start.1 = (bf16[256,15,256]{2,0,1:T(8,128)(2,1)S(1)}, bf16[256,15,256]{2,0,1:T(8,128)(2,1)}, u32[]{:S(2)}) copy-start(bf16[256,15,256]{2,0,1:T(8,128)(2,1)} %param.13) | copy-start | bytes 5898244
  5.4 62.7 %copy-start.5 = (bf16[3,256]{1,0:T(4,128)(2,1)S(1)}, bf16[3,256]{1,0:T(4,128)(2,1)}, u32[]{:S(2)}) copy-start(bf16[3,256]{1,0:T(4,128)(2,1)} %refs_3_.1) | copy-start | bytes 4612
  9.0 19.9 %copy-start.21 = (f32[2]{0:T(128)}, f32[2]{0:T(128)S(1)}, u32[]{:S(2)}) copy-start(f32[2]{0:T(128)S(1)} %slice_reduce_fusion.3) | copy-start | bytes 28
  9.1 16.3 %collective-permute-start.1 = (f32[2]{0:T(128)S(1)}, f32[2]{0:T(128)}, u32[]{:S(2)}, u32[]{:S(2)}) collective-permute-start(f32[2]{0:T(128)S(1)} %slice_reduce_fusion.3), channel_id=1, source_target_pairs={{0,2},{1,3},{2,0},{3,1},{4,6},{5,7},{6,4},{7,5},{8,10},{9,11},{10,... | collective-permute-start | bytes 32 | tf_op jit(solution)/shard_map/ppermute | solution.py:304
  13.1 12.8 %collective-permute-start.2 = (f32[2]{0:T(128)S(1)}, f32[2]{0:T(128)S(1)}, u32[]{:S(2)}, u32[]{:S(2)}) collective-permute-start(f32[2]{0:T(128)S(1)} %slice_reduce_fusion.3), channel_id=1, source_target_pairs={{0,3},{1,2},{2,1},{3,0},{4,7},{5,6},{6,5},{7,4},{8,11},{9,10},{10,... | collective-permute-start | bytes 32 | tf_op jit(solution)/shard_map/ppermute | solution.py:304
  14.4 14.5 %collective-permute-start = (f32[2]{0:T(128)S(1)}, f32[2]{0:T(128)}, u32[]{:S(2)}, u32[]{:S(2)}) collective-permute-start(f32[2]{0:T(128)S(1)} %slice_reduce_fusion.3), channel_id=1, source_target_pairs={{0,1},{1,0},{2,3},{3,2},{4,5},{5,4},{6,7},{7,6},{8,9},{9,8},{10,11... | collective-permute-start | bytes 32 | tf_op jit(solution)/shard_map/ppermute | solution.py:304
  15.5 37.5 %collective-permute-start.6 = (f32[256,256]{1,0:T(8,128)}, f32[256,256]{1,0:T(8,128)S(1)}, u32[]{:S(2)}, u32[]{:S(2)}) collective-permute-start(f32[256,256]{1,0:T(8,128)} %get-tuple-element.38), channel_id=1, source_target_pairs={{0,24},{4,28},{8,16},{12,20},{16,8},{20,12},{24,0},{28,4},{1,25},{... | collective-permute-start | bytes 786440 | tf_op jit(solution)/shard_map/ppermute | solution.py:304
  17.9 50.1 %collective-permute-start.8 = (f32[256,256]{1,0:T(8,128)}, f32[256,256]{1,0:T(8,128)S(1)}, u32[]{:S(2)}, u32[]{:S(2)}) collective-permute-start(f32[256,256]{1,0:T(8,128)} %get-tuple-element.38), channel_id=1, source_target_pairs={{0,8},{4,12},{8,0},{12,4},{16,24},{20,28},{24,16},{28,20},{1,9},{5... | collective-permute-start | bytes 786440 | tf_op jit(solution)/shard_map/ppermute | solution.py:304
  25.4 42.7 %collective-permute-start.9 = (f32[256,256]{1,0:T(8,128)}, f32[256,256]{1,0:T(8,128)S(1)}, u32[]{:S(2)}, u32[]{:S(2)}) collective-permute-start(f32[256,256]{1,0:T(8,128)} %get-tuple-element.38), channel_id=1, source_target_pairs={{0,16},{4,20},{8,24},{12,28},{16,0},{20,4},{24,8},{28,12},{1,17},{... | collective-permute-start | bytes 786440 | tf_op jit(solution)/shard_map/ppermute | solution.py:304
  26.5 41.6 %collective-permute-start.7 = (f32[256,256]{1,0:T(8,128)}, f32[256,256]{1,0:T(8,128)S(1)}, u32[]{:S(2)}, u32[]{:S(2)}) collective-permute-start(f32[256,256]{1,0:T(8,128)} %get-tuple-element.20), channel_id=1, source_target_pairs={{0,24},{4,28},{8,16},{12,20},{16,8},{20,12},{24,0},{28,4},{1,25},{... | collective-permute-start | bytes 786440 | tf_op jit(solution)/shard_map/ppermute | solution.py:304
  32.8 7.7 %collective-permute-start.4 = (f32[5,2]{0,1:T(2,128)}, f32[5,2]{0,1:T(2,128)S(1)}, u32[]{:S(2)}, u32[]{:S(2)}) collective-permute-start(f32[5,2]{0,1:T(2,128)} %stack.35), channel_id=1, source_target_pairs={{0,16},{4,20},{8,24},{12,28},{16,0},{20,4},{24,8},{28,12},{1,17},{... | collective-permute-start | bytes 128 | tf_op jit(solution)/shard_map/ppermute | solution.py:304
  40.5 4.7 %collective-permute-start.5 = (f32[5,2]{0,1:T(2,128)}, f32[5,2]{0,1:T(2,128)S(1)}, u32[]{:S(2)}, u32[]{:S(2)}) collective-permute-start(f32[5,2]{0,1:T(2,128)} %stack.35), channel_id=1, source_target_pairs={{0,24},{4,28},{8,16},{12,20},{16,8},{20,12},{24,0},{28,4},{1,25},{... | collective-permute-start | bytes 128 | tf_op jit(solution)/shard_map/ppermute | solution.py:304
  45.2 3.8 %collective-permute-start.3 = (f32[5,2]{0,1:T(2,128)}, f32[5,2]{0,1:T(2,128)S(1)}, u32[]{:S(2)}, u32[]{:S(2)}) collective-permute-start(f32[5,2]{0,1:T(2,128)} %stack.35), channel_id=1, source_target_pairs={{0,8},{4,12},{8,0},{12,4},{16,24},{20,28},{24,16},{28,20},{1,9},{5... | collective-permute-start | bytes 128 | tf_op jit(solution)/shard_map/ppermute | solution.py:304
  48.9 29.1 %collective-permute-start.10 = (f32[256,256]{1,0:T(8,128)}, f32[256,256]{1,0:T(8,128)}, u32[]{:S(2)}, u32[]{:S(2)}) collective-permute-start(f32[256,256]{1,0:T(8,128)} %get-tuple-element.20), channel_id=1, source_target_pairs={{0,8},{4,12},{8,0},{12,4},{16,24},{20,28},{24,16},{28,20},{1,9},{5... | collective-permute-start | bytes 786440 | tf_op jit(solution)/shard_map/ppermute | solution.py:304
  53.0 25.1 %collective-permute-start.11 = (f32[256,256]{1,0:T(8,128)}, f32[256,256]{1,0:T(8,128)}, u32[]{:S(2)}, u32[]{:S(2)}) collective-permute-start(f32[256,256]{1,0:T(8,128)} %get-tuple-element.20), channel_id=1, source_target_pairs={{0,16},{4,20},{8,24},{12,28},{16,0},{20,4},{24,8},{28,12},{1,17},{... | collective-permute-start | bytes 786440 | tf_op jit(solution)/shard_map/ppermute | solution.py:304
  78.1 8.3 %copy-start.8 = (f32[1656]{0:T(1024)S(1)}, f32[1656]{0:T(1024)}, u32[]{:S(2)}) copy-start(f32[1656]{0:T(1024)} %concatenate.12) | copy-start | bytes 19876
  82.1 8.0 %collective-permute-start.12 = (f32[480,256]{1,0:T(8,128)S(1)}, f32[480,256]{1,0:T(8,128)S(1)}, u32[]{:S(2)}, u32[]{:S(2)}) collective-permute-start(f32[480,256]{1,0:T(8,128)S(1)} %get-tuple-element.22), channel_id=1, source_target_pairs={{0,4},{4,0},{8,12},{12,8},{16,20},{20,16},{24,28},{28,24},{1,5},{5... | collective-permute-start | bytes 1474568 | tf_op jit(solution)/shard_map/ppermute | solution.py:304
  86.4 1.4 %collective-permute-start.13 = (f32[7,256]{1,0:T(8,128)S(1)}, f32[7,256]{1,0:T(8,128)S(1)}, u32[]{:S(2)}, u32[]{:S(2)}) collective-permute-start(f32[7,256]{1,0:T(8,128)S(1)} %reshape.153), channel_id=1, source_target_pairs={{0,4},{4,0},{8,12},{12,8},{16,20},{20,16},{24,28},{28,24},{1,5},{5... | collective-permute-start | bytes 21512 | tf_op jit(solution)/shard_map/ppermute | solution.py:304
  (18 other events, 84.4 us)

commit v2 on v0

--- a/solution.py
+++ b/solution.py
@@ -1,10 +1,20 @@
+import functools
+
 import jax
 import jax.numpy as jnp
+import numpy as np
 from jax import lax
+from jax.experimental import pallas as pl
+from jax.experimental.pallas import tpu as pltpu
 from jax.sharding import PartitionSpec as P
 
 TAU = 0.05
 WIDTH_LIST = ((3, 0), (5, 3), (7, 8))
+TAPS = 15
+REACH = 3
+PAD = 8
+OUTSIDE = np.float32(1024.0)
+BY_LAST = (((1,), (1,)), ((), ()))
 
 
 def convolve(columns, weights):
@@ -35,7 +45,11 @@
     return jnp.concatenate(outputs, axis=1)
 
 
-def local(
+def one_hots(codes, size):
+    return (codes[:, None] == jnp.arange(size, dtype=jnp.int32)[None, :]).astype(jnp.float32)
+
+
+def local_scatter(
     embedded,
     lengths,
     conv_weight,
@@ -67,15 +81,9 @@
     feature = jnp.stack(features, axis=1)
     head = head_weight.astype(jnp.float32)
     partial_pred = jnp.sum(feature * head[None, :, :], axis=(1, 2))
-    occ_hot = (
-        occupation[:, None] == jnp.arange(occ_table.shape[0], dtype=jnp.int32)[None, :]
-    ).astype(jnp.float32)
-    cohort_hot = (
-        cohort[:, None] == jnp.arange(cohort_table.shape[0], dtype=jnp.int32)[None, :]
-    ).astype(jnp.float32)
-    edu_hot = (
-        education[:, None] == jnp.arange(edu_table.shape[0], dtype=jnp.int32)[None, :]
-    ).astype(jnp.float32)
+    occ_hot = one_hots(occupation, occ_table.shape[0])
+    cohort_hot = one_hots(cohort, cohort_table.shape[0])
+    edu_hot = one_hots(education, edu_table.shape[0])
     highest = lax.Precision.HIGHEST
     offsets = (
         jnp.dot(occ_hot, occ_table, precision=highest)
@@ -104,7 +112,419 @@
     return (conv_grad, head_grad, occ_grad, cohort_grad, edu_grad, prediction)
 
 
+def load_post(x, xpad):
+    rows, width = x.shape
+    xpad[0:PAD, :] = jnp.zeros((PAD, width), jnp.float32)
+    xpad[PAD + rows :, :] = jnp.zeros((PAD, width), jnp.float32)
+    xpad[PAD : PAD + rows, :] = jnp.where(x < OUTSIDE, x, 0.0)
+
+
+def length_of(x):
+    inside = (x[:, 0:128] < OUTSIDE).astype(jnp.float32)
+    return jnp.max(jnp.sum(inside, axis=0, keepdims=True)).astype(jnp.int32)
+
+
+def make_cols(xpad, cols):
+    rows, width = cols.shape[0], xpad.shape[1]
+    for offset in range(2 * REACH + 1):
+        start = PAD - REACH + offset
+        cols[:, offset * width : (offset + 1) * width] = xpad[start : start + rows, :].astype(
+            jnp.bfloat16
+        )
+
+
+def forward(cols, w_ref, head, length, feat, share):
+    width = w_ref.shape[0] // TAPS
+    valid = lax.broadcasted_iota(jnp.int32, (cols.shape[0], head.shape[1]), 0) < length
+    part = jnp.zeros((1, head.shape[1]), jnp.float32)
+    for index, (taps, first) in enumerate(WIDTH_LIST):
+        half = taps // 2
+        conv = jnp.dot(
+            cols[:, (REACH - half) * width : (REACH + half + 1) * width],
+            w_ref[first * width : (first + taps) * width, :],
+            preferred_element_type=jnp.float32,
+        )
+        score = jnp.where(valid, conv * np.float32(1.0 / TAU), -jnp.inf)
+        top = jnp.max(score, axis=0, keepdims=True)
+        expd = jnp.exp(score - top)
+        total = jnp.sum(expd, axis=0, keepdims=True)
+        feature = np.float32(TAU) * (top + jnp.log(total))
+        feat[index : index + 1, :] = feature
+        part = part + feature * head[index : index + 1]
+        share[index] = expd * (head[index : index + 1] / total)
+    return part
+
+
+def pick_rows(d_ref, cols, slice_e):
+    rows = cols.shape[0]
+    width = cols.shape[1] // (2 * REACH + 1)
+    me = d_ref[0]
+    row = lax.broadcasted_iota(jnp.int32, (2 * slice_e, width), 0)
+    lane = lax.broadcasted_iota(jnp.int32, (2 * slice_e, width), 1)
+    wanted = jnp.where(row < slice_e, me * slice_e + row, (me ^ 1) * slice_e + row - slice_e)
+    pick = (lane == wanted).astype(jnp.bfloat16)
+    middle = cols[:, REACH * width : (REACH + 1) * width]
+    across = lax.dot_general(pick, middle, BY_LAST, preferred_element_type=jnp.float32)
+    place = lax.broadcasted_iota(jnp.int32, (2 * slice_e, rows), 1)
+    parts = []
+    for offset in range(-REACH, REACH + 1):
+        if offset:
+            moved = pltpu.roll(across, (-offset) % rows, 1)
+            inside = (place + offset >= 0) & (place + offset < rows)
+            parts.append(jnp.where(inside, moved, 0.0))
+        else:
+            parts.append(across)
+    return jnp.concatenate(parts, axis=0).astype(jnp.bfloat16)
+
+
+def backward(cols, d_ref, residual, share, acc_own, acc_other, slice_e):
+    at = pick_rows(d_ref, cols, slice_e)
+    step = 2 * slice_e
+    for index, (taps, first) in enumerate(WIDTH_LIST):
+        half = taps // 2
+        slope = (residual * share[index]).astype(jnp.bfloat16)
+        term = jnp.dot(
+            at[(REACH - half) * step : (REACH + half + 1) * step],
+            slope,
+            preferred_element_type=jnp.float32,
+        )
+        for j in range(taps):
+            place = slice((first + j) * slice_e, (first + j + 1) * slice_e)
+            acc_own[place, :] += term[j * step : j * step + slice_e]
+            acc_other[place, :] += term[j * step + slice_e : (j + 1) * step]
+
+
+def mask_kernel(len_ref, x_ref, *piece_refs):
+    rows, width = x_ref.shape[1:]
+    place = lax.broadcasted_iota(jnp.int32, (rows, width), 0)
+    for p, piece in enumerate(piece_refs):
+        piece[...] = jnp.where(place < len_ref[p], x_ref[p].astype(jnp.float32), OUTSIDE)
+
+
+def own_kernel(len_ref, pieces, w_ref, head_ref, part_ref, feat_ref, share_ref, xpads, cols):
+    posts = pieces.shape[0]
+    head = head_ref[...].astype(jnp.float32)
+    part_ref[...] = jnp.zeros_like(part_ref)
+
+    def post(p, carry):
+        load_post(pieces[p], xpads.at[p])
+        make_cols(xpads.at[p], cols)
+        part = forward(cols, w_ref, head, len_ref[p], feat_ref.at[p], share_ref.at[p])
+        part_ref[pl.ds(p, 1), :] = jnp.broadcast_to(
+            jnp.sum(part, axis=1, keepdims=True), (1, part_ref.shape[1])
+        )
+        return carry
+
+    lax.fori_loop(0, posts, post, 0)
+
+
+def facts_kernel(*refs):
+    occ_ref, coh_ref, edu_ref, wage_ref, occ_t, coh_t, edu_t = refs[:7]
+    one, two, pieces, facts_ref, pred_ref, pack_ref = refs[7:]
+    posts, rows, _ = pieces.shape
+    pred = one[...] + two[...]
+    lanes = pred.shape[1]
+    lane = lax.broadcasted_iota(jnp.int32, (1, lanes), 1)
+    facts_ref[...] = jnp.zeros_like(facts_ref)
+    out = jnp.zeros((1, lanes), jnp.float32)
+    for p in range(posts):
+        offset = occ_t[occ_ref[p]] + coh_t[coh_ref[p]] + edu_t[edu_ref[p]]
+        value = pred[p : p + 1] + offset
+        out = jnp.where(lane == p, value, out)
+        facts_ref[p : p + 1, :] = value - wage_ref[p]
+        for kind, ref in enumerate((occ_ref, coh_ref, edu_ref)):
+            row = (kind + 1) * posts + p
+            facts_ref[row : row + 1, :] = jnp.full(
+                (1, lanes), ref[p].astype(jnp.float32), jnp.float32
+            )
+    pred_ref[...] = out[:, :posts]
+    pack_ref[0:rows, :] = pieces[posts - 1]
+    pack_ref[rows:, :] = jnp.zeros((pack_ref.shape[0] - rows, pack_ref.shape[1]), jnp.float32)
+    pack_ref[rows:, 0:lanes] = facts_ref[...]
+
+
+def first_kernel(
+    n_near,
+    slice_e,
+    d_ref,
+    share_own,
+    facts,
+    own,
+    far,
+    far_facts,
+    *refs,
+):
+    near = refs[:n_near]
+    w_ref, head_ref, acc_own, acc_other, feat_far, feat_near, share_near = refs[n_near : n_near + 7]
+    xpads, share, cols = refs[n_near + 7 :]
+    posts = own.shape[0]
+    head = head_ref[...].astype(jnp.float32)
+    acc_own[...] = jnp.zeros_like(acc_own)
+    acc_other[...] = jnp.zeros_like(acc_other)
+
+    def own_post(p, carry):
+        load_post(own[p], xpads.at[0])
+        make_cols(xpads.at[0], cols)
+        residual = facts[pl.ds(p, 1), 0:1]
+        backward(cols, d_ref, residual, share_own.at[p], acc_own, acc_other, slice_e)
+        return carry
+
+    def far_post(p, carry):
+        load_post(far[p], xpads.at[0])
+        make_cols(xpads.at[0], cols)
+        forward(cols, w_ref, head, length_of(far[p]), feat_far.at[p], share)
+        residual = far_facts[pl.ds(p, 1), 0:1]
+        backward(cols, d_ref, residual, share, acc_own, acc_other, slice_e)
+        return carry
+
+    lax.fori_loop(0, posts, own_post, 0)
+    lax.fori_loop(0, posts, far_post, 0)
+    for k in range(n_near):
+        load_post(near[k][...], xpads.at[k])
+    lens = [length_of(near[k]) for k in range(n_near)]
+
+    def near_post(k, carry):
+        make_cols(xpads.at[k], cols)
+        length = lens[0]
+        for i in range(1, n_near):
+            length = jnp.where(k == i, lens[i], length)
+        forward(cols, w_ref, head, length, feat_near.at[k], share_near.at[k])
+        return carry
+
+    lax.fori_loop(0, n_near, near_post, 0)
+
+
+def last_kernel(n_near, sizes, slice_e, d_ref, in_own, in_other, share_near, *refs):
+    near = refs[:n_near]
+    packs = refs[n_near : 2 * n_near]
+    facts, far_facts, feat_own, feat_far, feat_near = refs[2 * n_near : 2 * n_near + 5]
+    w_ref, head_ref, acc_own, acc_other, sums_ref = refs[2 * n_near + 5 : 2 * n_near + 10]
+    xpads, facs, feat_last, share, cols = refs[2 * n_near + 10 :]
+    posts = feat_own.shape[0]
+    rows = near[0].shape[0]
+    head = head_ref[...].astype(jnp.float32)
+    filters = head.shape[1]
+    acc_own[...] = in_own[...]
+    acc_other[...] = in_other[...]
+    lens = []
+    for k in range(n_near):
+        load_post(near[k][...], xpads.at[2 * k])
+        load_post(packs[k][0:rows, :], xpads.at[2 * k + 1])
+        facs[k] = packs[k][rows:, :]
+        lens.append(length_of(packs[k].at[0:rows]))
+
+    def near_post(k, carry):
+        make_cols(xpads.at[2 * k], cols)
+        backward(
+            cols, d_ref, facs[k, 0:1, 0:1], share_near.at[k], acc_own, acc_other, slice_e
+        )
+        make_cols(xpads.at[2 * k + 1], cols)
+        length = lens[0]
+        for i in range(1, n_near):
+            length = jnp.where(k == i, lens[i], length)
+        forward(cols, w_ref, head, length, feat_last.at[k], share)
+        backward(cols, d_ref, facs[k, 1:2, 0:1], share, acc_own, acc_other, slice_e)
+        return carry
+
+    lax.fori_loop(0, n_near, near_post, 0)
+
+    def chip_terms(told, feature):
+        n_rows = code_rows(sizes, filters)
+        place = lax.broadcasted_iota(jnp.int32, (n_rows, filters), 0) * filters
+        place = place + lax.broadcasted_iota(jnp.int32, (n_rows, filters), 1)
+        head_term = jnp.zeros((3, filters), jnp.float32)
+        code_term = jnp.zeros((n_rows, filters), jnp.float32)
+        for p in range(posts):
+            residual = told[p : p + 1, 0:1]
+            head_term = head_term + residual * feature[p]
+            for kind, start in enumerate(code_starts(sizes, filters)):
+                at_row = (kind + 1) * posts + p
+                code = told[at_row : at_row + 1, 0:1].astype(jnp.int32) + start
+                code_term = code_term + jnp.where(place == code, residual, 0.0)
+        return head_term, code_term
+
+    terms = [
+        chip_terms(facts[...], [feat_own[p] for p in range(posts)]),
+        *[
+            chip_terms(facs[k], [feat_near[k, 0:3, :], feat_last[k, 0:3, :]])
+            for k in range(n_near)
+        ],
+        chip_terms(far_facts[...], [feat_far[p, 0:3, :] for p in range(posts)]),
+    ]
+    sums_ref[...] = jnp.zeros_like(sums_ref)
+    sums_ref[0:3, :] = tree_sum([term[0] for term in terms])
+    sums_ref[3 : 3 + code_rows(sizes, filters), :] = tree_sum([term[1] for term in terms])
+
+
+def tree_sum(values):
+    while len(values) > 1:
+        values = [values[i] + values[i + 1] for i in range(0, len(values), 2)]
+    return values[0]
+
+
+def code_starts(sizes, filters):
+    starts, start = [], 0
+    for size in sizes:
+        starts.append(start)
+        start += -(-size // filters) * filters
+    return starts
+
+
+def code_rows(sizes, filters):
+    return sum(-(-size // filters) for size in sizes)
+
+
+def sums_kernel(sizes, mine_ref, came_ref, head_ref, *code_refs):
+    filters = mine_ref.shape[1]
+    head_ref[...] = mine_ref[0:3, :] + came_ref[0:3, :]
+    row = 3
+    for size, ref in zip(sizes, code_refs):
+        for start in range(0, size, filters):
+            count = min(filters, size - start)
+            total = mine_ref[row : row + 1, :] + came_ref[row : row + 1, :]
+            ref[:, start : start + count] = total[:, :count]
+            row += 1
+
+
+def add_kernel(mine_ref, came_ref, out_ref):
+    out_ref[...] = mine_ref[...] + came_ref[...]
+
+
+def local_gather(n_doc, n_filt, *args):
+    (
+        embedded,
+        lengths,
+        conv_weight,
+        head_weight,
+        occupation,
+        cohort,
+        education,
+        occ_table,
+        cohort_table,
+        edu_table,
+        wage,
+    ) = args
+    posts, seq_len, dims = embedded.shape
+    filters = conv_weight.shape[2]
+    slice_e = dims // n_doc
+    sizes = (occ_table.shape[0], cohort_table.shape[0], edu_table.shape[0])
+    f32 = jnp.float32
+    me = lax.axis_index("doc").astype(jnp.int32).reshape(1)
+    vmem = pl.BlockSpec(memory_space=pltpu.VMEM)
+    smem = pl.BlockSpec(memory_space=pltpu.SMEM)
+    pad_shape = (seq_len + 2 * PAD, dims)
+    cols = pltpu.VMEM((seq_len, (2 * REACH + 1) * dims), jnp.bfloat16)
+    share_shape = (3, seq_len, filters)
+
+    def swap(x, k, axis="doc"):
+        size = n_doc if axis == "doc" else n_filt
+        return lax.ppermute(x, axis, [(i, i ^ k) for i in range(size)])
+
+    def call(kernel, n_smem, n_vmem, out, scratch=()):
+        return pl.pallas_call(
+            kernel,
+            in_specs=[smem] * n_smem + [vmem] * n_vmem,
+            out_specs=[vmem] * len(out),
+            out_shape=[jax.ShapeDtypeStruct(shape, f32) for shape in out],
+            scratch_shapes=list(scratch),
+            compiler_params=pltpu.CompilerParams(vmem_limit_bytes=24 << 20),
+            cost_estimate=pl.CostEstimate(flops=1, bytes_accessed=1, transcendentals=0),
+        )
+
+    def mask_all(len_ref, x_ref, all_ref, first_ref):
+        mask_kernel(len_ref, x_ref, *[all_ref.at[p] for p in range(posts)])
+        first_ref[...] = all_ref[0]
+
+    weights = jnp.transpose(conv_weight, (1, 0, 2)).reshape(TAPS * dims, filters)
+    pieces, piece = call(mask_all, 1, 1, [(posts, seq_len, dims), (seq_len, dims)])(
+        lengths, embedded
+    )
+
+    near = [k for k in range(2, n_doc, 2) if bin(k).count("1") == 1]
+    far = sum(near)
+    first = [swap(piece, k) for k in near]
+    far_pieces = swap(pieces, far)
+
+    part, feat_own, share_own = call(
+        own_kernel,
+        1,
+        3,
+        [(8, 128), (posts, 3, filters), (posts,) + share_shape],
+        [pltpu.VMEM((posts,) + pad_shape, f32), cols],
+    )(lengths, pieces, weights, head_weight)
+
+    k = 1
+    while 2 * k < n_filt:
+        part = part + swap(part, k, "filt")
+        k *= 2
+    other = swap(part, k, "filt")
+    first, other = lax.optimization_barrier((first, other))
+    n_facts = -(-4 * posts // 8) * 8
+    facts, prediction, pack = call(
+        facts_kernel,
+        7,
+        3,
+        [(n_facts, 128), (1, posts), (seq_len + n_facts, dims)],
+    )(occupation, cohort, education, wage, occ_table, cohort_table, edu_table, part, other, pieces)
+
+    far_facts = swap(facts, far)
+    packs = [swap(pack, k) for k in near]
+
+    acc_shape = (TAPS * slice_e, filters)
+    n_near = len(near)
+    acc_own, acc_other, feat_far, feat_near, share_near = call(
+        functools.partial(first_kernel, n_near, slice_e),
+        1,
+        5 + n_near + 2,
+        [acc_shape, acc_shape, (posts, 8, filters), (n_near, 8, filters), (n_near,) + share_shape],
+        [pltpu.VMEM((n_near,) + pad_shape, f32), pltpu.VMEM(share_shape, f32), cols],
+    )(me, share_own, facts, pieces, far_pieces, far_facts, *first, weights, head_weight)
+    acc_own, acc_other, sums = call(
+        functools.partial(last_kernel, n_near, sizes, slice_e),
+        1,
+        3 + 2 * n_near + 5 + 2,
+        [acc_shape, acc_shape, (-(-(3 + code_rows(sizes, filters)) // 8) * 8, filters)],
+        [
+            pltpu.VMEM((2 * n_near,) + pad_shape, f32),
+            pltpu.VMEM((n_near, n_facts, dims), f32),
+            pltpu.VMEM((n_near, 8, filters), f32),
+            pltpu.VMEM(share_shape, f32),
+            cols,
+        ],
+    )(
+        me,
+        acc_own,
+        acc_other,
+        share_near,
+        *first,
+        *packs,
+        facts,
+        far_facts,
+        feat_own,
+        feat_far,
+        feat_near,
+        weights,
+        head_weight,
+    )
+
+    head_grad, *codes = call(
+        functools.partial(sums_kernel, sizes),
+        0,
+        2,
+        [(3, filters)] + [(1, size) for size in sizes],
+    )(sums, swap(sums, 1))
+    codes = [code.reshape(size) for code, size in zip(codes, sizes)]
+    (grad,) = call(add_kernel, 0, 2, [acc_shape])(acc_own, swap(acc_other, 1))
+    conv_grad = jnp.transpose(grad.reshape(TAPS, slice_e, filters), (1, 0, 2))
+    return (conv_grad, head_grad, *codes, prediction.reshape(posts))
+
+
 def solution(mesh):
+    n_doc, n_filt = mesh.shape["doc"], mesh.shape["filt"]
+    if n_doc == 8 and n_filt in (2, 4):
+        local = functools.partial(local_gather, n_doc, n_filt)
+    else:
+        local = local_scatter
     return jax.shard_map(
         local,
         mesh=mesh,

time: 99.1 us -> 46.5 us (0.47)
  waiting for transfers between devices: 36.1 us -> 9.27 us
  blocking collectives: 26.4 us -> 0 us
  Pallas kernels: 0 us -> 15.5 us
  starting transfers between devices: 0.04 us -> 13.6 us
  between operations: 14.3 us -> 0.81 us
  matrix products: 6.48 us -> 0 us
  other arithmetic: 4.96 us -> 0.61 us
  local copies, waits for them, and re-layouts: 10.5 us -> 6.47 us
    reduce_scatter x1 -> x0, waiting for transfers between devices: 36.1 us -> none  [local(): lax.psum_scatter(grad_terms(columns, slopes), 'doc', scatter_dimension=0,...]
    psum x2 -> x0, blocking collectives: 26.4 us -> none  [the longest x1 13.5 us: local(): prediction = lax.psum(partial_pred, 'filt') + offsets]
    pallas_call x0 -> x7, Pallas kernels: none -> 15.5 us  [the longest x1 5.6 us: local_gather(): call(functools.partial(first_kernel, n_near, slice_e), 1, 5 + n_near + 2,...]
    ppermute x0 -> x10, starting transfers between devices: none -> 13.6 us  [swap(): return lax.ppermute(x, axis, [(i, i ^ k) for i in range(size)])]
    ppermute x0 -> x10, waiting for transfers between devices: none -> 9.27 us  [swap(): return lax.ppermute(x, axis, [(i, i ^ k) for i in range(size)])]
    dot_general x12 -> x0, matrix products: 6.48 us -> none  [the longest x3 3.25 us: grad_terms(): jnp.einsum('ptje,ptf->ejf', window, slopes[index], preferred_element_type...]
    concatenate x1 -> x0, local copies, waits for them, and re-layouts: 5.49 us -> none  [grad_terms(): return jnp.concatenate(outputs, axis=1)]
    concatenate x1 -> x0, other arithmetic: 2.12 us -> none  [grad_terms(): return jnp.concatenate(outputs, axis=1)]
  transfers between devices with their start and end apart: 1 -> 10, of which waited for: 1 -> 4; matrix products, arithmetic and copies ran while one was open for 1% -> 1% of each run, Pallas kernels for 0% -> 22%
where the time goes in v2:
time: 46.5 us; the launch traced here: 46.3 us
  Pallas kernels  15.5 us (33%)
  starting transfers between devices  13.6 us (29%)
  waiting for transfers between devices  9.27 us (20%)
  local copies, waits for them, and re-layouts  6.47 us (14%)
  between operations  0.81 us (2%)
  other arithmetic  0.61 us (1%)
    ppermute x10, starting transfers between devices, swap(): return lax.ppermute(x, axis, [(i, i ^ k) for i in range(size)])  13.6 us
    ppermute x10, waiting for transfers between devices, swap(): return lax.ppermute(x, axis, [(i, i ^ k) for i in range(size)])  9.27 us
    unnamed x34, local copies, waits for them, and re-layouts  6.47 us
    pallas_call x1, Pallas kernels, local_gather(): call(functools.partial(first_kernel, n_near, slice_e), 1, 5 + n_near + 2,...  5.6 us
    pallas_call x1, Pallas kernels, local_gather(): call(functools.partial(last_kernel, n_near, sizes, slice_e), 1, 3 + 2 * n...  4.02 us
    pallas_call x1, Pallas kernels, local_gather(): call(own_kernel, 1, 3, [(8, 128), (posts, 3, filters), (posts,) + share_s...  2.43 us
    pallas_call x1, Pallas kernels, local_gather(): call(facts_kernel, 7, 3, [(n_facts, 128), (1, posts), (seq_len + n_facts,...  1.37 us
  transfers between devices with their start and end apart: 10, of which 4 were waited for; matrix products, arithmetic and copies ran while one was open for 1% of the time, Pallas kernels for 22%

profile of v2, /device:TPU:0, one launch (start us, length us, event | category | flops | bytes accessed | tf_op | source)
XLA Modules:
  0.0 46.3 jit_solution(6078616524541213027)
XLA Ops:
  0.6 0.9 %copy-done.4 = bf16[2,256,256]{2,1,0:T(8,128)(2,1)S(1)} copy-done((bf16[2,256,256]{2,1,0:T(8,128)(2,1)S(1)}, bf16[2,256,256]{2,1,0:T(8,128)(2,1)}, u32[]{:S(2)}) %copy-start.4) | copy-done | bytes 262168
  1.6 0.7 %copy-done.10 = s32[2]{0:T(128)S(1)} copy-done((s32[2]{0:T(128)S(1)}, s32[2]{0:T(128)}, u32[]{:S(2)}) %copy-start.10) | copy-done | bytes 32
  2.3 0.6 %shard_map.154 = (f32[2,256,256]{2,1,0:T(8,128)S(1)}, f32[256,256]{1,0:T(8,128)S(1)}) custom-call(s32[2]{0:T(128)S(1)} %copy-done.10, bf16[2,256,256]{2,1,0:T(8,128)(2,1)S(1)} %copy-done.4), custom_call_target="tpu_custom_call" | custom-call | flops 1 | bytes 1 | tf_op jit(solution)/shard_map/pallas_call | solution.py:439
  2.9 3.0 %collective-permute-start.2 = (f32[256,256]{1,0:T(8,128)S(1)}, f32[256,256]{1,0:T(8,128)S(1)}, u32[]{:S(2)}, u32[]{:S(2)}) collective-permute-start(f32[256,256]{1,0:T(8,128)S(1)} %get-tuple-element.32), channel_id=1, source_target_pairs={{0,16},{4,20},{8,24},{12,28},{16,0},{20,4},{24,8},{28,12},{1,17},{... | collective-permute-start | bytes 786440 | tf_op jit(solution)/shard_map/ppermute | solution.py:421
  5.9 1.5 %collective-permute-start.1 = (f32[256,256]{1,0:T(8,128)S(1)}, f32[256,256]{1,0:T(8,128)S(1)}, u32[]{:S(2)}, u32[]{:S(2)}) collective-permute-start(f32[256,256]{1,0:T(8,128)S(1)} %get-tuple-element.32), channel_id=1, source_target_pairs={{0,8},{4,12},{8,0},{12,4},{16,24},{20,28},{24,16},{28,20},{1,9},{5... | collective-permute-start | bytes 786440 | tf_op jit(solution)/shard_map/ppermute | solution.py:421
  7.5 1.5 %copy-done = bf16[256,15,256]{2,0,1:T(8,128)(2,1)S(1)} copy-done((bf16[256,15,256]{2,0,1:T(8,128)(2,1)S(1)}, bf16[256,15,256]{2,0,1:T(8,128)(2,1)}, u32[]{:S(2)}) %copy-start) | copy-done | bytes 1966104
  9.0 0.7 %copy-done.5 = bf16[3,256]{1,0:T(4,128)(2,1)S(1)} copy-done((bf16[3,256]{1,0:T(4,128)(2,1)S(1)}, bf16[3,256]{1,0:T(4,128)(2,1)}, u32[]{:S(2)}) %copy-start.5) | copy-done | bytes 1560
  9.7 2.4 %shard_map.155 = (f32[8,128]{1,0:T(8,128)S(1)}, f32[2,3,256]{2,1,0:T(4,128)S(1)}, f32[2,3,256,256]{3,2,1,0:T(8,128)S(1)}) custom-call(s32[2]{0:T(128)S(1)} %copy-done.10, f32[2,256,256]{2,1,0:T(8,128)S(1)} %get-tuple-element.29.pieces.refs_9_.own, bf16[3840,256]{1,0:T(8,128)(2,1)S(1)} %bitcast.10, bf16[3,256]{1,0:T(4,128)(2,1)S(1)} %copy-done.5), custom_call_target="tpu_custom_call" | custom-call | flops 1 | bytes 1 | tf_op jit(solution)/shard_map/pallas_call | solution.py:448
  12.1 1.2 %copy-done.2 = f32[2,3,256,256]{3,2,1,0:T(8,128)} copy-done((f32[2,3,256,256]{3,2,1,0:T(8,128)}, f32[2,3,256,256]{3,2,1,0:T(8,128)S(1)}, u32[]{:S(2)}) %copy-start.2) | copy-done | bytes 1572888
  13.3 2.0 %collective-permute-start = (f32[8,128]{1,0:T(8,128)S(1)}, f32[8,128]{1,0:T(8,128)S(1)}, u32[]{:S(2)}, u32[]{:S(2)}) collective-permute-start(f32[8,128]{1,0:T(8,128)S(1)} %get-tuple-element.31), channel_id=1, source_target_pairs={{0,1},{1,0},{2,3},{3,2},{4,5},{5,4},{6,7},{7,6},{8,9},{9,8},{10,11... | collective-permute-start | bytes 12296 | tf_op jit(solution)/shard_map/ppermute | solution.py:421
  15.3 1.6 %collective-permute-done = f32[8,128]{1,0:T(8,128)S(1)} collective-permute-done((f32[8,128]{1,0:T(8,128)S(1)}, f32[8,128]{1,0:T(8,128)S(1)}, u32[]{:S(2)}, u32[]{:S(2)}) %collective-permute-start) | collective-permute-done | bytes 4128 | tf_op jit(solution)/shard_map/ppermute | solution.py:421
  17.0 3.0 %collective-permute-start.3 = (f32[8,128]{1,0:T(8,128)S(1)}, f32[8,128]{1,0:T(8,128)S(1)}, u32[]{:S(2)}, u32[]{:S(2)}) collective-permute-start(f32[8,128]{1,0:T(8,128)S(1)} %add.3.refs_7_), channel_id=1, source_target_pairs={{0,2},{1,3},{2,0},{3,1},{4,6},{5,7},{6,4},{7,5},{8,10},{9,11},{10,... | collective-permute-start | bytes 12296 | tf_op jit(solution)/shard_map/ppermute | solution.py:421
  20.0 1.6 %collective-permute-done.3.refs_8_ = f32[8,128]{1,0:T(8,128)S(1)} collective-permute-done((f32[8,128]{1,0:T(8,128)S(1)}, f32[8,128]{1,0:T(8,128)S(1)}, u32[]{:S(2)}, u32[]{:S(2)}) %collective-permute-start.3) | collective-permute-done | bytes 4128 | tf_op jit(solution)/shard_map/ppermute | solution.py:421
  21.6 1.4 %shard_map.156 = (f32[8,128]{1,0:T(8,128)S(1)}, f32[1,2]{1,0:T(1,128)}, f32[264,256]{1,0:T(8,128)}) custom-call(s32[2]{0:T(128)S(1)} %copy-done.11, s32[2]{0:T(128)S(1)} %copy-done.12, s32[2]{0:T(128)S(1)} %copy-done.13, f32[2]{0:T(128)S(1)} %copy-done.14, f32[840]{0:T(1024)S(1)} %copy-done.9, f32[40]{0:T(128)S(1)} %copy-done.15, f32[8]{0:T(128)S(1)} %copy-done.16, ...), custom_call_target="tpu_custom_call" | custom-call | flops 1 | bytes 1 | tf_op jit(solution)/shard_map/pallas_call | solution.py:463
  23.0 1.9 %collective-permute-start.7 = (f32[264,256]{1,0:T(8,128)}, f32[264,256]{1,0:T(8,128)}, u32[]{:S(2)}, u32[]{:S(2)}) collective-permute-start(f32[264,256]{1,0:T(8,128)} %get-tuple-element.40), channel_id=1, source_target_pairs={{0,16},{4,20},{8,24},{12,28},{16,0},{20,4},{24,8},{28,12},{1,17},{... | collective-permute-start | bytes 811016 | tf_op jit(solution)/shard_map/ppermute | solution.py:421
  24.9 1.5 %collective-permute-start.6 = (f32[264,256]{1,0:T(8,128)}, f32[264,256]{1,0:T(8,128)}, u32[]{:S(2)}, u32[]{:S(2)}) collective-permute-start(f32[264,256]{1,0:T(8,128)} %get-tuple-element.40), channel_id=1, source_target_pairs={{0,8},{4,12},{8,0},{12,4},{16,24},{20,28},{24,16},{28,20},{1,9},{5... | collective-permute-start | bytes 811016 | tf_op jit(solution)/shard_map/ppermute | solution.py:421
  26.5 4.7 %collective-permute-done.5.far_facts.refs_5_ = f32[8,128]{1,0:T(8,128)S(1)} collective-permute-done((f32[8,128]{1,0:T(8,128)S(1)}, f32[8,128]{1,0:T(8,128)S(1)}, u32[]{:S(2)}, u32[]{:S(2)}) %collective-permute-start.5) | collective-permute-done | bytes 4128 | tf_op jit(solution)/shard_map/ppermute | solution.py:421
  31.2 1.4 %copy-done.3 = f32[2,3,256,256]{3,2,1,0:T(8,128)S(1)} copy-done((f32[2,3,256,256]{3,2,1,0:T(8,128)S(1)}, f32[2,3,256,256]{3,2,1,0:T(8,128)}, u32[]{:S(2)}) %copy-start.3) | copy-done | bytes 1572888
  32.6 5.6 %shard_map.157 = (f32[480,256]{1,0:T(8,128)S(1)}, f32[480,256]{1,0:T(8,128)S(1)}, f32[2,8,256]{2,1,0:T(8,128)S(1)}, f32[2,8,256]{2,1,0:T(8,128)S(1)}, f32[2,3,256,256]{3,2,1,0:T(8,128)S(1)}) custom-call(s32[1]{0:T(128)} %bitcast.d_ref, f32[2,3,256,256]{3,2,1,0:T(8,128)S(1)} %copy-done.3, f32[8,128]{1,0:T(8,128)S(1)} %get-tuple-element.34.facts.refs_4_, ...), custom_call_target="tpu_custom_call" | custom-call | flops 1 | bytes 1 | tf_op jit(solution)/shard_map/pallas_call | solution.py:475
  38.2 4.0 %shard_map.158 = (f32[480,256]{1,0:T(8,128)S(1)}, f32[480,256]{1,0:T(8,128)S(1)}, f32[16,256]{1,0:T(8,128)S(1)}) custom-call(s32[1]{0:T(128)} %bitcast.d_ref, f32[480,256]{1,0:T(8,128)S(1)} %get-tuple-element.37.in_own, f32[480,256]{1,0:T(8,128)S(1)} %get-tuple-element.38.in_other, f32[2,3,256,256]{3,2,1,0:T(8,128)S(1)} %get-tuple-element.39.share_near, ...), custom_call_target="tpu_custom_call" | custom-call | flops 1 | bytes 1 | tf_op jit(solution)/shard_map/pallas_call | solution.py:482
  42.8 1.4 %collective-permute-done.9.came_ref = f32[16,256]{1,0:T(8,128)S(1)} collective-permute-done((f32[16,256]{1,0:T(8,128)S(1)}, f32[16,256]{1,0:T(8,128)S(1)}, u32[]{:S(2)}, u32[]{:S(2)}) %collective-permute-start.9) | collective-permute-done | bytes 16416 | tf_op jit(solution)/shard_map/ppermute | solution.py:421
  44.2 0.6 %shard_map.160 = (f32[3,256]{1,0:T(4,128)}, f32[1,840]{1,0:T(1,128)S(1)}, f32[1,40]{1,0:T(1,128)}, f32[1,8]{1,0:T(1,128)}) custom-call(f32[16,256]{1,0:T(8,128)S(1)} %get-tuple-element.46.mine_ref, f32[16,256]{1,0:T(8,128)S(1)} %collective-permute-done.9.came_ref), custom_call_target="tpu_custom_call" | custom-call | flops 1 | bytes 1 | tf_op jit(solution)/shard_map/pallas_call | solution.py:510
  44.8 0.6 %reduce = f32[840]{0:T(1024)} reduce(f32[1,840]{1,0:T(1,128)S(1)} %get-tuple-element.48, f32[]{:T(128)} %constant.12), dimensions={0}, to_apply=%get-tuple-element.48.reduce_sub_computation | reduce | bytes 6724 | tf_op jit(solution)/shard_map/pallas_call | solution.py:510
  45.4 0.8 %shard_map.159 = f32[480,256]{1,0:T(8,128)} custom-call(f32[480,256]{1,0:T(8,128)S(1)} %get-tuple-element.44.mine_ref, f32[480,256]{1,0:T(8,128)S(1)} %collective-permute-done.8.came_ref), custom_call_target="tpu_custom_call" | custom-call | flops 1 | bytes 1 | tf_op jit(solution)/shard_map/pallas_call | solution.py:517
  (39 shorter events, 0.8 us)
Async XLA Ops:
  2.2 19.3 %copy-start.9 = (f32[840]{0:T(1024)S(1)}, f32[840]{0:T(1024)}, u32[]{:S(2)}) copy-start(f32[840]{0:T(1024)} %refs_4_.1) | copy-start | bytes 10084
  2.2 19.3 %copy-start.11 = (s32[2]{0:T(128)S(1)}, s32[2]{0:T(128)}, u32[]{:S(2)}) copy-start(s32[2]{0:T(128)} %refs_0_.1) | copy-start | bytes 28
  2.2 19.3 %copy-start.12 = (s32[2]{0:T(128)S(1)}, s32[2]{0:T(128)}, u32[]{:S(2)}) copy-start(s32[2]{0:T(128)} %refs_1_.1) | copy-start | bytes 28
  2.2 19.3 %copy-start.13 = (s32[2]{0:T(128)S(1)}, s32[2]{0:T(128)}, u32[]{:S(2)}) copy-start(s32[2]{0:T(128)} %refs_2_.1) | copy-start | bytes 28
  2.3 19.3 %copy-start.14 = (f32[2]{0:T(128)S(1)}, f32[2]{0:T(128)}, u32[]{:S(2)}) copy-start(f32[2]{0:T(128)} %refs_3_.2) | copy-start | bytes 28
  2.3 19.3 %copy-start.15 = (f32[40]{0:T(128)S(1)}, f32[40]{0:T(128)}, u32[]{:S(2)}) copy-start(f32[40]{0:T(128)} %refs_5_.1) | copy-start | bytes 484
  2.3 19.3 %copy-start.16 = (f32[8]{0:T(128)S(1)}, f32[8]{0:T(128)}, u32[]{:S(2)}) copy-start(f32[8]{0:T(128)} %refs_6_.1) | copy-start | bytes 100
  2.9 28.3 %copy-start.6 = (bf16[3,256]{1,0:T(4,128)(2,1)S(1)}, bf16[3,256]{1,0:T(4,128)(2,1)}, u32[]{:S(2)}) copy-start(bf16[3,256]{1,0:T(4,128)(2,1)} %refs_10_.1) | copy-start | bytes 4612
  2.9 18.7 %collective-permute-start.2 = (f32[256,256]{1,0:T(8,128)S(1)}, f32[256,256]{1,0:T(8,128)S(1)}, u32[]{:S(2)}, u32[]{:S(2)}) collective-permute-start(f32[256,256]{1,0:T(8,128)S(1)} %get-tuple-element.32), channel_id=1, source_target_pairs={{0,16},{4,20},{8,24},{12,28},{16,0},{20,4},{24,8},{28,12},{1,17},{... | collective-permute-start | bytes 786440 | tf_op jit(solution)/shard_map/ppermute | solution.py:421
  5.9 15.6 %collective-permute-start.1 = (f32[256,256]{1,0:T(8,128)S(1)}, f32[256,256]{1,0:T(8,128)S(1)}, u32[]{:S(2)}, u32[]{:S(2)}) collective-permute-start(f32[256,256]{1,0:T(8,128)S(1)} %get-tuple-element.32), channel_id=1, source_target_pairs={{0,8},{4,12},{8,0},{12,4},{16,24},{20,28},{24,16},{28,20},{1,9},{5... | collective-permute-start | bytes 786440 | tf_op jit(solution)/shard_map/ppermute | solution.py:421
  7.4 23.7 %collective-permute-start.4 = (f32[2,256,256]{2,1,0:T(8,128)S(1)}, f32[2,256,256]{2,1,0:T(8,128)S(1)}, u32[]{:S(2)}, u32[]{:S(2)}) collective-permute-start(f32[2,256,256]{2,1,0:T(8,128)S(1)} %get-tuple-element.29.pieces.refs_9_.own), channel_id=1, source_target_pairs={{0,24},{4,28},{8,16},{12,20},{16,8},{20,12},{24,0},{28,4},{1,25},{... | collective-permute-start | bytes 1572872 | tf_op jit(solution)/shard_map/ppermute | solution.py:421
  7.5 1.5 %copy-start = (bf16[256,15,256]{2,0,1:T(8,128)(2,1)S(1)}, bf16[256,15,256]{2,0,1:T(8,128)(2,1)}, u32[]{:S(2)}) copy-start(bf16[256,15,256]{2,0,1:T(8,128)(2,1)} %param.13) | copy-start | bytes 5898244
  9.7 21.5 %copy-start.1 = (bf16[256,15,256]{2,0,1:T(8,128)(2,1)S(1)}, bf16[256,15,256]{2,0,1:T(8,128)(2,1)}, u32[]{:S(2)}) copy-start(bf16[256,15,256]{2,0,1:T(8,128)(2,1)} %param.13) | copy-start | bytes 5898244
  12.1 1.2 %copy-start.2 = (f32[2,3,256,256]{3,2,1,0:T(8,128)}, f32[2,3,256,256]{3,2,1,0:T(8,128)S(1)}, u32[]{:S(2)}) copy-start(f32[2,3,256,256]{3,2,1,0:T(8,128)S(1)} %get-tuple-element.30.share_own) | copy-start | bytes 4718596
  13.3 13.0 %copy-start.7 = (f32[2,3,256]{2,1,0:T(4,128)}, f32[2,3,256]{2,1,0:T(4,128)S(1)}, u32[]{:S(2)}) copy-start(f32[2,3,256]{2,1,0:T(4,128)S(1)} %get-tuple-element.41.refs_6_) | copy-start | bytes 18436
  13.3 3.6 %collective-permute-start = (f32[8,128]{1,0:T(8,128)S(1)}, f32[8,128]{1,0:T(8,128)S(1)}, u32[]{:S(2)}, u32[]{:S(2)}) collective-permute-start(f32[8,128]{1,0:T(8,128)S(1)} %get-tuple-element.31), channel_id=1, source_target_pairs={{0,1},{1,0},{2,3},{3,2},{4,5},{5,4},{6,7},{7,6},{8,9},{9,8},{10,11... | collective-permute-start | bytes 12296 | tf_op jit(solution)/shard_map/ppermute | solution.py:421
  17.0 4.6 %collective-permute-start.3 = (f32[8,128]{1,0:T(8,128)S(1)}, f32[8,128]{1,0:T(8,128)S(1)}, u32[]{:S(2)}, u32[]{:S(2)}) collective-permute-start(f32[8,128]{1,0:T(8,128)S(1)} %add.3.refs_7_), channel_id=1, source_target_pairs={{0,2},{1,3},{2,0},{3,1},{4,6},{5,7},{6,4},{7,5},{8,10},{9,11},{10,... | collective-permute-start | bytes 12296 | tf_op jit(solution)/shard_map/ppermute | solution.py:421
  23.0 15.2 %collective-permute-start.7 = (f32[264,256]{1,0:T(8,128)}, f32[264,256]{1,0:T(8,128)}, u32[]{:S(2)}, u32[]{:S(2)}) collective-permute-start(f32[264,256]{1,0:T(8,128)} %get-tuple-element.40), channel_id=1, source_target_pairs={{0,16},{4,20},{8,24},{12,28},{16,0},{20,4},{24,8},{28,12},{1,17},{... | collective-permute-start | bytes 811016 | tf_op jit(solution)/shard_map/ppermute | solution.py:421
  24.9 13.4 %collective-permute-start.6 = (f32[264,256]{1,0:T(8,128)}, f32[264,256]{1,0:T(8,128)}, u32[]{:S(2)}, u32[]{:S(2)}) collective-permute-start(f32[264,256]{1,0:T(8,128)} %get-tuple-element.40), channel_id=1, source_target_pairs={{0,8},{4,12},{8,0},{12,4},{16,24},{20,28},{24,16},{28,20},{1,9},{5... | collective-permute-start | bytes 811016 | tf_op jit(solution)/shard_map/ppermute | solution.py:421
  26.4 4.8 %collective-permute-start.5 = (f32[8,128]{1,0:T(8,128)S(1)}, f32[8,128]{1,0:T(8,128)S(1)}, u32[]{:S(2)}, u32[]{:S(2)}) collective-permute-start(f32[8,128]{1,0:T(8,128)S(1)} %get-tuple-element.34.facts.refs_4_), channel_id=1, source_target_pairs={{0,24},{4,28},{8,16},{12,20},{16,8},{20,12},{24,0},{28,4},{1,25},{... | collective-permute-start | bytes 12296 | tf_op jit(solution)/shard_map/ppermute | solution.py:421
  31.2 1.4 %copy-start.3 = (f32[2,3,256,256]{3,2,1,0:T(8,128)S(1)}, f32[2,3,256,256]{3,2,1,0:T(8,128)}, u32[]{:S(2)}) copy-start(f32[2,3,256,256]{3,2,1,0:T(8,128)} %copy-done.2) | copy-start | bytes 4718596
  32.6 5.6 %copy-start.8 = (f32[2,3,256]{2,1,0:T(4,128)S(1)}, f32[2,3,256]{2,1,0:T(4,128)}, u32[]{:S(2)}) copy-start(f32[2,3,256]{2,1,0:T(4,128)} %copy-done.7) | copy-start | bytes 18436
  42.3 3.2 %collective-permute-start.8 = (f32[480,256]{1,0:T(8,128)S(1)}, f32[480,256]{1,0:T(8,128)S(1)}, u32[]{:S(2)}, u32[]{:S(2)}) collective-permute-start(f32[480,256]{1,0:T(8,128)S(1)} %get-tuple-element.45), channel_id=1, source_target_pairs={{0,4},{4,0},{8,12},{12,8},{16,20},{20,16},{24,28},{28,24},{1,5},{5... | collective-permute-start | bytes 1474568 | tf_op jit(solution)/shard_map/ppermute | solution.py:421
  42.4 1.9 %collective-permute-start.9 = (f32[16,256]{1,0:T(8,128)S(1)}, f32[16,256]{1,0:T(8,128)S(1)}, u32[]{:S(2)}, u32[]{:S(2)}) collective-permute-start(f32[16,256]{1,0:T(8,128)S(1)} %get-tuple-element.46.mine_ref), channel_id=1, source_target_pairs={{0,4},{4,0},{8,12},{12,8},{16,20},{20,16},{24,28},{28,24},{1,5},{5... | collective-permute-start | bytes 49160 | tf_op jit(solution)/shard_map/ppermute | solution.py:421
  (3 other events, 2.3 us)

commit v3 on v0

--- a/solution.py
+++ b/solution.py
@@ -1,10 +1,20 @@
+import functools
+
 import jax
 import jax.numpy as jnp
+import numpy as np
 from jax import lax
+from jax.experimental import pallas as pl
+from jax.experimental.pallas import tpu as pltpu
 from jax.sharding import PartitionSpec as P
 
 TAU = 0.05
 WIDTH_LIST = ((3, 0), (5, 3), (7, 8))
+TAPS = 15
+REACH = 3
+PAD = 8
+OUTSIDE = np.float32(1024.0)
+BY_LAST = (((1,), (1,)), ((), ()))
 
 
 def convolve(columns, weights):
@@ -35,7 +45,11 @@
     return jnp.concatenate(outputs, axis=1)
 
 
-def local(
+def one_hots(codes, size):
+    return (codes[:, None] == jnp.arange(size, dtype=jnp.int32)[None, :]).astype(jnp.float32)
+
+
+def local_scatter(
     embedded,
     lengths,
     conv_weight,
@@ -67,15 +81,9 @@
     feature = jnp.stack(features, axis=1)
     head = head_weight.astype(jnp.float32)
     partial_pred = jnp.sum(feature * head[None, :, :], axis=(1, 2))
-    occ_hot = (
-        occupation[:, None] == jnp.arange(occ_table.shape[0], dtype=jnp.int32)[None, :]
-    ).astype(jnp.float32)
-    cohort_hot = (
-        cohort[:, None] == jnp.arange(cohort_table.shape[0], dtype=jnp.int32)[None, :]
-    ).astype(jnp.float32)
-    edu_hot = (
-        education[:, None] == jnp.arange(edu_table.shape[0], dtype=jnp.int32)[None, :]
-    ).astype(jnp.float32)
+    occ_hot = one_hots(occupation, occ_table.shape[0])
+    cohort_hot = one_hots(cohort, cohort_table.shape[0])
+    edu_hot = one_hots(education, edu_table.shape[0])
     highest = lax.Precision.HIGHEST
     offsets = (
         jnp.dot(occ_hot, occ_table, precision=highest)
@@ -104,7 +112,463 @@
     return (conv_grad, head_grad, occ_grad, cohort_grad, edu_grad, prediction)
 
 
+def load_post(x, xpad, count):
+    rows, width = x.shape
+    inside = x < OUTSIDE
+    xpad[0:PAD, :] = jnp.zeros((PAD, width), jnp.float32)
+    xpad[PAD + rows :, :] = jnp.zeros((PAD, width), jnp.float32)
+    xpad[PAD : PAD + rows, :] = jnp.where(inside, x, 0.0)
+    total = jnp.sum(inside.astype(jnp.float32), axis=0, keepdims=True)
+    count[...] = jnp.broadcast_to(total[:, 0:1], count.shape)
+
+
+def make_cols(xpad, cols):
+    rows, width = cols.shape[0], xpad.shape[1]
+    for offset in range(2 * REACH + 1):
+        start = PAD - REACH + offset
+        cols[:, offset * width : (offset + 1) * width] = xpad[start : start + rows, :].astype(
+            jnp.bfloat16
+        )
+
+
+def forward(index, cols, w_ref, head, count):
+    taps, first = WIDTH_LIST[index]
+    half = taps // 2
+    width = w_ref.shape[0] // TAPS
+    conv = jnp.dot(
+        cols[:, (REACH - half) * width : (REACH + half + 1) * width],
+        w_ref[first * width : (first + taps) * width, :],
+        preferred_element_type=jnp.float32,
+    )
+    place = lax.broadcasted_iota(jnp.int32, conv.shape, 0).astype(jnp.float32)
+    score = jnp.where(place < count[0:1, :], conv * np.float32(1.0 / TAU), -jnp.inf)
+    top = jnp.max(score, axis=0, keepdims=True)
+    expd = jnp.exp(score - top)
+    total = jnp.sum(expd, axis=0, keepdims=True)
+    feature = np.float32(TAU) * (top + jnp.log(total))
+    return feature, expd * (head[index : index + 1] / total)
+
+
+def pick_rows(d_ref, middle, slice_e):
+    rows, width = middle.shape
+    me = d_ref[0]
+    row = lax.broadcasted_iota(jnp.int32, (2 * slice_e, width), 0)
+    lane = lax.broadcasted_iota(jnp.int32, (2 * slice_e, width), 1)
+    wanted = jnp.where(row < slice_e, me * slice_e + row, (me ^ 1) * slice_e + row - slice_e)
+    pick = (lane == wanted).astype(jnp.bfloat16)
+    across = lax.dot_general(pick, middle, BY_LAST, preferred_element_type=jnp.float32)
+    place = lax.broadcasted_iota(jnp.int32, (2 * slice_e, rows), 1)
+    parts = []
+    for offset in range(-REACH, REACH + 1):
+        if offset:
+            moved = pltpu.roll(across, (-offset) % rows, 1)
+            inside = (place + offset >= 0) & (place + offset < rows)
+            parts.append(jnp.where(inside, moved, 0.0))
+        else:
+            parts.append(across)
+    return jnp.concatenate(parts, axis=0).astype(jnp.bfloat16)
+
+
+def middle_of(cols):
+    width = cols.shape[1] // (2 * REACH + 1)
+    return cols[:, REACH * width : (REACH + 1) * width]
+
+
+def add_terms(at, slopes, acc_own, acc_other, slice_e, fresh=False):
+    step = 2 * slice_e
+    for index, (taps, first) in enumerate(WIDTH_LIST):
+        half = taps // 2
+        term = jnp.dot(
+            at[(REACH - half) * step : (REACH + half + 1) * step],
+            slopes[index],
+            preferred_element_type=jnp.float32,
+        )
+        for j in range(taps):
+            place = slice((first + j) * slice_e, (first + j + 1) * slice_e)
+            own = term[j * step : j * step + slice_e]
+            other = term[j * step + slice_e : (j + 1) * step]
+            if fresh:
+                acc_own[place, :] = own
+                acc_other[place, :] = other
+            else:
+                acc_own[place, :] += own
+                acc_other[place, :] += other
+
+
+def mask_kernel(len_any, x_any, pieces, x_ref, len_ref, sems):
+    posts, rows, width = x_ref.shape
+    copies = [pltpu.make_async_copy(len_any, len_ref, sems.at[posts])]
+    copies += [pltpu.make_async_copy(x_any.at[p], x_ref.at[p], sems.at[p]) for p in range(posts)]
+    for copy in copies:
+        copy.start()
+    place = lax.broadcasted_iota(jnp.int32, (rows, width), 0)
+    copies[0].wait()
+    for p in range(posts):
+        copies[1 + p].wait()
+        pieces[p] = jnp.where(place < len_ref[p], x_ref[p].astype(jnp.float32), OUTSIDE)
+
+
+def own_kernel(*refs):
+    small = refs[:8]
+    w_any, pieces, part_ref, feat_ref, share_ref, base_ref = refs[8:14]
+    held = refs[14:22]
+    w_ref, xpad, cols, counts, small_sems, w_sems = refs[22:]
+    posts = pieces.shape[0]
+    width = w_ref.shape[0] // TAPS
+    loads = []
+    for tap in range(TAPS):
+        place = pl.ds(tap * width, width)
+        loads.append(pltpu.make_async_copy(w_any.at[place], w_ref.at[place], w_sems.at[tap]))
+    copies = [pltpu.make_async_copy(small[i], held[i], small_sems.at[i]) for i in range(8)]
+    for load in loads[::-1]:
+        load.start()
+    for copy in copies:
+        copy.start()
+    for p in range(posts):
+        load_post(pieces[p], xpad.at[p], counts.at[p])
+        make_cols(xpad.at[p], cols.at[p])
+    copies[7].wait()
+    head = held[7][...].astype(jnp.float32)
+    parts = [jnp.zeros((1, head.shape[1]), jnp.float32) for _ in range(posts)]
+    for index in (2, 1, 0):
+        taps, first = WIDTH_LIST[index]
+        for load in loads[first : first + taps]:
+            load.wait()
+        for p in range(posts):
+            feature, share = forward(index, cols.at[p], w_ref, head, counts.at[p])
+            feat_ref[p, index : index + 1, :] = feature
+            share_ref[p, index] = share
+            parts[p] = parts[p] + feature * head[index : index + 1]
+    lanes = part_ref.shape[1]
+    part_ref[...] = jnp.zeros_like(part_ref)
+    for p in range(posts):
+        total = jnp.sum(parts[p], axis=1, keepdims=True)
+        part_ref[p : p + 1, :] = jnp.broadcast_to(total, (1, lanes))
+    for copy in copies[:7]:
+        copy.wait()
+    codes, wage_ref, tables = held[:3], held[3], held[4:7]
+    base_ref[...] = jnp.zeros_like(base_ref)
+    for p in range(posts):
+        offset = sum(table[code[p]] for code, table in zip(codes, tables))
+        values = [offset] + [code[p].astype(jnp.float32) for code in codes] + [wage_ref[p]]
+        for kind, value in enumerate(values):
+            row = kind * posts + p
+            base_ref[row : row + 1, :] = jnp.full((1, lanes), value, jnp.float32)
+
+
+def own_terms_kernel(slice_e, d_ref, pieces, share_ref, own_ref, other_ref):
+    for p in range(pieces.shape[0]):
+        x = pieces[p]
+        at = pick_rows(d_ref, jnp.where(x < OUTSIDE, x, 0.0).astype(jnp.bfloat16), slice_e)
+        slopes = [share_ref[p, index].astype(jnp.bfloat16) for index in range(3)]
+        add_terms(at, slopes, own_ref.at[p], other_ref.at[p], slice_e, fresh=True)
+
+
+def facts_kernel(one, two, base, keep_own, keep_other, facts_ref, pred_ref):
+    posts = pred_ref.shape[0]
+    facts_ref[...] = base[...]
+    for p in range(posts):
+        value = one[p : p + 1, :] + two[p : p + 1, :] + base[p : p + 1, :]
+        pred_ref[pl.ds(p, 1)] = value[0, 0:1]
+        facts_ref[p : p + 1, :] = value - base[4 * posts + p : 4 * posts + p + 1, :]
+
+
+def first_kernel(n_near, slice_e, d_ref, terms_own, terms_other, facts, *refs):
+    near = refs[:n_near]
+    w_ref, head_ref, acc_own, acc_other, feat_near, near_own, near_other = refs[n_near : n_near + 7]
+    xs, sems, xpads, counts, cols = refs[n_near + 7 :]
+    posts = terms_own.shape[0]
+    copies = []
+    for k in range(n_near):
+        for p in range(posts):
+            i = k * posts + p
+            copies.append(pltpu.make_async_copy(near[k].at[p], xs.at[i], sems.at[i]))
+            copies[-1].start()
+    head = head_ref[...].astype(jnp.float32)
+    for acc, terms in ((acc_own, terms_own), (acc_other, terms_other)):
+        acc[...] = sum(facts[p : p + 1, 0:1] * terms[p] for p in range(posts))
+    for i, copy in enumerate(copies):
+        copy.wait()
+        load_post(xs[i], xpads.at[i], counts.at[i])
+
+    def near_posts(k, carry):
+        for p in range(posts):
+            make_cols(xpads.at[k * posts + p], cols.at[p])
+        for p in range(posts):
+            i = k * posts + p
+            slopes = []
+            for index in range(3):
+                feature, share = forward(index, cols.at[p], w_ref, head, counts.at[i])
+                feat_near[i, index : index + 1, :] = feature
+                slopes.append(share.astype(jnp.bfloat16))
+            at = pick_rows(d_ref, middle_of(cols.at[p]), slice_e)
+            add_terms(at, slopes, near_own.at[i], near_other.at[i], slice_e, fresh=True)
+        return carry
+
+    lax.fori_loop(0, n_near, near_posts, 0)
+
+
+def last_kernel(n_near, sizes, slice_e, d_ref, in_own, in_other, near_own, near_other, *refs):
+    near_facts = refs[:n_near]
+    facts, far_facts, feat_own, feat_near, far = refs[n_near : n_near + 5]
+    w_ref, head_ref, acc_own, acc_other = refs[n_near + 5 : n_near + 9]
+    xs, sems, xpads, counts, cols = refs[n_near + 9 :]
+    posts = feat_own.shape[0]
+    copies = []
+    for p in range(posts):
+        copies.append(pltpu.make_async_copy(far.at[p], xs.at[p], sems.at[p]))
+        copies[-1].start()
+    n_rows, filters = in_own.shape
+    head = head_ref[...].astype(jnp.float32)
+    for acc, start, terms in ((acc_own, in_own, near_own), (acc_other, in_other, near_other)):
+        total = start[...]
+        for k in range(n_near):
+            for p in range(posts):
+                total = total + near_facts[k][p : p + 1, 0:1] * terms[k * posts + p]
+        acc[0:n_rows, :] = total
+
+    for p in range(posts):
+        copies[p].wait()
+        load_post(xs[p], xpads.at[p], counts.at[p])
+        make_cols(xpads.at[p], cols.at[p])
+    slopes = [[], [], []]
+    feat_far = [[], []]
+    for p in range(posts):
+        for index in range(3):
+            feature, share = forward(index, cols.at[p], w_ref, head, counts.at[p])
+            feat_far[p].append(feature)
+            slopes[index].append((far_facts[p : p + 1, 0:1] * share).astype(jnp.bfloat16))
+    at = jnp.concatenate([pick_rows(d_ref, middle_of(cols.at[p]), slice_e) for p in range(posts)], axis=1)
+    slopes = [jnp.concatenate(parts, axis=0) for parts in slopes]
+    add_terms(at, slopes, acc_own, acc_other, slice_e)
+
+    n_codes = code_rows(sizes, filters)
+    place = lax.broadcasted_iota(jnp.int32, (n_codes, filters), 0) * filters
+    place = place + lax.broadcasted_iota(jnp.int32, (n_codes, filters), 1)
+
+    def chip_terms(told, feature):
+        head_term = jnp.zeros((3, filters), jnp.float32)
+        code_term = jnp.zeros((n_codes, filters), jnp.float32)
+        for p in range(posts):
+            residual = told[p : p + 1, 0:1]
+            head_term = head_term + residual * feature[p]
+            for kind, start in enumerate(code_starts(sizes, filters)):
+                at_row = (kind + 1) * posts + p
+                code = told[at_row : at_row + 1, 0:1].astype(jnp.int32) + start
+                code_term = code_term + jnp.where(place == code, residual, 0.0)
+        return head_term, code_term
+
+    terms = [
+        chip_terms(facts[...], [feat_own[p] for p in range(posts)]),
+        *[
+            chip_terms(
+                near_facts[k][...], [feat_near[k * posts + p, 0:3, :] for p in range(posts)]
+            )
+            for k in range(n_near)
+        ],
+        chip_terms(far_facts[...], [jnp.concatenate(parts, axis=0) for parts in feat_far]),
+    ]
+    acc_other[n_rows:, :] = jnp.zeros((acc_other.shape[0] - n_rows, filters), jnp.float32)
+    acc_other[n_rows : n_rows + 3, :] = tree_sum([term[0] for term in terms])
+    acc_other[n_rows + 3 : n_rows + 3 + n_codes, :] = tree_sum([term[1] for term in terms])
+
+
+def tree_sum(values):
+    while len(values) > 1:
+        values = [values[i] + values[i + 1] for i in range(0, len(values), 2)]
+    return values[0]
+
+
+def code_starts(sizes, filters):
+    starts, start = [], 0
+    for size in sizes:
+        starts.append(start)
+        start += -(-size // filters) * filters
+    return starts
+
+
+def code_rows(sizes, filters):
+    return sum(-(-size // filters) for size in sizes)
+
+
+def swap_kernel(sizes, own_ref, mine_ref, came_ref, grad_ref, head_ref, *code_refs):
+    n_rows, filters = own_ref.shape
+    grad_ref[...] = own_ref[...] + came_ref[0:n_rows, :]
+    head_ref[...] = mine_ref[n_rows : n_rows + 3, :] + came_ref[n_rows : n_rows + 3, :]
+    row = n_rows + 3
+    for size, ref in zip(sizes, code_refs):
+        for start in range(0, size, filters):
+            count = min(filters, size - start)
+            total = mine_ref[row : row + 1, :] + came_ref[row : row + 1, :]
+            ref[pl.ds(start, count)] = total[0, :count]
+            row += 1
+
+
+def local_gather(n_doc, n_filt, *args):
+    (
+        embedded,
+        lengths,
+        conv_weight,
+        head_weight,
+        occupation,
+        cohort,
+        education,
+        occ_table,
+        cohort_table,
+        edu_table,
+        wage,
+    ) = args
+    posts, seq_len, dims = embedded.shape
+    filters = conv_weight.shape[2]
+    slice_e = dims // n_doc
+    sizes = (occ_table.shape[0], cohort_table.shape[0], edu_table.shape[0])
+    f32, i32 = jnp.float32, jnp.int32
+    me = lax.axis_index("doc").astype(i32).reshape(1)
+    vmem = pl.BlockSpec(memory_space=pltpu.VMEM)
+    smem = pl.BlockSpec(memory_space=pltpu.SMEM)
+    anywhere = pl.BlockSpec(memory_space=pl.ANY)
+    hbm = pl.BlockSpec(memory_space=pltpu.HBM)
+
+    def arrived_scratch(n):
+        return [pltpu.VMEM((n, seq_len, dims), f32), pltpu.SemaphoreType.DMA((n,))]
+
+    def posts_scratch(n):
+        return [
+            pltpu.VMEM((n, seq_len + 2 * PAD, dims), f32),
+            pltpu.VMEM((n, 8, filters), f32),
+            pltpu.VMEM((posts, seq_len, (2 * REACH + 1) * dims), jnp.bfloat16),
+        ]
+
+    def swap(x, k, axis="doc"):
+        size = n_doc if axis == "doc" else n_filt
+        return lax.ppermute(x, axis, [(i, i ^ k) for i in range(size)])
+
+    def call(kernel, specs, out, scratch=()):
+        def run(*operands):
+            operands = [
+                pltpu.with_memory_space_constraint(x, pltpu.HBM) if spec is hbm else x
+                for x, spec in zip(operands, specs)
+            ]
+            return built(*operands)
+
+        built = pl.pallas_call(
+            kernel,
+            in_specs=specs,
+            out_specs=[vmem] * len(out),
+            out_shape=[jax.ShapeDtypeStruct(shape, f32) for shape in out],
+            scratch_shapes=list(scratch),
+            compiler_params=pltpu.CompilerParams(vmem_limit_bytes=24 << 20),
+            cost_estimate=pl.CostEstimate(flops=1, bytes_accessed=1, transcendentals=0),
+        )
+        return run
+
+    weights = jnp.transpose(conv_weight, (1, 0, 2)).reshape(TAPS * dims, filters)
+    (pieces,) = call(
+        mask_kernel,
+        [hbm] * 2,
+        [(posts, seq_len, dims)],
+        [
+            pltpu.VMEM((posts, seq_len, dims), jnp.bfloat16),
+            pltpu.SMEM((posts,), i32),
+            pltpu.SemaphoreType.DMA((posts + 1,)),
+        ],
+    )(lengths, embedded)
+
+    near = [k for k in range(2, n_doc, 2) if bin(k).count("1") == 1][::-1]
+    far = sum(near)
+    n_near = len(near)
+    near_pieces = [swap(pieces, k) for k in near]
+    far_pieces = swap(pieces, far)
+
+    n_facts = -(-5 * posts // 8) * 8
+    part, feat_own, share_own, base = call(
+        own_kernel,
+        [hbm] * 9 + [vmem],
+        [(8, 128), (posts, 3, filters), (posts, 3, seq_len, filters), (n_facts, 128)],
+        [pltpu.SMEM((posts,), i32)] * 3
+        + [pltpu.SMEM((posts,), f32)]
+        + [pltpu.SMEM((size,), f32) for size in sizes]
+        + [pltpu.VMEM(head_weight.shape, head_weight.dtype)]
+        + [pltpu.VMEM(weights.shape, weights.dtype)]
+        + [posts_scratch(posts)[i] for i in (0, 2, 1)]
+        + [pltpu.SemaphoreType.DMA((8,)), pltpu.SemaphoreType.DMA((TAPS,))],
+    )(
+        occupation,
+        cohort,
+        education,
+        wage,
+        occ_table,
+        cohort_table,
+        edu_table,
+        head_weight,
+        weights,
+        pieces,
+    )
+    acc_shape = (TAPS * slice_e, filters)
+    terms_own, terms_other = call(
+        functools.partial(own_terms_kernel, slice_e),
+        [smem] + [vmem] * 2,
+        [(posts,) + acc_shape] * 2,
+    )(me, pieces, share_own)
+
+    k = 1
+    while 2 * k < n_filt:
+        part = part + swap(part, k, "filt")
+        part, terms_own, terms_other = lax.optimization_barrier((part, terms_own, terms_other))
+        k *= 2
+    other = swap(part, k, "filt")
+    near_pieces, other = lax.optimization_barrier((near_pieces, other))
+    facts, prediction = call(
+        facts_kernel, [vmem] * 3 + [anywhere] * 2, [(n_facts, 128), (posts,)]
+    )(part, other, base, terms_own, terms_other)
+
+    near_facts = [swap(facts, k) for k in near]
+    far_facts = swap(facts, far)
+
+    near_shape = (n_near * posts,) + acc_shape
+    acc_own, acc_other, feat_near, near_own, near_other = call(
+        functools.partial(first_kernel, n_near, slice_e),
+        [smem] + [vmem] * 3 + [hbm] * n_near + [vmem] * 2,
+        [acc_shape, acc_shape, (n_near * posts, 8, filters), near_shape, near_shape],
+        arrived_scratch(n_near * posts) + posts_scratch(n_near * posts),
+    )(me, terms_own, terms_other, facts, *near_pieces, weights, head_weight)
+    extra = -(-(3 + code_rows(sizes, filters)) // 8) * 8
+    acc_own, acc_other = call(
+        functools.partial(last_kernel, n_near, sizes, slice_e),
+        [smem] + [vmem] * (4 + n_near + 4) + [hbm] + [vmem] * 2,
+        [acc_shape, (acc_shape[0] + extra, filters)],
+        arrived_scratch(posts) + posts_scratch(posts),
+    )(
+        me,
+        acc_own,
+        acc_other,
+        near_own,
+        near_other,
+        *near_facts,
+        facts,
+        far_facts,
+        feat_own,
+        feat_near,
+        far_pieces,
+        weights,
+        head_weight,
+    )
+
+    grad, head_grad, *codes = call(
+        functools.partial(swap_kernel, sizes),
+        [vmem] * 3,
+        [acc_shape, (3, filters)] + [(size,) for size in sizes],
+    )(acc_own, acc_other, swap(acc_other, 1))
+    conv_grad = jnp.transpose(grad.reshape(TAPS, slice_e, filters), (1, 0, 2))
+    return (conv_grad, head_grad, *codes, prediction)
+
+
 def solution(mesh):
+    n_doc, n_filt = mesh.shape["doc"], mesh.shape["filt"]
+    if n_doc == 8 and n_filt in (2, 4):
+        local = functools.partial(local_gather, n_doc, n_filt)
+    else:
+        local = local_scatter
     return jax.shard_map(
         local,
         mesh=mesh,

time: 99.1 us -> 36.5 us (0.37)
  waiting for transfers between devices: 36.1 us -> 5.62 us
  blocking collectives: 26.4 us -> 0 us
  Pallas kernels: 0 us -> 16 us
  between operations: 14.3 us -> 0.72 us
  starting transfers between devices: 0.04 us -> 13.2 us
  local copies, waits for them, and re-layouts: 10.5 us -> 0.78 us
  matrix products: 6.48 us -> 0 us
  other arithmetic: 4.96 us -> 0.01 us
    reduce_scatter x1 -> x0, waiting for transfers between devices: 36.1 us -> none  [local(): lax.psum_scatter(grad_terms(columns, slopes), 'doc', scatter_dimension=0,...]
    psum x2 -> x0, blocking collectives: 26.4 us -> none  [the longest x1 13.5 us: local(): prediction = lax.psum(partial_pred, 'filt') + offsets]
    pallas_call x0 -> x7, Pallas kernels: none -> 16 us  [run(): return built(*operands)]
    ppermute x0 -> x9, starting transfers between devices: none -> 13.2 us  [swap(): return lax.ppermute(x, axis, [(i, i ^ k) for i in range(size)])]
    dot_general x12 -> x0, matrix products: 6.48 us -> none  [the longest x3 3.25 us: grad_terms(): jnp.einsum('ptje,ptf->ejf', window, slopes[index], preferred_element_type...]
    ppermute x0 -> x9, waiting for transfers between devices: none -> 5.62 us  [swap(): return lax.ppermute(x, axis, [(i, i ^ k) for i in range(size)])]
    concatenate x1 -> x0, local copies, waits for them, and re-layouts: 5.49 us -> none  [grad_terms(): return jnp.concatenate(outputs, axis=1)]
    unnamed x36 -> x8, local copies, waits for them, and re-layouts: 4.72 us -> 0.78 us
  transfers between devices with their start and end apart: 1 -> 9, of which waited for: 1 -> 4; matrix products, arithmetic and copies ran while one was open for 1% -> 0% of each run, Pallas kernels for 0% -> 31%
where the time goes in v3:
time: 36.5 us; the launch traced here: 36.3 us
  Pallas kernels  16 us (44%)
  starting transfers between devices  13.2 us (36%)
  waiting for transfers between devices  5.62 us (15%)
  local copies, waits for them, and re-layouts  0.78 us (2%)
  between operations  0.72 us (2%)
    pallas_call x7, Pallas kernels, run(): return built(*operands)  16 us
    ppermute x9, starting transfers between devices, swap(): return lax.ppermute(x, axis, [(i, i ^ k) for i in range(size)])  13.2 us
    ppermute x9, waiting for transfers between devices, swap(): return lax.ppermute(x, axis, [(i, i ^ k) for i in range(size)])  5.62 us
    unnamed x8, local copies, waits for them, and re-layouts  0.78 us
  transfers between devices with their start and end apart: 9, of which 4 were waited for; matrix products, arithmetic and copies ran while one was open for 0% of the time, Pallas kernels for 31%

profile of v3, /device:TPU:0, one launch (start us, length us, event | category | flops | bytes accessed | tf_op | source)
XLA Modules:
  0.0 36.3 jit_solution(13049235524897595510)
XLA Ops:
  0.6 1.0 %shard_map.154.refs_9_.pieces = f32[2,256,256]{2,1,0:T(8,128)S(1)} custom-call(s32[2]{0:T(128)} %len_any.1, bf16[2,256,256]{2,1,0:T(8,128)(2,1)} %x_any.1), custom_call_target="tpu_custom_call" | custom-call | flops 1 | bytes 1 | tf_op jit(solution)/shard_map/pallas_call | solution.py:452
  1.7 3.0 %collective-permute-start.1 = (f32[2,256,256]{2,1,0:T(8,128)S(1)}, f32[2,256,256]{2,1,0:T(8,128)S(1)}, u32[]{:S(2)}, u32[]{:S(2)}) collective-permute-start(f32[2,256,256]{2,1,0:T(8,128)S(1)} %shard_map.154.refs_9_.pieces), channel_id=1, source_target_pairs={{0,16},{4,20},{8,24},{12,28},{16,0},{20,4},{24,8},{28,12},{1,17},{... | collective-permute-start | bytes 1572872 | tf_op jit(solution)/shard_map/ppermute | solution.py:444
  4.7 1.5 %collective-permute-start.2 = (f32[2,256,256]{2,1,0:T(8,128)S(1)}, f32[2,256,256]{2,1,0:T(8,128)}, u32[]{:S(2)}, u32[]{:S(2)}) collective-permute-start(f32[2,256,256]{2,1,0:T(8,128)S(1)} %shard_map.154.refs_9_.pieces), channel_id=1, source_target_pairs={{0,8},{4,12},{8,0},{12,4},{16,24},{20,28},{24,16},{28,20},{1,9},{5... | collective-permute-start | bytes 1572872 | tf_op jit(solution)/shard_map/ppermute | solution.py:444
  6.2 0.0 collective-permute-start.7
  6.2 3.7 %shard_map.155 = (f32[8,128]{1,0:T(8,128)S(1)}, f32[2,3,256]{2,1,0:T(4,128)S(1)}, f32[2,3,256,256]{3,2,1,0:T(8,128)S(1)}, f32[16,128]{1,0:T(8,128)S(1)}) custom-call(s32[2]{0:T(128)} %refs_0_.1, s32[2]{0:T(128)} %refs_1_.1, s32[2]{0:T(128)} %refs_2_.1, f32[2]{0:T(128)} %refs_3_.2, f32[840]{0:T(1024)} %refs_4_.1, f32[40]{0:T(128)} %refs_5_.1, f32[8]{0:T(128)} %refs_6_.1, ...), custom_call_target="tpu_custom_call" | custom-call | flops 1 | bytes 1 | tf_op jit(solution)/shard_map/pallas_call | solution.py:452
  9.9 2.1 %collective-permute-start = (f32[8,128]{1,0:T(8,128)S(1)}, f32[8,128]{1,0:T(8,128)S(1)}, u32[]{:S(2)}, u32[]{:S(2)}) collective-permute-start(f32[8,128]{1,0:T(8,128)S(1)} %get-tuple-element.32), channel_id=1, source_target_pairs={{0,1},{1,0},{2,3},{3,2},{4,5},{5,4},{6,7},{7,6},{8,9},{9,8},{10,11... | collective-permute-start | bytes 12296 | tf_op jit(solution)/shard_map/ppermute | solution.py:444
  12.0 0.9 %shard_map.156 = (f32[2,480,256]{2,1,0:T(8,128)S(1)}, f32[2,480,256]{2,1,0:T(8,128)S(1)}) custom-call(s32[1]{0:T(128)} %bitcast.d_ref, f32[2,256,256]{2,1,0:T(8,128)S(1)} %shard_map.154.refs_9_.pieces, f32[2,3,256,256]{3,2,1,0:T(8,128)S(1)} %get-tuple-element.33.share_ref), custom_call_target="tpu_custom_call" | custom-call | flops 1 | bytes 1 | tf_op jit(solution)/shard_map/pallas_call | solution.py:452
  12.9 0.7 %collective-permute-done = f32[8,128]{1,0:T(8,128)S(1)} collective-permute-done((f32[8,128]{1,0:T(8,128)S(1)}, f32[8,128]{1,0:T(8,128)S(1)}, u32[]{:S(2)}, u32[]{:S(2)}) %collective-permute-start) | collective-permute-done | bytes 4128 | tf_op jit(solution)/shard_map/ppermute | solution.py:444
  13.6 3.0 %collective-permute-start.3 = (f32[8,128]{1,0:T(8,128)S(1)}, f32[8,128]{1,0:T(8,128)S(1)}, u32[]{:S(2)}, u32[]{:S(2)}) collective-permute-start(f32[8,128]{1,0:T(8,128)S(1)} %add.3.one), channel_id=1, source_target_pairs={{0,2},{1,3},{2,0},{3,1},{4,6},{5,7},{6,4},{7,5},{8,10},{9,11},{10,... | collective-permute-start | bytes 12296 | tf_op jit(solution)/shard_map/ppermute | solution.py:444
  16.6 1.6 %collective-permute-done.3.two = f32[8,128]{1,0:T(8,128)S(1)} collective-permute-done((f32[8,128]{1,0:T(8,128)S(1)}, f32[8,128]{1,0:T(8,128)S(1)}, u32[]{:S(2)}, u32[]{:S(2)}) %collective-permute-start.3) | collective-permute-done | bytes 4128 | tf_op jit(solution)/shard_map/ppermute | solution.py:444
  18.2 0.0 collective-permute-done.1.refs_0_
  18.2 1.4 %collective-permute-done.2.refs_1_ = f32[2,256,256]{2,1,0:T(8,128)} collective-permute-done((f32[2,256,256]{2,1,0:T(8,128)S(1)}, f32[2,256,256]{2,1,0:T(8,128)}, u32[]{:S(2)}, u32[]{:S(2)}) %collective-permute-start.2) | collective-permute-done | bytes 524320 | tf_op jit(solution)/shard_map/ppermute | solution.py:444
  19.6 0.6 %shard_map.157 = (f32[16,128]{1,0:T(8,128)S(1)}, f32[2]{0:T(128)}) custom-call(f32[8,128]{1,0:T(8,128)S(1)} %add.3.one, f32[8,128]{1,0:T(8,128)S(1)} %collective-permute-done.3.two, f32[16,128]{1,0:T(8,128)S(1)} %get-tuple-element.40.base, f32[2,480,256]{2,1,0:T(8,128)S(1)} %get-tuple-element.36.keep_own.terms_own, ...), custom_call_target="tpu_custom_call" | custom-call | flops 1 | bytes 1 | tf_op jit(solution)/shard_map/pallas_call | solution.py:452
  20.2 0.5 %collective-permute-start.4 = (f32[16,128]{1,0:T(8,128)S(1)}, f32[16,128]{1,0:T(8,128)S(1)}, u32[]{:S(2)}, u32[]{:S(2)}) collective-permute-start(f32[16,128]{1,0:T(8,128)S(1)} %get-tuple-element.41.facts.refs_2_), channel_id=1, source_target_pairs={{0,16},{4,20},{8,24},{12,28},{16,0},{20,4},{24,8},{28,12},{1,17},{... | collective-permute-start | bytes 24584 | tf_op jit(solution)/shard_map/ppermute | solution.py:444
  20.8 1.5 %collective-permute-start.5 = (f32[16,128]{1,0:T(8,128)S(1)}, f32[16,128]{1,0:T(8,128)S(1)}, u32[]{:S(2)}, u32[]{:S(2)}) collective-permute-start(f32[16,128]{1,0:T(8,128)S(1)} %get-tuple-element.41.facts.refs_2_), channel_id=1, source_target_pairs={{0,8},{4,12},{8,0},{12,4},{16,24},{20,28},{24,16},{28,20},{1,9},{5... | collective-permute-start | bytes 24584 | tf_op jit(solution)/shard_map/ppermute | solution.py:444
  22.3 1.5 %collective-permute-start.6 = (f32[16,128]{1,0:T(8,128)S(1)}, f32[16,128]{1,0:T(8,128)S(1)}, u32[]{:S(2)}, u32[]{:S(2)}) collective-permute-start(f32[16,128]{1,0:T(8,128)S(1)} %get-tuple-element.41.facts.refs_2_), channel_id=1, source_target_pairs={{0,24},{4,28},{8,16},{12,20},{16,8},{20,12},{24,0},{28,4},{1,25},{... | collective-permute-start | bytes 24584 | tf_op jit(solution)/shard_map/ppermute | solution.py:444
  23.7 5.9 %shard_map.158 = (f32[480,256]{1,0:T(8,128)S(1)}, f32[480,256]{1,0:T(8,128)S(1)}, f32[4,8,256]{2,1,0:T(8,128)S(1)}, f32[4,480,256]{2,1,0:T(8,128)S(1)}, f32[4,480,256]{2,1,0:T(8,128)S(1)}) custom-call(s32[1]{0:T(128)} %bitcast.d_ref, f32[2,480,256]{2,1,0:T(8,128)S(1)} %get-tuple-element.36.keep_own.terms_own, ...), custom_call_target="tpu_custom_call" | custom-call | flops 1 | bytes 1 | tf_op jit(solution)/shard_map/pallas_call | solution.py:452
  29.7 0.0 collective-permute-done.4.refs_0_
  29.7 0.0 collective-permute-done.5.refs_1_
  29.7 0.8 %copy-done.2 = f32[2,256,256]{2,1,0:T(8,128)} copy-done((f32[2,256,256]{2,1,0:T(8,128)}, f32[2,256,256]{2,1,0:T(8,128)S(1)}, u32[]{:S(2)}) %copy-start.2) | copy-done | bytes 524312
  30.5 3.0 %shard_map.159 = (f32[480,256]{1,0:T(8,128)S(1)}, f32[496,256]{1,0:T(8,128)S(1)}) custom-call(s32[1]{0:T(128)} %bitcast.d_ref, f32[480,256]{1,0:T(8,128)S(1)} %get-tuple-element.44.in_own, f32[480,256]{1,0:T(8,128)S(1)} %get-tuple-element.45.in_other, f32[4,480,256]{2,1,0:T(8,128)S(1)} %get-tuple-element.46.near_own, ...), custom_call_target="tpu_custom_call" | custom-call | flops 1 | bytes 1 | tf_op jit(solution)/shard_map/pallas_call | solution.py:452
  33.5 0.1 collective-permute-start.8
  33.6 1.9 %collective-permute-done.8.came_ref = f32[496,256]{1,0:T(8,128)S(1)} collective-permute-done((f32[496,256]{1,0:T(8,128)S(1)}, f32[496,256]{1,0:T(8,128)S(1)}, u32[]{:S(2)}, u32[]{:S(2)}) %collective-permute-start.8) | collective-permute-done | bytes 507936 | tf_op jit(solution)/shard_map/ppermute | solution.py:444
  35.5 0.8 %shard_map.160 = (f32[480,256]{1,0:T(8,128)}, f32[3,256]{1,0:T(4,128)}, f32[840]{0:T(1024)}, f32[40]{0:T(128)}, f32[8]{0:T(128)}) custom-call(f32[480,256]{1,0:T(8,128)S(1)} %get-tuple-element.50.own_ref, f32[496,256]{1,0:T(8,128)S(1)} %get-tuple-element.51.mine_ref, f32[496,256]{1,0:T(8,128)S(1)} %collective-permute-done.8.came_ref), custom_call_target="tpu_custom_call" | custom-call | flops 1 | bytes 1 | tf_op jit(solution)/shard_map/pallas_call | solution.py:452
  (10 shorter events, 0.0 us)
Async XLA Ops:
  1.7 16.6 %collective-permute-start.1 = (f32[2,256,256]{2,1,0:T(8,128)S(1)}, f32[2,256,256]{2,1,0:T(8,128)S(1)}, u32[]{:S(2)}, u32[]{:S(2)}) collective-permute-start(f32[2,256,256]{2,1,0:T(8,128)S(1)} %shard_map.154.refs_9_.pieces), channel_id=1, source_target_pairs={{0,16},{4,20},{8,24},{12,28},{16,0},{20,4},{24,8},{28,12},{1,17},{... | collective-permute-start | bytes 1572872 | tf_op jit(solution)/shard_map/ppermute | solution.py:444
  4.7 15.0 %collective-permute-start.2 = (f32[2,256,256]{2,1,0:T(8,128)S(1)}, f32[2,256,256]{2,1,0:T(8,128)}, u32[]{:S(2)}, u32[]{:S(2)}) collective-permute-start(f32[2,256,256]{2,1,0:T(8,128)S(1)} %shard_map.154.refs_9_.pieces), channel_id=1, source_target_pairs={{0,8},{4,12},{8,0},{12,4},{16,24},{20,28},{24,16},{28,20},{1,9},{5... | collective-permute-start | bytes 1572872 | tf_op jit(solution)/shard_map/ppermute | solution.py:444
  6.2 23.5 %collective-permute-start.7 = (f32[2,256,256]{2,1,0:T(8,128)S(1)}, f32[2,256,256]{2,1,0:T(8,128)S(1)}, u32[]{:S(2)}, u32[]{:S(2)}) collective-permute-start(f32[2,256,256]{2,1,0:T(8,128)S(1)} %shard_map.154.refs_9_.pieces), channel_id=1, source_target_pairs={{0,24},{4,28},{8,16},{12,20},{16,8},{20,12},{24,0},{28,4},{1,25},{... | collective-permute-start | bytes 1572872 | tf_op jit(solution)/shard_map/ppermute | solution.py:444
  9.9 3.7 %collective-permute-start = (f32[8,128]{1,0:T(8,128)S(1)}, f32[8,128]{1,0:T(8,128)S(1)}, u32[]{:S(2)}, u32[]{:S(2)}) collective-permute-start(f32[8,128]{1,0:T(8,128)S(1)} %get-tuple-element.32), channel_id=1, source_target_pairs={{0,1},{1,0},{2,3},{3,2},{4,5},{5,4},{6,7},{7,6},{8,9},{9,8},{10,11... | collective-permute-start | bytes 12296 | tf_op jit(solution)/shard_map/ppermute | solution.py:444
  12.0 11.7 %copy-start = (bf16[256,15,256]{2,0,1:T(8,128)(2,1)S(1)}, bf16[256,15,256]{2,0,1:T(8,128)(2,1)}, u32[]{:S(2)}) copy-start(bf16[256,15,256]{2,0,1:T(8,128)(2,1)} %param.13) | copy-start | bytes 5898244
  12.0 11.7 %copy-start.1 = (bf16[3,256]{1,0:T(4,128)(2,1)S(1)}, bf16[3,256]{1,0:T(4,128)(2,1)}, u32[]{:S(2)}) copy-start(bf16[3,256]{1,0:T(4,128)(2,1)} %refs_8_.1) | copy-start | bytes 4612
  13.6 4.6 %collective-permute-start.3 = (f32[8,128]{1,0:T(8,128)S(1)}, f32[8,128]{1,0:T(8,128)S(1)}, u32[]{:S(2)}, u32[]{:S(2)}) collective-permute-start(f32[8,128]{1,0:T(8,128)S(1)} %add.3.one), channel_id=1, source_target_pairs={{0,2},{1,3},{2,0},{3,1},{4,6},{5,7},{6,4},{7,5},{8,10},{9,11},{10,... | collective-permute-start | bytes 12296 | tf_op jit(solution)/shard_map/ppermute | solution.py:444
  18.2 5.5 %copy-start.3 = (f32[2,256,256]{2,1,0:T(8,128)}, f32[2,256,256]{2,1,0:T(8,128)S(1)}, u32[]{:S(2)}) copy-start(f32[2,256,256]{2,1,0:T(8,128)S(1)} %collective-permute-done.1.refs_0_) | copy-start | bytes 1572868
  20.2 9.5 %collective-permute-start.4 = (f32[16,128]{1,0:T(8,128)S(1)}, f32[16,128]{1,0:T(8,128)S(1)}, u32[]{:S(2)}, u32[]{:S(2)}) collective-permute-start(f32[16,128]{1,0:T(8,128)S(1)} %get-tuple-element.41.facts.refs_2_), channel_id=1, source_target_pairs={{0,16},{4,20},{8,24},{12,28},{16,0},{20,4},{24,8},{28,12},{1,17},{... | collective-permute-start | bytes 24584 | tf_op jit(solution)/shard_map/ppermute | solution.py:444
  20.8 8.9 %collective-permute-start.5 = (f32[16,128]{1,0:T(8,128)S(1)}, f32[16,128]{1,0:T(8,128)S(1)}, u32[]{:S(2)}, u32[]{:S(2)}) collective-permute-start(f32[16,128]{1,0:T(8,128)S(1)} %get-tuple-element.41.facts.refs_2_), channel_id=1, source_target_pairs={{0,8},{4,12},{8,0},{12,4},{16,24},{20,28},{24,16},{28,20},{1,9},{5... | collective-permute-start | bytes 24584 | tf_op jit(solution)/shard_map/ppermute | solution.py:444
  22.3 7.5 %collective-permute-start.6 = (f32[16,128]{1,0:T(8,128)S(1)}, f32[16,128]{1,0:T(8,128)S(1)}, u32[]{:S(2)}, u32[]{:S(2)}) collective-permute-start(f32[16,128]{1,0:T(8,128)S(1)} %get-tuple-element.41.facts.refs_2_), channel_id=1, source_target_pairs={{0,24},{4,28},{8,16},{12,20},{16,8},{20,12},{24,0},{28,4},{1,25},{... | collective-permute-start | bytes 24584 | tf_op jit(solution)/shard_map/ppermute | solution.py:444
  29.7 0.8 %copy-start.2 = (f32[2,256,256]{2,1,0:T(8,128)}, f32[2,256,256]{2,1,0:T(8,128)S(1)}, u32[]{:S(2)}) copy-start(f32[2,256,256]{2,1,0:T(8,128)S(1)} %collective-permute-done.7.refs_6_) | copy-start | bytes 1572868
  33.5 2.0 %collective-permute-start.8 = (f32[496,256]{1,0:T(8,128)S(1)}, f32[496,256]{1,0:T(8,128)S(1)}, u32[]{:S(2)}, u32[]{:S(2)}) collective-permute-start(f32[496,256]{1,0:T(8,128)S(1)} %get-tuple-element.51.mine_ref), channel_id=1, source_target_pairs={{0,4},{4,0},{8,12},{12,8},{16,20},{20,16},{24,28},{28,24},{1,5},{5... | collective-permute-start | bytes 1523720 | tf_op jit(solution)/shard_map/ppermute | solution.py:444

commit v4 on v3

--- a/solution.py
+++ b/solution.py
@@ -195,7 +195,7 @@
                 acc_other[place, :] += other
 
 
-def mask_kernel(len_any, x_any, pieces, x_ref, len_ref, sems):
+def mask_kernel(d_ref, len_any, x_any, pieces, x_ref, len_ref, sems):
     posts, rows, width = x_ref.shape
     copies = [pltpu.make_async_copy(len_any, len_ref, sems.at[posts])]
     copies += [pltpu.make_async_copy(x_any.at[p], x_ref.at[p], sems.at[p]) for p in range(posts)]
@@ -264,7 +264,8 @@
         add_terms(at, slopes, own_ref.at[p], other_ref.at[p], slice_e, fresh=True)
 
 
-def facts_kernel(one, two, base, keep_own, keep_other, facts_ref, pred_ref):
+def facts_kernel(n_keep, one, two, base, *refs):
+    facts_ref, pred_ref = refs[n_keep:]
     posts = pred_ref.shape[0]
     facts_ref[...] = base[...]
     for p in range(posts):
@@ -273,72 +274,54 @@
         facts_ref[p : p + 1, :] = value - base[4 * posts + p : 4 * posts + p + 1, :]
 
 
-def first_kernel(n_near, slice_e, d_ref, terms_own, terms_other, facts, *refs):
-    near = refs[:n_near]
-    w_ref, head_ref, acc_own, acc_other, feat_near, near_own, near_other = refs[n_near : n_near + 7]
-    xs, sems, xpads, counts, cols = refs[n_near + 7 :]
-    posts = terms_own.shape[0]
-    copies = []
-    for k in range(n_near):
-        for p in range(posts):
-            i = k * posts + p
-            copies.append(pltpu.make_async_copy(near[k].at[p], xs.at[i], sems.at[i]))
-            copies[-1].start()
+def near_kernel(n_keep, slice_e, d_ref, x_ref, w_ref, head_ref, *refs):
+    feat_ref, own_ref, other_ref, xpads, counts, cols = refs[n_keep:]
+    posts = x_ref.shape[0]
     head = head_ref[...].astype(jnp.float32)
-    for acc, terms in ((acc_own, terms_own), (acc_other, terms_other)):
-        acc[...] = sum(facts[p : p + 1, 0:1] * terms[p] for p in range(posts))
-    for i, copy in enumerate(copies):
-        copy.wait()
-        load_post(xs[i], xpads.at[i], counts.at[i])
-
-    def near_posts(k, carry):
-        for p in range(posts):
-            make_cols(xpads.at[k * posts + p], cols.at[p])
-        for p in range(posts):
-            i = k * posts + p
-            slopes = []
-            for index in range(3):
-                feature, share = forward(index, cols.at[p], w_ref, head, counts.at[i])
-                feat_near[i, index : index + 1, :] = feature
-                slopes.append(share.astype(jnp.bfloat16))
-            at = pick_rows(d_ref, middle_of(cols.at[p]), slice_e)
-            add_terms(at, slopes, near_own.at[i], near_other.at[i], slice_e, fresh=True)
-        return carry
-
-    lax.fori_loop(0, n_near, near_posts, 0)
-
-
-def last_kernel(n_near, sizes, slice_e, d_ref, in_own, in_other, near_own, near_other, *refs):
-    near_facts = refs[:n_near]
-    facts, far_facts, feat_own, feat_near, far = refs[n_near : n_near + 5]
-    w_ref, head_ref, acc_own, acc_other = refs[n_near + 5 : n_near + 9]
-    xs, sems, xpads, counts, cols = refs[n_near + 9 :]
-    posts = feat_own.shape[0]
-    copies = []
-    for p in range(posts):
-        copies.append(pltpu.make_async_copy(far.at[p], xs.at[p], sems.at[p]))
-        copies[-1].start()
-    n_rows, filters = in_own.shape
+    for p in range(posts):
+        load_post(x_ref[p], xpads.at[p], counts.at[p])
+        make_cols(xpads.at[p], cols.at[p])
+    for p in range(posts):
+        slopes = []
+        for index in range(3):
+            feature, share = forward(index, cols.at[p], w_ref, head, counts.at[p])
+            feat_ref[p, index : index + 1, :] = feature
+            slopes.append(share.astype(jnp.bfloat16))
+        at = pick_rows(d_ref, middle_of(cols.at[p]), slice_e)
+        add_terms(at, slopes, own_ref.at[p], other_ref.at[p], slice_e, fresh=True)
+
+
+def scaled_sum(start, facts, terms):
+    total = start
+    for fact, term in zip(facts, terms):
+        for p in range(term.shape[0]):
+            total = total + fact[p : p + 1, 0:1] * term[p]
+    return total
+
+
+def last_kernel(n_near, sizes, slice_e, d_ref, far, *refs):
+    facts = refs[: 2 + n_near]
+    feats = refs[2 + n_near : 3 + 2 * n_near]
+    terms = refs[3 + 2 * n_near : 4 + 3 * n_near]
+    w_ref, head_ref, acc_own, acc_other, xpads, counts, cols = refs[4 + 3 * n_near :]
+    posts = far.shape[0]
+    n_rows, filters = acc_own.shape
     head = head_ref[...].astype(jnp.float32)
-    for acc, start, terms in ((acc_own, in_own, near_own), (acc_other, in_other, near_other)):
-        total = start[...]
-        for k in range(n_near):
-            for p in range(posts):
-                total = total + near_facts[k][p : p + 1, 0:1] * terms[k * posts + p]
-        acc[0:n_rows, :] = total
-
-    for p in range(posts):
-        copies[p].wait()
-        load_post(xs[p], xpads.at[p], counts.at[p])
+    for p in range(posts):
+        load_post(far[p], xpads.at[p], counts.at[p])
         make_cols(xpads.at[p], cols.at[p])
+    acc_own[...] = jnp.zeros_like(acc_own)
+    acc_other[0:n_rows, :] = scaled_sum(jnp.zeros_like(acc_own), facts, terms)
     slopes = [[], [], []]
     feat_far = [[], []]
     for p in range(posts):
         for index in range(3):
             feature, share = forward(index, cols.at[p], w_ref, head, counts.at[p])
             feat_far[p].append(feature)
-            slopes[index].append((far_facts[p : p + 1, 0:1] * share).astype(jnp.bfloat16))
-    at = jnp.concatenate([pick_rows(d_ref, middle_of(cols.at[p]), slice_e) for p in range(posts)], axis=1)
+            slopes[index].append((facts[-1][p : p + 1, 0:1] * share).astype(jnp.bfloat16))
+    at = jnp.concatenate(
+        [pick_rows(d_ref, middle_of(cols.at[p]), slice_e) for p in range(posts)], axis=1
+    )
     slopes = [jnp.concatenate(parts, axis=0) for parts in slopes]
     add_terms(at, slopes, acc_own, acc_other, slice_e)
 
@@ -358,19 +341,16 @@
                 code_term = code_term + jnp.where(place == code, residual, 0.0)
         return head_term, code_term
 
-    terms = [
-        chip_terms(facts[...], [feat_own[p] for p in range(posts)]),
-        *[
-            chip_terms(
-                near_facts[k][...], [feat_near[k * posts + p, 0:3, :] for p in range(posts)]
-            )
-            for k in range(n_near)
-        ],
-        chip_terms(far_facts[...], [jnp.concatenate(parts, axis=0) for parts in feat_far]),
-    ]
+    features = [[feat[p, 0:3, :] for p in range(posts)] for feat in feats]
+    features.append([jnp.concatenate(parts, axis=0) for parts in feat_far])
+    sums = [chip_terms(fact[...], feature) for fact, feature in zip(facts, features)]
     acc_other[n_rows:, :] = jnp.zeros((acc_other.shape[0] - n_rows, filters), jnp.float32)
-    acc_other[n_rows : n_rows + 3, :] = tree_sum([term[0] for term in terms])
-    acc_other[n_rows + 3 : n_rows + 3 + n_codes, :] = tree_sum([term[1] for term in terms])
+    acc_other[n_rows : n_rows + 3, :] = tree_sum([total[0] for total in sums])
+    acc_other[n_rows + 3 : n_rows + 3 + n_codes, :] = tree_sum([total[1] for total in sums])
+
+
+def gather_kernel(n, acc, *refs):
+    refs[-1][...] = scaled_sum(acc[...], refs[:n], refs[n : 2 * n])
 
 
 def tree_sum(values):
@@ -429,9 +409,6 @@
     anywhere = pl.BlockSpec(memory_space=pl.ANY)
     hbm = pl.BlockSpec(memory_space=pltpu.HBM)
 
-    def arrived_scratch(n):
-        return [pltpu.VMEM((n, seq_len, dims), f32), pltpu.SemaphoreType.DMA((n,))]
-
     def posts_scratch(n):
         return [
             pltpu.VMEM((n, seq_len + 2 * PAD, dims), f32),
@@ -443,10 +420,15 @@
         size = n_doc if axis == "doc" else n_filt
         return lax.ppermute(x, axis, [(i, i ^ k) for i in range(size)])
 
-    def call(kernel, specs, out, scratch=()):
+    held = pl.BlockSpec(memory_space=pltpu.VMEM)
+    spaces = {id(hbm): pltpu.HBM, id(held): pltpu.VMEM}
+
+    def call(kernel, specs, out, scratch=(), stay=()):
         def run(*operands):
             operands = [
-                pltpu.with_memory_space_constraint(x, pltpu.HBM) if spec is hbm else x
+                pltpu.with_memory_space_constraint(x, spaces[id(spec)])
+                if id(spec) in spaces
+                else x
                 for x, spec in zip(operands, specs)
             ]
             return built(*operands)
@@ -455,7 +437,10 @@
             kernel,
             in_specs=specs,
             out_specs=[vmem] * len(out),
-            out_shape=[jax.ShapeDtypeStruct(shape, f32) for shape in out],
+            out_shape=[
+                pltpu.VMEM(shape, f32) if i in stay else jax.ShapeDtypeStruct(shape, f32)
+                for i, shape in enumerate(out)
+            ],
             scratch_shapes=list(scratch),
             compiler_params=pltpu.CompilerParams(vmem_limit_bytes=24 << 20),
             cost_estimate=pl.CostEstimate(flops=1, bytes_accessed=1, transcendentals=0),
@@ -465,14 +450,14 @@
     weights = jnp.transpose(conv_weight, (1, 0, 2)).reshape(TAPS * dims, filters)
     (pieces,) = call(
         mask_kernel,
-        [hbm] * 2,
+        [smem] + [hbm] * 2,
         [(posts, seq_len, dims)],
         [
             pltpu.VMEM((posts, seq_len, dims), jnp.bfloat16),
             pltpu.SMEM((posts,), i32),
             pltpu.SemaphoreType.DMA((posts + 1,)),
         ],
-    )(lengths, embedded)
+    )(me, lengths, embedded)
 
     near = [k for k in range(2, n_doc, 2) if bin(k).count("1") == 1][::-1]
     far = sum(near)
@@ -492,6 +477,7 @@
         + [pltpu.VMEM(weights.shape, weights.dtype)]
         + [posts_scratch(posts)[i] for i in (0, 2, 1)]
         + [pltpu.SemaphoreType.DMA((8,)), pltpu.SemaphoreType.DMA((TAPS,))],
+        stay=(2,),
     )(
         occupation,
         cohort,
@@ -507,58 +493,71 @@
     acc_shape = (TAPS * slice_e, filters)
     terms_own, terms_other = call(
         functools.partial(own_terms_kernel, slice_e),
-        [smem] + [vmem] * 2,
+        [smem, vmem, held],
         [(posts,) + acc_shape] * 2,
     )(me, pieces, share_own)
 
+    terms = [(terms_own, terms_other)]
     k = 1
     while 2 * k < n_filt:
         part = part + swap(part, k, "filt")
-        part, terms_own, terms_other = lax.optimization_barrier((part, terms_own, terms_other))
+        part, *terms[0] = lax.optimization_barrier((part, *terms[0]))
         k *= 2
     other = swap(part, k, "filt")
-    near_pieces, other = lax.optimization_barrier((near_pieces, other))
+
+    def near_terms(x, keep):
+        feat, *terms = call(
+            functools.partial(near_kernel, len(keep), slice_e),
+            [smem] + [vmem] * 3 + [anywhere] * len(keep),
+            [(posts, 8, filters)] + [(posts,) + acc_shape] * 2,
+            posts_scratch(posts),
+        )(me, x, weights, head_weight, *keep)
+        return feat, terms
+
+    feats = [feat_own]
+    feat, term = near_terms(near_pieces[0], ())
+    other, feat, *term = lax.optimization_barrier((other, feat, *term))
+    feats.append(feat)
+    terms.append(term)
+    keep = [x for pair in terms for x in pair]
     facts, prediction = call(
-        facts_kernel, [vmem] * 3 + [anywhere] * 2, [(n_facts, 128), (posts,)]
-    )(part, other, base, terms_own, terms_other)
-
-    near_facts = [swap(facts, k) for k in near]
-    far_facts = swap(facts, far)
-
-    near_shape = (n_near * posts,) + acc_shape
-    acc_own, acc_other, feat_near, near_own, near_other = call(
-        functools.partial(first_kernel, n_near, slice_e),
-        [smem] + [vmem] * 3 + [hbm] * n_near + [vmem] * 2,
-        [acc_shape, acc_shape, (n_near * posts, 8, filters), near_shape, near_shape],
-        arrived_scratch(n_near * posts) + posts_scratch(n_near * posts),
-    )(me, terms_own, terms_other, facts, *near_pieces, weights, head_weight)
+        functools.partial(facts_kernel, len(keep)),
+        [vmem] * 3 + [anywhere] * len(keep),
+        [(n_facts, 128), (posts,)],
+    )(part, other, base, *keep)
+
+    all_facts = [facts] + [swap(facts, k) for k in near] + [swap(facts, far)]
+    for x in near_pieces[1:]:
+        feat, term = near_terms(x, keep)
+        feats.append(feat)
+        terms.append(term)
     extra = -(-(3 + code_rows(sizes, filters)) // 8) * 8
     acc_own, acc_other = call(
         functools.partial(last_kernel, n_near, sizes, slice_e),
-        [smem] + [vmem] * (4 + n_near + 4) + [hbm] + [vmem] * 2,
+        [smem] + [vmem] * (4 + 3 * n_near + 3),
         [acc_shape, (acc_shape[0] + extra, filters)],
-        arrived_scratch(posts) + posts_scratch(posts),
+        posts_scratch(posts),
     )(
         me,
-        acc_own,
-        acc_other,
-        near_own,
-        near_other,
-        *near_facts,
-        facts,
-        far_facts,
-        feat_own,
-        feat_near,
         far_pieces,
+        *all_facts,
+        *feats,
+        *[pair[1] for pair in terms],
         weights,
         head_weight,
     )
 
+    came = swap(acc_other, 1)
+    (total,) = call(
+        functools.partial(gather_kernel, 1 + n_near),
+        [vmem] * (1 + 2 * (1 + n_near)),
+        [acc_shape],
+    )(acc_own, *all_facts[:-1], *[pair[0] for pair in terms])
     grad, head_grad, *codes = call(
         functools.partial(swap_kernel, sizes),
         [vmem] * 3,
         [acc_shape, (3, filters)] + [(size,) for size in sizes],
-    )(acc_own, acc_other, swap(acc_other, 1))
+    )(total, acc_other, came)
     conv_grad = jnp.transpose(grad.reshape(TAPS, slice_e, filters), (1, 0, 2))
     return (conv_grad, head_grad, *codes, prediction)
 

time: 36.5 us -> 34.7 us (0.951)
  Pallas kernels: 16 us -> 14.4 us
  local copies, waits for them, and re-layouts: 0.78 us -> 0.01 us
  waiting for transfers between devices: 5.62 us -> 6.22 us
    pallas_call x7 -> x9, Pallas kernels: 16 us -> 14.4 us  [run(): return built(*operands)]
    unnamed x8 -> x4, local copies, waits for them, and re-layouts: 0.78 us -> 0.01 us
    ppermute x9, waiting for transfers between devices: 5.62 us -> 6.22 us  [swap(): return lax.ppermute(x, axis, [(i, i ^ k) for i in range(size)])]
  transfers between devices with their start and end apart: 9 -> 9, of which waited for: 4 -> 5; matrix products, arithmetic and copies ran while one was open for 0% -> 0% of each run, Pallas kernels for 31% -> 30%
where the time goes in v4:
time: 34.7 us; the launch traced here: 34.6 us
  Pallas kernels  14.4 us (41%)
  starting transfers between devices  13.2 us (38%)
  waiting for transfers between devices  6.22 us (18%)
  between operations  0.7 us (2%)
    pallas_call x9, Pallas kernels, run(): return built(*operands)  14.4 us
    ppermute x9, starting transfers between devices, swap(): return lax.ppermute(x, axis, [(i, i ^ k) for i in range(size)])  13.2 us
    ppermute x9, waiting for transfers between devices, swap(): return lax.ppermute(x, axis, [(i, i ^ k) for i in range(size)])  6.22 us
  transfers between devices with their start and end apart: 9, of which 5 were waited for; matrix products, arithmetic and copies ran while one was open for 0% of the time, Pallas kernels for 30%

profile of v4, /device:TPU:0, one launch (start us, length us, event | category | flops | bytes accessed | tf_op | source)
XLA Modules:
  0.0 34.6 jit_solution(6795734495967360241)
XLA Ops:
  0.6 1.0 %shard_map.154.refs_9_.pieces = f32[2,256,256]{2,1,0:T(8,128)S(1)} custom-call(s32[1]{0:T(128)} %bitcast.d_ref, s32[2]{0:T(128)} %len_any.1, bf16[2,256,256]{2,1,0:T(8,128)(2,1)} %x_any.1), custom_call_target="tpu_custom_call" | custom-call | flops 1 | bytes 1 | tf_op jit(solution)/shard_map/pallas_call | solution.py:434
  1.7 3.0 %collective-permute-start.3 = (f32[2,256,256]{2,1,0:T(8,128)S(1)}, f32[2,256,256]{2,1,0:T(8,128)S(1)}, u32[]{:S(2)}, u32[]{:S(2)}) collective-permute-start(f32[2,256,256]{2,1,0:T(8,128)S(1)} %shard_map.154.refs_9_.pieces), channel_id=1, source_target_pairs={{0,16},{4,20},{8,24},{12,28},{16,0},{20,4},{24,8},{28,12},{1,17},{... | collective-permute-start | bytes 1572872 | tf_op jit(solution)/shard_map/ppermute | solution.py:421
  4.7 1.5 %collective-permute-start.7 = (f32[2,256,256]{2,1,0:T(8,128)S(1)}, f32[2,256,256]{2,1,0:T(8,128)S(1)}, u32[]{:S(2)}, u32[]{:S(2)}) collective-permute-start(f32[2,256,256]{2,1,0:T(8,128)S(1)} %shard_map.154.refs_9_.pieces), channel_id=1, source_target_pairs={{0,8},{4,12},{8,0},{12,4},{16,24},{20,28},{24,16},{28,20},{1,9},{5... | collective-permute-start | bytes 1572872 | tf_op jit(solution)/shard_map/ppermute | solution.py:421
  6.2 0.0 collective-permute-start
  6.2 3.8 %shard_map.155 = (f32[8,128]{1,0:T(8,128)S(1)}, f32[2,3,256]{2,1,0:T(4,128)S(1)}, f32[2,3,256,256]{3,2,1,0:T(8,128)S(1)}, f32[16,128]{1,0:T(8,128)S(1)}) custom-call(s32[2]{0:T(128)} %refs_0_.1, s32[2]{0:T(128)} %refs_1_.1, s32[2]{0:T(128)} %refs_2_.1, f32[2]{0:T(128)} %refs_3_.1, f32[840]{0:T(1024)} %refs_4_.1, f32[40]{0:T(128)} %refs_5_.1, f32[8]{0:T(128)} %refs_6_.1, ...), custom_call_target="tpu_custom_call" | custom-call | flops 1 | bytes 1 | tf_op jit(solution)/shard_map/pallas_call | solution.py:434
  10.1 2.1 %collective-permute-start.1 = (f32[8,128]{1,0:T(8,128)S(1)}, f32[8,128]{1,0:T(8,128)S(1)}, u32[]{:S(2)}, u32[]{:S(2)}) collective-permute-start(f32[8,128]{1,0:T(8,128)S(1)} %get-tuple-element.34), channel_id=1, source_target_pairs={{0,1},{1,0},{2,3},{3,2},{4,5},{5,4},{6,7},{7,6},{8,9},{9,8},{10,11... | collective-permute-start | bytes 12296 | tf_op jit(solution)/shard_map/ppermute | solution.py:421
  12.2 0.9 %shard_map.156 = (f32[2,480,256]{2,1,0:T(8,128)S(1)}, f32[2,480,256]{2,1,0:T(8,128)S(1)}) custom-call(s32[1]{0:T(128)} %bitcast.d_ref, f32[2,256,256]{2,1,0:T(8,128)S(1)} %shard_map.154.refs_9_.pieces, f32[2,3,256,256]{3,2,1,0:T(8,128)S(1)} %get-tuple-element.35.share_ref), custom_call_target="tpu_custom_call" | custom-call | flops 1 | bytes 1 | tf_op jit(solution)/shard_map/pallas_call | solution.py:434
  13.0 0.7 %collective-permute-done.1 = f32[8,128]{1,0:T(8,128)S(1)} collective-permute-done((f32[8,128]{1,0:T(8,128)S(1)}, f32[8,128]{1,0:T(8,128)S(1)}, u32[]{:S(2)}, u32[]{:S(2)}) %collective-permute-start.1) | collective-permute-done | bytes 4128 | tf_op jit(solution)/shard_map/ppermute | solution.py:421
  13.8 3.0 %collective-permute-start.2 = (f32[8,128]{1,0:T(8,128)S(1)}, f32[8,128]{1,0:T(8,128)S(1)}, u32[]{:S(2)}, u32[]{:S(2)}) collective-permute-start(f32[8,128]{1,0:T(8,128)S(1)} %add.3.one), channel_id=1, source_target_pairs={{0,2},{1,3},{2,0},{3,1},{4,6},{5,7},{6,4},{7,5},{8,10},{9,11},{10,... | collective-permute-start | bytes 12296 | tf_op jit(solution)/shard_map/ppermute | solution.py:421
  16.8 0.0 collective-permute-done.3.x_ref
  16.8 2.4 %shard_map.157 = (f32[2,8,256]{2,1,0:T(8,128)S(1)}, f32[2,480,256]{2,1,0:T(8,128)S(1)}, f32[2,480,256]{2,1,0:T(8,128)S(1)}) custom-call(s32[1]{0:T(128)} %bitcast.d_ref, f32[2,256,256]{2,1,0:T(8,128)S(1)} %collective-permute-done.3.x_ref, bf16[3840,256]{1,0:T(8,128)(2,1)S(1)} %bitcast.8, bf16[3,256]{1,0:T(4,128)(2,1)S(1)} %copy-done.1), custom_call_target="tpu_custom_call" | custom-call | flops 1 | bytes 1 | tf_op jit(solution)/shard_map/pallas_call | solution.py:434
  19.2 0.6 %shard_map.158 = (f32[16,128]{1,0:T(8,128)S(1)}, f32[2]{0:T(128)}) custom-call(f32[8,128]{1,0:T(8,128)S(1)} %add.3.one, f32[8,128]{1,0:T(8,128)S(1)} %collective-permute-done.2.two, f32[16,128]{1,0:T(8,128)S(1)} %get-tuple-element.43.base, f32[2,480,256]{2,1,0:T(8,128)S(1)} %get-tuple-element.44.refs_0_.refs_3_, ...), custom_call_target="tpu_custom_call" | custom-call | flops 1 | bytes 1 | tf_op jit(solution)/shard_map/pallas_call | solution.py:434
  19.8 2.8 %collective-permute-start.6 = (f32[16,128]{1,0:T(8,128)S(1)}, f32[16,128]{1,0:T(8,128)S(1)}, u32[]{:S(2)}, u32[]{:S(2)}) collective-permute-start(f32[16,128]{1,0:T(8,128)S(1)} %get-tuple-element.48.refs_0_), channel_id=1, source_target_pairs={{0,24},{4,28},{8,16},{12,20},{16,8},{20,12},{24,0},{28,4},{1,25},{... | collective-permute-start | bytes 24584 | tf_op jit(solution)/shard_map/ppermute | solution.py:421
  22.5 0.5 %collective-permute-start.5 = (f32[16,128]{1,0:T(8,128)S(1)}, f32[16,128]{1,0:T(8,128)S(1)}, u32[]{:S(2)}, u32[]{:S(2)}) collective-permute-start(f32[16,128]{1,0:T(8,128)S(1)} %get-tuple-element.48.refs_0_), channel_id=1, source_target_pairs={{0,8},{4,12},{8,0},{12,4},{16,24},{20,28},{24,16},{28,20},{1,9},{5... | collective-permute-start | bytes 24584 | tf_op jit(solution)/shard_map/ppermute | solution.py:421
  23.1 0.2 collective-permute-start.4
  23.3 2.4 %shard_map.159 = (f32[2,8,256]{2,1,0:T(8,128)S(1)}, f32[2,480,256]{2,1,0:T(8,128)S(1)}, f32[2,480,256]{2,1,0:T(8,128)S(1)}) custom-call(s32[1]{0:T(128)} %bitcast.d_ref, f32[2,256,256]{2,1,0:T(8,128)S(1)} %collective-permute-done.7.x_ref, bf16[3840,256]{1,0:T(8,128)(2,1)S(1)} %bitcast.9, bf16[3,256]{1,0:T(4,128)(2,1)S(1)} %copy-done.1, ...), custom_call_target="tpu_custom_call" | custom-call | flops 1 | bytes 1 | tf_op jit(solution)/shard_map/pallas_call | solution.py:434
  25.6 3.7 %collective-permute-done.far = f32[2,256,256]{2,1,0:T(8,128)S(1)} collective-permute-done((f32[2,256,256]{2,1,0:T(8,128)S(1)}, f32[2,256,256]{2,1,0:T(8,128)S(1)}, u32[]{:S(2)}, u32[]{:S(2)}) %collective-permute-start) | collective-permute-done | bytes 524320 | tf_op jit(solution)/shard_map/ppermute | solution.py:421
  29.4 0.1 collective-permute-done.6.refs_3_
  29.5 0.2 collective-permute-done.5.refs_2_
  29.7 2.1 %shard_map.160 = (f32[480,256]{1,0:T(8,128)S(1)}, f32[496,256]{1,0:T(8,128)S(1)}) custom-call(s32[1]{0:T(128)} %bitcast.d_ref, f32[2,256,256]{2,1,0:T(8,128)S(1)} %collective-permute-done.far, f32[16,128]{1,0:T(8,128)S(1)} %get-tuple-element.48.refs_0_, f32[16,128]{1,0:T(8,128)S(1)} %collective-permute-done.4.refs_1_, ...), custom_call_target="tpu_custom_call" | custom-call | flops 1 | bytes 1 | tf_op jit(solution)/shard_map/pallas_call | solution.py:434
  31.8 0.1 collective-permute-start.8
  31.9 0.5 %shard_map.161.own_ref = f32[480,256]{1,0:T(8,128)S(1)} custom-call(f32[480,256]{1,0:T(8,128)S(1)} %get-tuple-element.53.acc, f32[16,128]{1,0:T(8,128)S(1)} %get-tuple-element.48.refs_0_, f32[16,128]{1,0:T(8,128)S(1)} %collective-permute-done.4.refs_1_, f32[16,128]{1,0:T(8,128)S(1)} %collective-permute-done.5.refs_2_, ...), custom_call_target="tpu_custom_call" | custom-call | flops 1 | bytes 1 | tf_op jit(solution)/shard_map/pallas_call | solution.py:434
  32.3 1.4 %collective-permute-done.8.came_ref = f32[496,256]{1,0:T(8,128)S(1)} collective-permute-done((f32[496,256]{1,0:T(8,128)S(1)}, f32[496,256]{1,0:T(8,128)S(1)}, u32[]{:S(2)}, u32[]{:S(2)}) %collective-permute-start.8) | collective-permute-done | bytes 507936 | tf_op jit(solution)/shard_map/ppermute | solution.py:421
  33.7 0.8 %shard_map.162 = (f32[480,256]{1,0:T(8,128)}, f32[3,256]{1,0:T(4,128)}, f32[840]{0:T(1024)}, f32[40]{0:T(128)}, f32[8]{0:T(128)}) custom-call(f32[480,256]{1,0:T(8,128)S(1)} %shard_map.161.own_ref, f32[496,256]{1,0:T(8,128)S(1)} %get-tuple-element.55.mine_ref, f32[496,256]{1,0:T(8,128)S(1)} %collective-permute-done.8.came_ref), custom_call_target="tpu_custom_call" | custom-call | flops 1 | bytes 1 | tf_op jit(solution)/shard_map/pallas_call | solution.py:434
  (8 shorter events, 0.0 us)
Async XLA Ops:
  1.7 15.1 %collective-permute-start.3 = (f32[2,256,256]{2,1,0:T(8,128)S(1)}, f32[2,256,256]{2,1,0:T(8,128)S(1)}, u32[]{:S(2)}, u32[]{:S(2)}) collective-permute-start(f32[2,256,256]{2,1,0:T(8,128)S(1)} %shard_map.154.refs_9_.pieces), channel_id=1, source_target_pairs={{0,16},{4,20},{8,24},{12,28},{16,0},{20,4},{24,8},{28,12},{1,17},{... | collective-permute-start | bytes 1572872 | tf_op jit(solution)/shard_map/ppermute | solution.py:421
  4.7 18.6 %collective-permute-start.7 = (f32[2,256,256]{2,1,0:T(8,128)S(1)}, f32[2,256,256]{2,1,0:T(8,128)S(1)}, u32[]{:S(2)}, u32[]{:S(2)}) collective-permute-start(f32[2,256,256]{2,1,0:T(8,128)S(1)} %shard_map.154.refs_9_.pieces), channel_id=1, source_target_pairs={{0,8},{4,12},{8,0},{12,4},{16,24},{20,28},{24,16},{28,20},{1,9},{5... | collective-permute-start | bytes 1572872 | tf_op jit(solution)/shard_map/ppermute | solution.py:421
  6.2 23.2 %collective-permute-start = (f32[2,256,256]{2,1,0:T(8,128)S(1)}, f32[2,256,256]{2,1,0:T(8,128)S(1)}, u32[]{:S(2)}, u32[]{:S(2)}) collective-permute-start(f32[2,256,256]{2,1,0:T(8,128)S(1)} %shard_map.154.refs_9_.pieces), channel_id=1, source_target_pairs={{0,24},{4,28},{8,16},{12,20},{16,8},{20,12},{24,0},{28,4},{1,25},{... | collective-permute-start | bytes 1572872 | tf_op jit(solution)/shard_map/ppermute | solution.py:421
  6.2 10.6 %copy-start = (bf16[256,15,256]{2,0,1:T(8,128)(2,1)S(1)}, bf16[256,15,256]{2,0,1:T(8,128)(2,1)}, u32[]{:S(2)}) copy-start(bf16[256,15,256]{2,0,1:T(8,128)(2,1)} %param.13) | copy-start | bytes 5898244
  6.2 10.6 %copy-start.1 = (bf16[3,256]{1,0:T(4,128)(2,1)S(1)}, bf16[3,256]{1,0:T(4,128)(2,1)}, u32[]{:S(2)}) copy-start(bf16[3,256]{1,0:T(4,128)(2,1)} %refs_11_.1) | copy-start | bytes 4612
  10.1 3.7 %collective-permute-start.1 = (f32[8,128]{1,0:T(8,128)S(1)}, f32[8,128]{1,0:T(8,128)S(1)}, u32[]{:S(2)}, u32[]{:S(2)}) collective-permute-start(f32[8,128]{1,0:T(8,128)S(1)} %get-tuple-element.34), channel_id=1, source_target_pairs={{0,1},{1,0},{2,3},{3,2},{4,5},{5,4},{6,7},{7,6},{8,9},{9,8},{10,11... | collective-permute-start | bytes 12296 | tf_op jit(solution)/shard_map/ppermute | solution.py:421
  13.8 5.4 %collective-permute-start.2 = (f32[8,128]{1,0:T(8,128)S(1)}, f32[8,128]{1,0:T(8,128)S(1)}, u32[]{:S(2)}, u32[]{:S(2)}) collective-permute-start(f32[8,128]{1,0:T(8,128)S(1)} %add.3.one), channel_id=1, source_target_pairs={{0,2},{1,3},{2,0},{3,1},{4,6},{5,7},{6,4},{7,5},{8,10},{9,11},{10,... | collective-permute-start | bytes 12296 | tf_op jit(solution)/shard_map/ppermute | solution.py:421
  19.8 9.7 %collective-permute-start.6 = (f32[16,128]{1,0:T(8,128)S(1)}, f32[16,128]{1,0:T(8,128)S(1)}, u32[]{:S(2)}, u32[]{:S(2)}) collective-permute-start(f32[16,128]{1,0:T(8,128)S(1)} %get-tuple-element.48.refs_0_), channel_id=1, source_target_pairs={{0,24},{4,28},{8,16},{12,20},{16,8},{20,12},{24,0},{28,4},{1,25},{... | collective-permute-start | bytes 24584 | tf_op jit(solution)/shard_map/ppermute | solution.py:421
  22.5 7.2 %collective-permute-start.5 = (f32[16,128]{1,0:T(8,128)S(1)}, f32[16,128]{1,0:T(8,128)S(1)}, u32[]{:S(2)}, u32[]{:S(2)}) collective-permute-start(f32[16,128]{1,0:T(8,128)S(1)} %get-tuple-element.48.refs_0_), channel_id=1, source_target_pairs={{0,8},{4,12},{8,0},{12,4},{16,24},{20,28},{24,16},{28,20},{1,9},{5... | collective-permute-start | bytes 24584 | tf_op jit(solution)/shard_map/ppermute | solution.py:421
  23.1 6.6 %collective-permute-start.4 = (f32[16,128]{1,0:T(8,128)S(1)}, f32[16,128]{1,0:T(8,128)S(1)}, u32[]{:S(2)}, u32[]{:S(2)}) collective-permute-start(f32[16,128]{1,0:T(8,128)S(1)} %get-tuple-element.48.refs_0_), channel_id=1, source_target_pairs={{0,16},{4,20},{8,24},{12,28},{16,0},{20,4},{24,8},{28,12},{1,17},{... | collective-permute-start | bytes 24584 | tf_op jit(solution)/shard_map/ppermute | solution.py:421
  31.8 2.0 %collective-permute-start.8 = (f32[496,256]{1,0:T(8,128)S(1)}, f32[496,256]{1,0:T(8,128)S(1)}, u32[]{:S(2)}, u32[]{:S(2)}) collective-permute-start(f32[496,256]{1,0:T(8,128)S(1)} %get-tuple-element.55.mine_ref), channel_id=1, source_target_pairs={{0,4},{4,0},{8,12},{12,8},{16,20},{20,16},{24,28},{28,24},{1,5},{5... | collective-permute-start | bytes 1523720 | tf_op jit(solution)/shard_map/ppermute | solution.py:421

commit v5 on v4

--- a/solution.py
+++ b/solution.py
@@ -195,7 +195,7 @@
                 acc_other[place, :] += other
 
 
-def mask_kernel(d_ref, len_any, x_any, pieces, x_ref, len_ref, sems):
+def mask_kernel(d_ref, z_ref, len_any, x_any, pieces, far_piece, x_ref, len_ref, sems):
     posts, rows, width = x_ref.shape
     copies = [pltpu.make_async_copy(len_any, len_ref, sems.at[posts])]
     copies += [pltpu.make_async_copy(x_any.at[p], x_ref.at[p], sems.at[p]) for p in range(posts)]
@@ -206,13 +206,14 @@
     for p in range(posts):
         copies[1 + p].wait()
         pieces[p] = jnp.where(place < len_ref[p], x_ref[p].astype(jnp.float32), OUTSIDE)
+    far_piece[...] = pieces[z_ref[0]]
 
 
 def own_kernel(*refs):
     small = refs[:8]
-    w_any, pieces, part_ref, feat_ref, share_ref, base_ref = refs[8:14]
-    held = refs[14:22]
-    w_ref, xpad, cols, counts, small_sems, w_sems = refs[22:]
+    w_any, pieces, part_ref, feat_ref, share_ref, base_ref, w_ref = refs[8:15]
+    held = refs[15:23]
+    xpad, cols, counts, small_sems, w_sems = refs[23:]
     posts = pieces.shape[0]
     width = w_ref.shape[0] // TAPS
     loads = []
@@ -264,12 +265,13 @@
         add_terms(at, slopes, own_ref.at[p], other_ref.at[p], slice_e, fresh=True)
 
 
-def facts_kernel(n_keep, one, two, base, *refs):
-    facts_ref, pred_ref = refs[n_keep:]
+def facts_kernel(n_keep, base, *refs):
+    facts_ref, pred_ref = refs[-2:]
     posts = pred_ref.shape[0]
     facts_ref[...] = base[...]
-    for p in range(posts):
-        value = one[p : p + 1, :] + two[p : p + 1, :] + base[p : p + 1, :]
+    total = tree_sum([part[...] for part in refs[: len(refs) - 2 - n_keep]])
+    for p in range(posts):
+        value = total[p : p + 1, :] + base[p : p + 1, :]
         pred_ref[pl.ds(p, 1)] = value[0, 0:1]
         facts_ref[p : p + 1, :] = value - base[4 * posts + p : 4 * posts + p + 1, :]
 
@@ -291,36 +293,45 @@
         add_terms(at, slopes, own_ref.at[p], other_ref.at[p], slice_e, fresh=True)
 
 
-def scaled_sum(start, facts, terms):
-    total = start
-    for fact, term in zip(facts, terms):
+def scaled_sum(residuals, terms):
+    total, i = 0.0, 0
+    for term in terms:
         for p in range(term.shape[0]):
-            total = total + fact[p : p + 1, 0:1] * term[p]
+            total = total + residuals[i] * term[p]
+            i += 1
     return total
 
 
-def last_kernel(n_near, sizes, slice_e, d_ref, far, *refs):
-    facts = refs[: 2 + n_near]
-    feats = refs[2 + n_near : 3 + 2 * n_near]
-    terms = refs[3 + 2 * n_near : 4 + 3 * n_near]
-    w_ref, head_ref, acc_own, acc_other, xpads, counts, cols = refs[4 + 3 * n_near :]
-    posts = far.shape[0]
+def last_kernel(sizes, slice_e, d_ref, z_ref, *refs):
+    facts, last, far = refs[:4], refs[4], refs[5]
+    feats, terms = refs[6:9], refs[9:12]
+    w_ref, head_ref, acc_own, acc_other, xpads, counts, cols = refs[12:]
+    posts = last.shape[0]
     n_rows, filters = acc_own.shape
     head = head_ref[...].astype(jnp.float32)
-    for p in range(posts):
-        load_post(far[p], xpads.at[p], counts.at[p])
+    pieces = [last[p] for p in range(posts)] + [far[...]]
+    here = z_ref[0]
+    residuals = [facts[2][p : p + 1, 0:1] for p in range(posts)]
+    residuals.append(facts[3][pl.ds(1 - here, 1), 0:1])
+    for p, piece in enumerate(pieces):
+        load_post(piece, xpads.at[p], counts.at[p])
         make_cols(xpads.at[p], cols.at[p])
     acc_own[...] = jnp.zeros_like(acc_own)
-    acc_other[0:n_rows, :] = scaled_sum(jnp.zeros_like(acc_own), facts, terms)
+    made = [facts[0][p : p + 1, 0:1] for p in range(posts)]
+    made += [facts[1][p : p + 1, 0:1] for p in range(posts)]
+    made.append(facts[3][pl.ds(here, 1), 0:1])
+    acc_other[0:n_rows, :] = scaled_sum(made, terms)
     slopes = [[], [], []]
-    feat_far = [[], []]
-    for p in range(posts):
+    feat_last = []
+    for p, residual in enumerate(residuals):
+        features = []
         for index in range(3):
             feature, share = forward(index, cols.at[p], w_ref, head, counts.at[p])
-            feat_far[p].append(feature)
-            slopes[index].append((facts[-1][p : p + 1, 0:1] * share).astype(jnp.bfloat16))
+            features.append(feature)
+            slopes[index].append((residual * share).astype(jnp.bfloat16))
+        feat_last.append(jnp.concatenate(features, axis=0))
     at = jnp.concatenate(
-        [pick_rows(d_ref, middle_of(cols.at[p]), slice_e) for p in range(posts)], axis=1
+        [pick_rows(d_ref, middle_of(cols.at[p]), slice_e) for p in range(posts + 1)], axis=1
     )
     slopes = [jnp.concatenate(parts, axis=0) for parts in slopes]
     add_terms(at, slopes, acc_own, acc_other, slice_e)
@@ -341,16 +352,21 @@
                 code_term = code_term + jnp.where(place == code, residual, 0.0)
         return head_term, code_term
 
-    features = [[feat[p, 0:3, :] for p in range(posts)] for feat in feats]
-    features.append([jnp.concatenate(parts, axis=0) for parts in feat_far])
+    features = [[feat[p, 0:3, :] for p in range(posts)] for feat in feats[:2]]
+    features.append(feat_last[:posts])
+    one, two = feats[2][0, 0:3, :], feat_last[posts]
+    features.append([jnp.where(here == p, one, two) for p in range(posts)])
     sums = [chip_terms(fact[...], feature) for fact, feature in zip(facts, features)]
     acc_other[n_rows:, :] = jnp.zeros((acc_other.shape[0] - n_rows, filters), jnp.float32)
     acc_other[n_rows : n_rows + 3, :] = tree_sum([total[0] for total in sums])
     acc_other[n_rows + 3 : n_rows + 3 + n_codes, :] = tree_sum([total[1] for total in sums])
 
 
-def gather_kernel(n, acc, *refs):
-    refs[-1][...] = scaled_sum(acc[...], refs[:n], refs[n : 2 * n])
+def gather_kernel(z_ref, acc, own_facts, near_facts, far_facts, *refs):
+    posts = refs[0].shape[0]
+    made = [facts[p : p + 1, 0:1] for facts in (own_facts, near_facts) for p in range(posts)]
+    made.append(far_facts[pl.ds(z_ref[0], 1), 0:1])
+    refs[-1][...] = acc[...] + scaled_sum(made, refs[:-1])
 
 
 def tree_sum(values):
@@ -413,22 +429,18 @@
         return [
             pltpu.VMEM((n, seq_len + 2 * PAD, dims), f32),
             pltpu.VMEM((n, 8, filters), f32),
-            pltpu.VMEM((posts, seq_len, (2 * REACH + 1) * dims), jnp.bfloat16),
+            pltpu.VMEM((n, seq_len, (2 * REACH + 1) * dims), jnp.bfloat16),
         ]
 
     def swap(x, k, axis="doc"):
         size = n_doc if axis == "doc" else n_filt
         return lax.ppermute(x, axis, [(i, i ^ k) for i in range(size)])
 
-    held = pl.BlockSpec(memory_space=pltpu.VMEM)
-    spaces = {id(hbm): pltpu.HBM, id(held): pltpu.VMEM}
-
-    def call(kernel, specs, out, scratch=(), stay=()):
+
+    def call(kernel, specs, out, scratch=()):
         def run(*operands):
             operands = [
-                pltpu.with_memory_space_constraint(x, spaces[id(spec)])
-                if id(spec) in spaces
-                else x
+                pltpu.with_memory_space_constraint(x, pltpu.HBM) if spec is hbm else x
                 for x, spec in zip(operands, specs)
             ]
             return built(*operands)
@@ -438,8 +450,7 @@
             in_specs=specs,
             out_specs=[vmem] * len(out),
             out_shape=[
-                pltpu.VMEM(shape, f32) if i in stay else jax.ShapeDtypeStruct(shape, f32)
-                for i, shape in enumerate(out)
+                jax.ShapeDtypeStruct(x, f32) if isinstance(x, tuple) else x for x in out
             ],
             scratch_shapes=list(scratch),
             compiler_params=pltpu.CompilerParams(vmem_limit_bytes=24 << 20),
@@ -447,37 +458,42 @@
         )
         return run
 
+    acc_shape = (TAPS * slice_e, filters)
+    n_facts = -(-5 * posts // 8) * 8
     weights = jnp.transpose(conv_weight, (1, 0, 2)).reshape(TAPS * dims, filters)
-    (pieces,) = call(
+    half = (lax.axis_index("filt").astype(i32) & 1).reshape(1)
+    pieces, far_piece = call(
         mask_kernel,
-        [smem] + [hbm] * 2,
-        [(posts, seq_len, dims)],
+        [smem] * 2 + [hbm] * 2,
+        [(posts, seq_len, dims), (seq_len, dims)],
         [
             pltpu.VMEM((posts, seq_len, dims), jnp.bfloat16),
             pltpu.SMEM((posts,), i32),
             pltpu.SemaphoreType.DMA((posts + 1,)),
         ],
-    )(me, lengths, embedded)
+    )(me, half, lengths, embedded)
 
     near = [k for k in range(2, n_doc, 2) if bin(k).count("1") == 1][::-1]
     far = sum(near)
-    n_near = len(near)
+    far_one = swap(far_piece, far)
     near_pieces = [swap(pieces, k) for k in near]
-    far_pieces = swap(pieces, far)
-
-    n_facts = -(-5 * posts // 8) * 8
-    part, feat_own, share_own, base = call(
+
+    part, feat_own, share_own, base, weights = call(
         own_kernel,
         [hbm] * 9 + [vmem],
-        [(8, 128), (posts, 3, filters), (posts, 3, seq_len, filters), (n_facts, 128)],
+        [
+            (8, 128),
+            (posts, 3, filters),
+            (posts, 3, seq_len, filters),
+            (n_facts, 128),
+            jax.ShapeDtypeStruct(weights.shape, weights.dtype),
+        ],
         [pltpu.SMEM((posts,), i32)] * 3
         + [pltpu.SMEM((posts,), f32)]
         + [pltpu.SMEM((size,), f32) for size in sizes]
         + [pltpu.VMEM(head_weight.shape, head_weight.dtype)]
-        + [pltpu.VMEM(weights.shape, weights.dtype)]
         + [posts_scratch(posts)[i] for i in (0, 2, 1)]
         + [pltpu.SemaphoreType.DMA((8,)), pltpu.SemaphoreType.DMA((TAPS,))],
-        stay=(2,),
     )(
         occupation,
         cohort,
@@ -490,69 +506,61 @@
         weights,
         pieces,
     )
-    acc_shape = (TAPS * slice_e, filters)
-    terms_own, terms_other = call(
-        functools.partial(own_terms_kernel, slice_e),
-        [smem, vmem, held],
-        [(posts,) + acc_shape] * 2,
-    )(me, pieces, share_own)
-
-    terms = [(terms_own, terms_other)]
-    k = 1
-    while 2 * k < n_filt:
-        part = part + swap(part, k, "filt")
-        part, *terms[0] = lax.optimization_barrier((part, *terms[0]))
-        k *= 2
-    other = swap(part, k, "filt")
 
     def near_terms(x, keep):
         feat, *terms = call(
             functools.partial(near_kernel, len(keep), slice_e),
             [smem] + [vmem] * 3 + [anywhere] * len(keep),
-            [(posts, 8, filters)] + [(posts,) + acc_shape] * 2,
-            posts_scratch(posts),
+            [(x.shape[0], 8, filters)] + [(x.shape[0],) + acc_shape] * 2,
+            posts_scratch(x.shape[0]),
         )(me, x, weights, head_weight, *keep)
         return feat, terms
 
-    feats = [feat_own]
-    feat, term = near_terms(near_pieces[0], ())
-    other, feat, *term = lax.optimization_barrier((other, feat, *term))
-    feats.append(feat)
-    terms.append(term)
-    keep = [x for pair in terms for x in pair]
+    own_terms = call(
+        functools.partial(own_terms_kernel, slice_e),
+        [smem, vmem, vmem],
+        [(posts,) + acc_shape] * 2,
+    )(me, pieces, share_own)
+    parts = [part] + [swap(part, k, "filt") for k in range(1, n_filt)]
+    far_feat, far_terms = near_terms(far_one[None], ())
+    parts, far_one, far_feat, far_terms, own_terms = lax.optimization_barrier(
+        (parts, far_one, far_feat, far_terms, own_terms)
+    )
+    far_two = swap(far_one, 1, "filt")
+    keep = [*own_terms, *far_terms]
     facts, prediction = call(
         functools.partial(facts_kernel, len(keep)),
-        [vmem] * 3 + [anywhere] * len(keep),
+        [vmem] * (n_filt + 1) + [anywhere] * len(keep),
         [(n_facts, 128), (posts,)],
-    )(part, other, base, *keep)
+    )(base, *parts, *keep)
 
     all_facts = [facts] + [swap(facts, k) for k in near] + [swap(facts, far)]
-    for x in near_pieces[1:]:
-        feat, term = near_terms(x, keep)
-        feats.append(feat)
-        terms.append(term)
+    near_feat, first_terms = near_terms(near_pieces[0], keep)
+    terms = list(zip(own_terms, first_terms, far_terms))
     extra = -(-(3 + code_rows(sizes, filters)) // 8) * 8
     acc_own, acc_other = call(
-        functools.partial(last_kernel, n_near, sizes, slice_e),
-        [smem] + [vmem] * (4 + 3 * n_near + 3),
+        functools.partial(last_kernel, sizes, slice_e),
+        [smem] * 2 + [vmem] * 14,
         [acc_shape, (acc_shape[0] + extra, filters)],
-        posts_scratch(posts),
+        posts_scratch(posts + 1),
     )(
         me,
-        far_pieces,
+        half,
         *all_facts,
-        *feats,
-        *[pair[1] for pair in terms],
+        near_pieces[1],
+        far_two,
+        feat_own,
+        near_feat,
+        far_feat,
+        *terms[1],
         weights,
         head_weight,
     )
 
     came = swap(acc_other, 1)
-    (total,) = call(
-        functools.partial(gather_kernel, 1 + n_near),
-        [vmem] * (1 + 2 * (1 + n_near)),
-        [acc_shape],
-    )(acc_own, *all_facts[:-1], *[pair[0] for pair in terms])
+    (total,) = call(gather_kernel, [smem] + [vmem] * 7, [acc_shape])(
+        half, acc_own, all_facts[0], all_facts[1], all_facts[3], *terms[0]
+    )
     grad, head_grad, *codes = call(
         functools.partial(swap_kernel, sizes),
         [vmem] * 3,
@@ -564,7 +572,7 @@
 
 def solution(mesh):
     n_doc, n_filt = mesh.shape["doc"], mesh.shape["filt"]
-    if n_doc == 8 and n_filt in (2, 4):
+    if n_doc == 8 and n_filt == 4:
         local = functools.partial(local_gather, n_doc, n_filt)
     else:
         local = local_scatter

time: 34.7 us -> 32.4 us (0.934)
  waiting for transfers between devices: 6.22 us -> 2.31 us
  starting transfers between devices: 13.2 us -> 15.2 us
  Pallas kernels: 14.4 us -> 13.9 us
    ppermute x9 -> x11, waiting for transfers between devices: 6.22 us -> 2.31 us  [swap(): return lax.ppermute(x, axis, [(i, i ^ k) for i in range(size)])]
    ppermute x9 -> x11, starting transfers between devices: 13.2 us -> 15.2 us  [swap(): return lax.ppermute(x, axis, [(i, i ^ k) for i in range(size)])]
    pallas_call x9, Pallas kernels: 14.4 us -> 13.9 us  [run(): return built(*operands)]
  transfers between devices with their start and end apart: 9 -> 11, of which waited for: 5 -> 3; matrix products, arithmetic and copies ran while one was open for 0% -> 0% of each run, Pallas kernels for 30% -> 28%
where the time goes in v5:
time: 32.4 us; the launch traced here: 32.2 us
  starting transfers between devices  15.2 us (47%)
  Pallas kernels  13.9 us (43%)
  waiting for transfers between devices  2.31 us (7%)
  between operations  0.74 us (2%)
    ppermute x11, starting transfers between devices, swap(): return lax.ppermute(x, axis, [(i, i ^ k) for i in range(size)])  15.2 us
    pallas_call x9, Pallas kernels, run(): return built(*operands)  13.9 us
    ppermute x11, waiting for transfers between devices, swap(): return lax.ppermute(x, axis, [(i, i ^ k) for i in range(size)])  2.31 us
  transfers between devices with their start and end apart: 11, of which 3 were waited for; matrix products, arithmetic and copies ran while one was open for 0% of the time, Pallas kernels for 28%

profile of v5, /device:TPU:0, one launch (start us, length us, event | category | flops | bytes accessed | tf_op | source)
XLA Modules:
  0.0 32.2 jit_solution(12492254336658791853)
XLA Ops:
  0.6 1.1 %shard_map.154 = (f32[2,256,256]{2,1,0:T(8,128)S(1)}, f32[256,256]{1,0:T(8,128)S(1)}) custom-call(s32[1]{0:T(128)} %bitcast.1.d_ref, s32[1]{0:T(128)} %bitcast.z_ref, s32[2]{0:T(128)} %len_any.1, bf16[2,256,256]{2,1,0:T(8,128)(2,1)} %x_any.1), custom_call_target="tpu_custom_call" | custom-call | flops 1 | bytes 1 | tf_op jit(solution)/shard_map/pallas_call | solution.py:446
  1.7 3.0 %collective-permute-start.9 = (f32[2,256,256]{2,1,0:T(8,128)S(1)}, f32[2,256,256]{2,1,0:T(8,128)S(1)}, u32[]{:S(2)}, u32[]{:S(2)}) collective-permute-start(f32[2,256,256]{2,1,0:T(8,128)S(1)} %get-tuple-element.40.refs_9_.pieces), channel_id=1, source_target_pairs={{0,16},{4,20},{8,24},{12,28},{16,0},{20,4},{24,8},{28,12},{1,17},{... | collective-permute-start | bytes 1572872 | tf_op jit(solution)/shard_map/ppermute | solution.py:437
  4.7 1.4 %collective-permute-start.3 = (f32[256,256]{1,0:T(8,128)S(1)}, f32[256,256]{1,0:T(8,128)S(1)}, u32[]{:S(2)}, u32[]{:S(2)}) collective-permute-start(f32[256,256]{1,0:T(8,128)S(1)} %get-tuple-element.43), channel_id=1, source_target_pairs={{0,24},{4,28},{8,16},{12,20},{16,8},{20,12},{24,0},{28,4},{1,25},{... | collective-permute-start | bytes 786440 | tf_op jit(solution)/shard_map/ppermute | solution.py:437
  6.2 0.1 collective-permute-start.7
  6.3 3.7 %shard_map.155 = (f32[8,128]{1,0:T(8,128)S(1)}, f32[2,3,256]{2,1,0:T(4,128)S(1)}, f32[2,3,256,256]{3,2,1,0:T(8,128)S(1)}, f32[16,128]{1,0:T(8,128)S(1)}, bf16[3840,256]{1,0:T(8,128)(2,1)S(1)}) custom-call(s32[2]{0:T(128)} %refs_0_.1, s32[2]{0:T(128)} %refs_1_.1, s32[2]{0:T(128)} %refs_2_.1, f32[2]{0:T(128)} %refs_3_.1, f32[840]{0:T(1024)} %refs_4_.1, ...), custom_call_target="tpu_custom_call" | custom-call | flops 1 | bytes 1 | tf_op jit(solution)/shard_map/pallas_call | solution.py:446
  10.0 4.1 %collective-permute-start.2 = (f32[8,128]{1,0:T(8,128)S(1)}, f32[8,128]{1,0:T(8,128)S(1)}, u32[]{:S(2)}, u32[]{:S(2)}) collective-permute-start(f32[8,128]{1,0:T(8,128)S(1)} %get-tuple-element.51.refs_0_), channel_id=1, source_target_pairs={{0,3},{1,2},{2,1},{3,0},{4,7},{5,6},{6,5},{7,4},{8,11},{9,10},{10,... | collective-permute-start | bytes 12296 | tf_op jit(solution)/shard_map/ppermute | solution.py:437
  14.1 0.0 collective-permute-start.1
  14.1 0.7 %collective-permute-done.3 = f32[256,256]{1,0:T(8,128)S(1)} collective-permute-done((f32[256,256]{1,0:T(8,128)S(1)}, f32[256,256]{1,0:T(8,128)S(1)}, u32[]{:S(2)}, u32[]{:S(2)}) %collective-permute-start.3) | collective-permute-done | bytes 262176 | tf_op jit(solution)/shard_map/ppermute | solution.py:437
  14.9 1.6 %collective-permute-start = (f32[8,128]{1,0:T(8,128)S(1)}, f32[8,128]{1,0:T(8,128)S(1)}, u32[]{:S(2)}, u32[]{:S(2)}) collective-permute-start(f32[8,128]{1,0:T(8,128)S(1)} %get-tuple-element.51.refs_0_), channel_id=1, source_target_pairs={{0,1},{1,0},{2,3},{3,2},{4,5},{5,4},{6,7},{7,6},{8,9},{9,8},{10,11... | collective-permute-start | bytes 12296 | tf_op jit(solution)/shard_map/ppermute | solution.py:437
  16.4 0.9 %shard_map.157 = (f32[2,480,256]{2,1,0:T(8,128)S(1)}, f32[2,480,256]{2,1,0:T(8,128)S(1)}) custom-call(s32[1]{0:T(128)} %bitcast.1.d_ref, f32[2,256,256]{2,1,0:T(8,128)S(1)} %get-tuple-element.40.refs_9_.pieces, f32[2,3,256,256]{3,2,1,0:T(8,128)S(1)} %get-tuple-element.48.share_ref), custom_call_target="tpu_custom_call" | custom-call | flops 1 | bytes 1 | tf_op jit(solution)/shard_map/pallas_call | solution.py:446
  17.3 1.2 %shard_map.156 = (f32[1,8,256]{2,1,0:T(8,128)S(1)}, f32[1,480,256]{2,1,0:T(8,128)S(1)}, f32[1,480,256]{2,1,0:T(8,128)S(1)}) custom-call(s32[1]{0:T(128)} %bitcast.1.d_ref, f32[1,256,256]{2,1,0:T(8,128)S(1)} %bitcast.9, bf16[3840,256]{1,0:T(8,128)(2,1)S(1)} %get-tuple-element.44.w_ref.refs_12_, bf16[3,256]{1,0:T(4,128)(2,1)S(1)} %copy-done), custom_call_target="tpu_custom_call" | custom-call | flops 1 | bytes 1 | tf_op jit(solution)/shard_map/pallas_call | solution.py:446
  18.5 0.0 collective-permute-done.2.refs_3_
  18.5 0.1 collective-permute-done.1.refs_2_
  18.6 1.4 %collective-permute-start.8 = (f32[256,256]{1,0:T(8,128)S(1)}, f32[256,256]{1,0:T(8,128)S(1)}, u32[]{:S(2)}, u32[]{:S(2)}) collective-permute-start(f32[256,256]{1,0:T(8,128)S(1)} %collective-permute-done.3), channel_id=1, source_target_pairs={{0,1},{1,0},{2,3},{3,2},{4,5},{5,4},{6,7},{7,6},{8,9},{9,8},{10,11... | collective-permute-start | bytes 786440 | tf_op jit(solution)/shard_map/ppermute | solution.py:437
  20.1 0.6 %shard_map.158 = (f32[16,128]{1,0:T(8,128)S(1)}, f32[2]{0:T(128)}) custom-call(f32[16,128]{1,0:T(8,128)S(1)} %get-tuple-element.41.base, f32[8,128]{1,0:T(8,128)S(1)} %get-tuple-element.51.refs_0_, f32[8,128]{1,0:T(8,128)S(1)} %collective-permute-done.refs_1_, f32[8,128]{1,0:T(8,128)S(1)} %collective-permute-done.1.refs_2_, ...), custom_call_target="tpu_custom_call" | custom-call | flops 1 | bytes 1 | tf_op jit(solution)/shard_map/pallas_call | solution.py:446
  20.6 1.4 %collective-permute-start.6 = (f32[16,128]{1,0:T(8,128)S(1)}, f32[16,128]{1,0:T(8,128)S(1)}, u32[]{:S(2)}, u32[]{:S(2)}) collective-permute-start(f32[16,128]{1,0:T(8,128)S(1)} %get-tuple-element.59.refs_0_.own_facts), channel_id=1, source_target_pairs={{0,24},{4,28},{8,16},{12,20},{16,8},{20,12},{24,0},{28,4},{1,25},{... | collective-permute-start | bytes 24584 | tf_op jit(solution)/shard_map/ppermute | solution.py:437
  22.1 0.5 %collective-permute-start.5 = (f32[16,128]{1,0:T(8,128)S(1)}, f32[16,128]{1,0:T(8,128)S(1)}, u32[]{:S(2)}, u32[]{:S(2)}) collective-permute-start(f32[16,128]{1,0:T(8,128)S(1)} %get-tuple-element.59.refs_0_.own_facts), channel_id=1, source_target_pairs={{0,8},{4,12},{8,0},{12,4},{16,24},{20,28},{24,16},{28,20},{1,9},{5... | collective-permute-start | bytes 24584 | tf_op jit(solution)/shard_map/ppermute | solution.py:437
  22.6 1.5 %collective-permute-start.4 = (f32[16,128]{1,0:T(8,128)S(1)}, f32[16,128]{1,0:T(8,128)S(1)}, u32[]{:S(2)}, u32[]{:S(2)}) collective-permute-start(f32[16,128]{1,0:T(8,128)S(1)} %get-tuple-element.59.refs_0_.own_facts), channel_id=1, source_target_pairs={{0,16},{4,20},{8,24},{12,28},{16,0},{20,4},{24,8},{28,12},{1,17},{... | collective-permute-start | bytes 24584 | tf_op jit(solution)/shard_map/ppermute | solution.py:437
  24.1 2.4 %shard_map.159 = (f32[2,8,256]{2,1,0:T(8,128)S(1)}, f32[2,480,256]{2,1,0:T(8,128)S(1)}, f32[2,480,256]{2,1,0:T(8,128)S(1)}) custom-call(s32[1]{0:T(128)} %bitcast.1.d_ref, f32[2,256,256]{2,1,0:T(8,128)S(1)} %collective-permute-done.9.x_ref, bf16[3840,256]{1,0:T(8,128)(2,1)S(1)} %get-tuple-element.44.w_ref.refs_12_, bf16[3,256]{1,0:T(4,128)(2,1)S(1)} %copy-done, ...), custom_call_target="tpu_custom_call" | custom-call | flops 1 | bytes 1 | tf_op jit(solution)/shard_map/pallas_call | solution.py:446
  26.6 2.8 %shard_map.160 = (f32[480,256]{1,0:T(8,128)S(1)}, f32[496,256]{1,0:T(8,128)S(1)}) custom-call(s32[1]{0:T(128)} %bitcast.1.d_ref, s32[1]{0:T(128)} %bitcast.z_ref, f32[16,128]{1,0:T(8,128)S(1)} %get-tuple-element.59.refs_0_.own_facts, f32[16,128]{1,0:T(8,128)S(1)} %collective-permute-done.4.refs_1_.near_facts, f32[16,128]{1,0:T(8,128)S(1)} %collective-permute-done.5.refs_2_, ...), custom_call_target="tpu_custom_call" | custom-call | flops 1 | bytes 1 | tf_op jit(solution)/shard_map/pallas_call | solution.py:446
  29.4 0.1 collective-permute-start.10
  29.5 0.4 %shard_map.161.own_ref = f32[480,256]{1,0:T(8,128)S(1)} custom-call(s32[1]{0:T(128)} %bitcast.z_ref, f32[480,256]{1,0:T(8,128)S(1)} %get-tuple-element.65.acc, f32[16,128]{1,0:T(8,128)S(1)} %get-tuple-element.59.refs_0_.own_facts, f32[16,128]{1,0:T(8,128)S(1)} %collective-permute-done.4.refs_1_.near_facts, ...), custom_call_target="tpu_custom_call" | custom-call | flops 1 | bytes 1 | tf_op jit(solution)/shard_map/pallas_call | solution.py:446
  29.9 1.5 %collective-permute-done.10.came_ref = f32[496,256]{1,0:T(8,128)S(1)} collective-permute-done((f32[496,256]{1,0:T(8,128)S(1)}, f32[496,256]{1,0:T(8,128)S(1)}, u32[]{:S(2)}, u32[]{:S(2)}) %collective-permute-start.10) | collective-permute-done | bytes 507936 | tf_op jit(solution)/shard_map/ppermute | solution.py:437
  31.4 0.9 %shard_map.162 = (f32[480,256]{1,0:T(8,128)}, f32[3,256]{1,0:T(4,128)}, f32[840]{0:T(1024)}, f32[40]{0:T(128)}, f32[8]{0:T(128)}) custom-call(f32[480,256]{1,0:T(8,128)S(1)} %shard_map.161.own_ref, f32[496,256]{1,0:T(8,128)S(1)} %get-tuple-element.67.mine_ref, f32[496,256]{1,0:T(8,128)S(1)} %collective-permute-done.10.came_ref), custom_call_target="tpu_custom_call" | custom-call | flops 1 | bytes 1 | tf_op jit(solution)/shard_map/pallas_call | solution.py:446
  (9 shorter events, 0.0 us)
Async XLA Ops:
  1.7 20.9 %collective-permute-start.9 = (f32[2,256,256]{2,1,0:T(8,128)S(1)}, f32[2,256,256]{2,1,0:T(8,128)S(1)}, u32[]{:S(2)}, u32[]{:S(2)}) collective-permute-start(f32[2,256,256]{2,1,0:T(8,128)S(1)} %get-tuple-element.40.refs_9_.pieces), channel_id=1, source_target_pairs={{0,16},{4,20},{8,24},{12,28},{16,0},{20,4},{24,8},{28,12},{1,17},{... | collective-permute-start | bytes 1572872 | tf_op jit(solution)/shard_map/ppermute | solution.py:437
  4.7 10.1 %collective-permute-start.3 = (f32[256,256]{1,0:T(8,128)S(1)}, f32[256,256]{1,0:T(8,128)S(1)}, u32[]{:S(2)}, u32[]{:S(2)}) collective-permute-start(f32[256,256]{1,0:T(8,128)S(1)} %get-tuple-element.43), channel_id=1, source_target_pairs={{0,24},{4,28},{8,16},{12,20},{16,8},{20,12},{24,0},{28,4},{1,25},{... | collective-permute-start | bytes 786440 | tf_op jit(solution)/shard_map/ppermute | solution.py:437
  6.2 20.4 %collective-permute-start.7 = (f32[2,256,256]{2,1,0:T(8,128)S(1)}, f32[2,256,256]{2,1,0:T(8,128)S(1)}, u32[]{:S(2)}, u32[]{:S(2)}) collective-permute-start(f32[2,256,256]{2,1,0:T(8,128)S(1)} %get-tuple-element.40.refs_9_.pieces), channel_id=1, source_target_pairs={{0,8},{4,12},{8,0},{12,4},{16,24},{20,28},{24,16},{28,20},{1,9},{5... | collective-permute-start | bytes 1572872 | tf_op jit(solution)/shard_map/ppermute | solution.py:437
  6.3 11.0 %copy-start = (bf16[3,256]{1,0:T(4,128)(2,1)S(1)}, bf16[3,256]{1,0:T(4,128)(2,1)}, u32[]{:S(2)}) copy-start(bf16[3,256]{1,0:T(4,128)(2,1)} %refs_13_.1) | copy-start | bytes 4612
  10.0 8.5 %collective-permute-start.2 = (f32[8,128]{1,0:T(8,128)S(1)}, f32[8,128]{1,0:T(8,128)S(1)}, u32[]{:S(2)}, u32[]{:S(2)}) collective-permute-start(f32[8,128]{1,0:T(8,128)S(1)} %get-tuple-element.51.refs_0_), channel_id=1, source_target_pairs={{0,3},{1,2},{2,1},{3,0},{4,7},{5,6},{6,5},{7,4},{8,11},{9,10},{10,... | collective-permute-start | bytes 12296 | tf_op jit(solution)/shard_map/ppermute | solution.py:437
  14.1 4.5 %collective-permute-start.1 = (f32[8,128]{1,0:T(8,128)S(1)}, f32[8,128]{1,0:T(8,128)S(1)}, u32[]{:S(2)}, u32[]{:S(2)}) collective-permute-start(f32[8,128]{1,0:T(8,128)S(1)} %get-tuple-element.51.refs_0_), channel_id=1, source_target_pairs={{0,2},{1,3},{2,0},{3,1},{4,6},{5,7},{6,4},{7,5},{8,10},{9,11},{10,... | collective-permute-start | bytes 12296 | tf_op jit(solution)/shard_map/ppermute | solution.py:437
  14.9 3.8 %collective-permute-start = (f32[8,128]{1,0:T(8,128)S(1)}, f32[8,128]{1,0:T(8,128)S(1)}, u32[]{:S(2)}, u32[]{:S(2)}) collective-permute-start(f32[8,128]{1,0:T(8,128)S(1)} %get-tuple-element.51.refs_0_), channel_id=1, source_target_pairs={{0,1},{1,0},{2,3},{3,2},{4,5},{5,4},{6,7},{7,6},{8,9},{9,8},{10,11... | collective-permute-start | bytes 12296 | tf_op jit(solution)/shard_map/ppermute | solution.py:437
  18.6 7.9 %collective-permute-start.8 = (f32[256,256]{1,0:T(8,128)S(1)}, f32[256,256]{1,0:T(8,128)S(1)}, u32[]{:S(2)}, u32[]{:S(2)}) collective-permute-start(f32[256,256]{1,0:T(8,128)S(1)} %collective-permute-done.3), channel_id=1, source_target_pairs={{0,1},{1,0},{2,3},{3,2},{4,5},{5,4},{6,7},{7,6},{8,9},{9,8},{10,11... | collective-permute-start | bytes 786440 | tf_op jit(solution)/shard_map/ppermute | solution.py:437
  20.6 5.9 %collective-permute-start.6 = (f32[16,128]{1,0:T(8,128)S(1)}, f32[16,128]{1,0:T(8,128)S(1)}, u32[]{:S(2)}, u32[]{:S(2)}) collective-permute-start(f32[16,128]{1,0:T(8,128)S(1)} %get-tuple-element.59.refs_0_.own_facts), channel_id=1, source_target_pairs={{0,24},{4,28},{8,16},{12,20},{16,8},{20,12},{24,0},{28,4},{1,25},{... | collective-permute-start | bytes 24584 | tf_op jit(solution)/shard_map/ppermute | solution.py:437
  22.1 4.4 %collective-permute-start.5 = (f32[16,128]{1,0:T(8,128)S(1)}, f32[16,128]{1,0:T(8,128)S(1)}, u32[]{:S(2)}, u32[]{:S(2)}) collective-permute-start(f32[16,128]{1,0:T(8,128)S(1)} %get-tuple-element.59.refs_0_.own_facts), channel_id=1, source_target_pairs={{0,8},{4,12},{8,0},{12,4},{16,24},{20,28},{24,16},{28,20},{1,9},{5... | collective-permute-start | bytes 24584 | tf_op jit(solution)/shard_map/ppermute | solution.py:437
  22.6 3.9 %collective-permute-start.4 = (f32[16,128]{1,0:T(8,128)S(1)}, f32[16,128]{1,0:T(8,128)S(1)}, u32[]{:S(2)}, u32[]{:S(2)}) collective-permute-start(f32[16,128]{1,0:T(8,128)S(1)} %get-tuple-element.59.refs_0_.own_facts), channel_id=1, source_target_pairs={{0,16},{4,20},{8,24},{12,28},{16,0},{20,4},{24,8},{28,12},{1,17},{... | collective-permute-start | bytes 24584 | tf_op jit(solution)/shard_map/ppermute | solution.py:437
  29.4 2.0 %collective-permute-start.10 = (f32[496,256]{1,0:T(8,128)S(1)}, f32[496,256]{1,0:T(8,128)S(1)}, u32[]{:S(2)}, u32[]{:S(2)}) collective-permute-start(f32[496,256]{1,0:T(8,128)S(1)} %get-tuple-element.67.mine_ref), channel_id=1, source_target_pairs={{0,4},{4,0},{8,12},{12,8},{16,20},{20,16},{24,28},{28,24},{1,5},{5... | collective-permute-start | bytes 1523720 | tf_op jit(solution)/shard_map/ppermute | solution.py:437

commit v6 on v5

--- a/solution.py
+++ b/solution.py
@@ -211,18 +211,11 @@
 
 def own_kernel(*refs):
     small = refs[:8]
-    w_any, pieces, part_ref, feat_ref, share_ref, base_ref, w_ref = refs[8:15]
-    held = refs[15:23]
-    xpad, cols, counts, small_sems, w_sems = refs[23:]
+    w_ref, pieces, part_ref, feat_ref, share_ref, base_ref = refs[8:14]
+    held = refs[14:22]
+    xpad, cols, counts, small_sems = refs[22:]
     posts = pieces.shape[0]
-    width = w_ref.shape[0] // TAPS
-    loads = []
-    for tap in range(TAPS):
-        place = pl.ds(tap * width, width)
-        loads.append(pltpu.make_async_copy(w_any.at[place], w_ref.at[place], w_sems.at[tap]))
     copies = [pltpu.make_async_copy(small[i], held[i], small_sems.at[i]) for i in range(8)]
-    for load in loads[::-1]:
-        load.start()
     for copy in copies:
         copy.start()
     for p in range(posts):
@@ -232,9 +225,6 @@
     head = held[7][...].astype(jnp.float32)
     parts = [jnp.zeros((1, head.shape[1]), jnp.float32) for _ in range(posts)]
     for index in (2, 1, 0):
-        taps, first = WIDTH_LIST[index]
-        for load in loads[first : first + taps]:
-            load.wait()
         for p in range(posts):
             feature, share = forward(index, cols.at[p], w_ref, head, counts.at[p])
             feat_ref[p, index : index + 1, :] = feature
@@ -276,21 +266,23 @@
         facts_ref[p : p + 1, :] = value - base[4 * posts + p : 4 * posts + p + 1, :]
 
 
-def near_kernel(n_keep, slice_e, d_ref, x_ref, w_ref, head_ref, *refs):
+def far_kernel(n_keep, slice_e, d_ref, x_ref, w_ref, head_ref, *refs):
     feat_ref, own_ref, other_ref, xpads, counts, cols = refs[n_keep:]
-    posts = x_ref.shape[0]
     head = head_ref[...].astype(jnp.float32)
-    for p in range(posts):
-        load_post(x_ref[p], xpads.at[p], counts.at[p])
-        make_cols(xpads.at[p], cols.at[p])
-    for p in range(posts):
-        slopes = []
-        for index in range(3):
-            feature, share = forward(index, cols.at[p], w_ref, head, counts.at[p])
-            feat_ref[p, index : index + 1, :] = feature
-            slopes.append(share.astype(jnp.bfloat16))
-        at = pick_rows(d_ref, middle_of(cols.at[p]), slice_e)
-        add_terms(at, slopes, own_ref.at[p], other_ref.at[p], slice_e, fresh=True)
+    load_post(x_ref[...], xpads.at[0], counts.at[0])
+    make_cols(xpads.at[0], cols.at[0])
+    slopes = []
+    for index in range(3):
+        feature, share = forward(index, cols.at[0], w_ref, head, counts.at[0])
+        feat_ref[index : index + 1, :] = feature
+        slopes.append(share.astype(jnp.bfloat16))
+    at = pick_rows(d_ref, middle_of(cols.at[0]), slice_e)
+    add_terms(at, slopes, own_ref.at[0], other_ref.at[0], slice_e, fresh=True)
+
+
+def made_residuals(here, posts, own, far):
+    rows = [own[p : p + 1, 0:1] for p in range(posts)]
+    return rows + [far[pl.ds(here, 1), 0:1], far[pl.ds(1 - here, 1), 0:1]]
 
 
 def scaled_sum(residuals, terms):
@@ -303,24 +295,20 @@
 
 
 def last_kernel(sizes, slice_e, d_ref, z_ref, *refs):
-    facts, last, far = refs[:4], refs[4], refs[5]
-    feats, terms = refs[6:9], refs[9:12]
+    facts, near = refs[:4], refs[4:6]
+    (feat_own, *feat_far), terms = refs[6:9], refs[9:12]
     w_ref, head_ref, acc_own, acc_other, xpads, counts, cols = refs[12:]
-    posts = last.shape[0]
+    posts = near[0].shape[0]
     n_rows, filters = acc_own.shape
     head = head_ref[...].astype(jnp.float32)
-    pieces = [last[p] for p in range(posts)] + [far[...]]
     here = z_ref[0]
-    residuals = [facts[2][p : p + 1, 0:1] for p in range(posts)]
-    residuals.append(facts[3][pl.ds(1 - here, 1), 0:1])
+    pieces = [x[p] for x in near for p in range(posts)]
+    residuals = [fact[p : p + 1, 0:1] for fact in facts[1:3] for p in range(posts)]
     for p, piece in enumerate(pieces):
         load_post(piece, xpads.at[p], counts.at[p])
         make_cols(xpads.at[p], cols.at[p])
     acc_own[...] = jnp.zeros_like(acc_own)
-    made = [facts[0][p : p + 1, 0:1] for p in range(posts)]
-    made += [facts[1][p : p + 1, 0:1] for p in range(posts)]
-    made.append(facts[3][pl.ds(here, 1), 0:1])
-    acc_other[0:n_rows, :] = scaled_sum(made, terms)
+    acc_other[0:n_rows, :] = scaled_sum(made_residuals(here, posts, facts[0], facts[3]), terms)
     slopes = [[], [], []]
     feat_last = []
     for p, residual in enumerate(residuals):
@@ -331,7 +319,7 @@
             slopes[index].append((residual * share).astype(jnp.bfloat16))
         feat_last.append(jnp.concatenate(features, axis=0))
     at = jnp.concatenate(
-        [pick_rows(d_ref, middle_of(cols.at[p]), slice_e) for p in range(posts + 1)], axis=1
+        [pick_rows(d_ref, middle_of(cols.at[p]), slice_e) for p in range(len(pieces))], axis=1
     )
     slopes = [jnp.concatenate(parts, axis=0) for parts in slopes]
     add_terms(at, slopes, acc_own, acc_other, slice_e)
@@ -352,20 +340,23 @@
                 code_term = code_term + jnp.where(place == code, residual, 0.0)
         return head_term, code_term
 
-    features = [[feat[p, 0:3, :] for p in range(posts)] for feat in feats[:2]]
-    features.append(feat_last[:posts])
-    one, two = feats[2][0, 0:3, :], feat_last[posts]
-    features.append([jnp.where(here == p, one, two) for p in range(posts)])
+    features = [
+        [feat_own[p] for p in range(posts)],
+        feat_last[:posts],
+        feat_last[posts:],
+        [
+            jnp.where(here == p, feat_far[0][0:3, :], feat_far[1][0:3, :])
+            for p in range(posts)
+        ],
+    ]
     sums = [chip_terms(fact[...], feature) for fact, feature in zip(facts, features)]
     acc_other[n_rows:, :] = jnp.zeros((acc_other.shape[0] - n_rows, filters), jnp.float32)
     acc_other[n_rows : n_rows + 3, :] = tree_sum([total[0] for total in sums])
     acc_other[n_rows + 3 : n_rows + 3 + n_codes, :] = tree_sum([total[1] for total in sums])
 
 
-def gather_kernel(z_ref, acc, own_facts, near_facts, far_facts, *refs):
-    posts = refs[0].shape[0]
-    made = [facts[p : p + 1, 0:1] for facts in (own_facts, near_facts) for p in range(posts)]
-    made.append(far_facts[pl.ds(z_ref[0], 1), 0:1])
+def gather_kernel(z_ref, acc, own_facts, far_facts, *refs):
+    made = made_residuals(z_ref[0], refs[0].shape[0], own_facts, far_facts)
     refs[-1][...] = acc[...] + scaled_sum(made, refs[:-1])
 
 
@@ -437,7 +428,7 @@
         return lax.ppermute(x, axis, [(i, i ^ k) for i in range(size)])
 
 
-    def call(kernel, specs, out, scratch=()):
+    def call(kernel, specs, out, scratch=(), cost=1):
         def run(*operands):
             operands = [
                 pltpu.with_memory_space_constraint(x, pltpu.HBM) if spec is hbm else x
@@ -454,7 +445,7 @@
             ],
             scratch_shapes=list(scratch),
             compiler_params=pltpu.CompilerParams(vmem_limit_bytes=24 << 20),
-            cost_estimate=pl.CostEstimate(flops=1, bytes_accessed=1, transcendentals=0),
+            cost_estimate=pl.CostEstimate(flops=cost, bytes_accessed=1, transcendentals=0),
         )
         return run
 
@@ -471,6 +462,7 @@
             pltpu.SMEM((posts,), i32),
             pltpu.SemaphoreType.DMA((posts + 1,)),
         ],
+        cost=10000000000,
     )(me, half, lengths, embedded)
 
     near = [k for k in range(2, n_doc, 2) if bin(k).count("1") == 1][::-1]
@@ -478,22 +470,21 @@
     far_one = swap(far_piece, far)
     near_pieces = [swap(pieces, k) for k in near]
 
-    part, feat_own, share_own, base, weights = call(
+    part, feat_own, share_own, base = call(
         own_kernel,
-        [hbm] * 9 + [vmem],
+        [hbm] * 8 + [vmem] * 2,
         [
             (8, 128),
             (posts, 3, filters),
             (posts, 3, seq_len, filters),
             (n_facts, 128),
-            jax.ShapeDtypeStruct(weights.shape, weights.dtype),
         ],
         [pltpu.SMEM((posts,), i32)] * 3
         + [pltpu.SMEM((posts,), f32)]
         + [pltpu.SMEM((size,), f32) for size in sizes]
         + [pltpu.VMEM(head_weight.shape, head_weight.dtype)]
         + [posts_scratch(posts)[i] for i in (0, 2, 1)]
-        + [pltpu.SemaphoreType.DMA((8,)), pltpu.SemaphoreType.DMA((TAPS,))],
+        + [pltpu.SemaphoreType.DMA((8,))],
     )(
         occupation,
         cohort,
@@ -507,12 +498,13 @@
         pieces,
     )
 
-    def near_terms(x, keep):
+    def far_terms_of(x, keep, cost=1):
         feat, *terms = call(
-            functools.partial(near_kernel, len(keep), slice_e),
+            functools.partial(far_kernel, len(keep), slice_e),
             [smem] + [vmem] * 3 + [anywhere] * len(keep),
-            [(x.shape[0], 8, filters)] + [(x.shape[0],) + acc_shape] * 2,
-            posts_scratch(x.shape[0]),
+            [(8, filters)] + [(1,) + acc_shape] * 2,
+            posts_scratch(1),
+            cost,
         )(me, x, weights, head_weight, *keep)
         return feat, terms
 
@@ -521,45 +513,47 @@
         [smem, vmem, vmem],
         [(posts,) + acc_shape] * 2,
     )(me, pieces, share_own)
-    parts = [part] + [swap(part, k, "filt") for k in range(1, n_filt)]
-    far_feat, far_terms = near_terms(far_one[None], ())
-    parts, far_one, far_feat, far_terms, own_terms = lax.optimization_barrier(
-        (parts, far_one, far_feat, far_terms, own_terms)
-    )
+    k = n_filt // 2
+    while k > 1:
+        part = part + swap(part, k, "filt")
+        part, far_one, own_terms = lax.optimization_barrier((part, far_one, own_terms))
+        k //= 2
+    parts = [part, swap(part, 1, "filt")]
     far_two = swap(far_one, 1, "filt")
+    far_feat, far_terms = far_terms_of(far_one, (), 4000000000)
+    parts, far_feat, far_terms = lax.optimization_barrier((parts, far_feat, far_terms))
     keep = [*own_terms, *far_terms]
     facts, prediction = call(
         functools.partial(facts_kernel, len(keep)),
-        [vmem] * (n_filt + 1) + [anywhere] * len(keep),
+        [vmem] * (1 + len(parts)) + [anywhere] * len(keep),
         [(n_facts, 128), (posts,)],
     )(base, *parts, *keep)
 
     all_facts = [facts] + [swap(facts, k) for k in near] + [swap(facts, far)]
-    near_feat, first_terms = near_terms(near_pieces[0], keep)
-    terms = list(zip(own_terms, first_terms, far_terms))
+    far_feat_two, far_terms_two = far_terms_of(far_two, keep)
+    terms = list(zip(own_terms, far_terms, far_terms_two))
     extra = -(-(3 + code_rows(sizes, filters)) // 8) * 8
     acc_own, acc_other = call(
         functools.partial(last_kernel, sizes, slice_e),
         [smem] * 2 + [vmem] * 14,
         [acc_shape, (acc_shape[0] + extra, filters)],
-        posts_scratch(posts + 1),
+        posts_scratch(2 * posts),
     )(
         me,
         half,
         *all_facts,
-        near_pieces[1],
-        far_two,
+        *near_pieces,
         feat_own,
-        near_feat,
         far_feat,
+        far_feat_two,
         *terms[1],
         weights,
         head_weight,
     )
 
     came = swap(acc_other, 1)
-    (total,) = call(gather_kernel, [smem] + [vmem] * 7, [acc_shape])(
-        half, acc_own, all_facts[0], all_facts[1], all_facts[3], *terms[0]
+    (total,) = call(gather_kernel, [smem] + [vmem] * 6, [acc_shape])(
+        half, acc_own, all_facts[0], all_facts[3], *terms[0]
     )
     grad, head_grad, *codes = call(
         functools.partial(swap_kernel, sizes),

time: 32.4 us -> 31.8 us (0.981)
  waiting for transfers between devices: 2.31 us -> 4.36 us
  Pallas kernels: 13.9 us -> 11.9 us
  starting transfers between devices: 15.2 us -> 14.6 us
    ppermute x11 -> x10, waiting for transfers between devices: 2.31 us -> 4.36 us  [swap(): return lax.ppermute(x, axis, [(i, i ^ k) for i in range(size)])]
    pallas_call x9, Pallas kernels: 13.9 us -> 11.9 us  [run(): return built(*operands)]
    ppermute x11 -> x10, starting transfers between devices: 15.2 us -> 14.6 us  [swap(): return lax.ppermute(x, axis, [(i, i ^ k) for i in range(size)])]
  transfers between devices with their start and end apart: 11 -> 10, of which waited for: 3 -> 5; matrix products, arithmetic and copies ran while one was open for 0% -> 0% of each run, Pallas kernels for 28% -> 20%
where the time goes in v6:
time: 31.8 us; the launch traced here: 31.6 us
  starting transfers between devices  14.6 us (46%)
  Pallas kernels  11.9 us (37%)
  waiting for transfers between devices  4.36 us (14%)
  between operations  0.72 us (2%)
    ppermute x10, starting transfers between devices, swap(): return lax.ppermute(x, axis, [(i, i ^ k) for i in range(size)])  14.6 us
    pallas_call x9, Pallas kernels, run(): return built(*operands)  11.9 us
    ppermute x10, waiting for transfers between devices, swap(): return lax.ppermute(x, axis, [(i, i ^ k) for i in range(size)])  4.36 us
  transfers between devices with their start and end apart: 10, of which 5 were waited for; matrix products, arithmetic and copies ran while one was open for 0% of the time, Pallas kernels for 20%

profile of v6, /device:TPU:0, one launch (start us, length us, event | category | flops | bytes accessed | tf_op | source)
XLA Modules:
  0.0 31.6 jit_solution(15148896537722710460)
XLA Ops:
  0.6 1.2 %shard_map.154 = (f32[2,256,256]{2,1,0:T(8,128)S(1)}, f32[256,256]{1,0:T(8,128)S(1)}) custom-call(s32[1]{0:T(128)} %bitcast.1.d_ref, s32[1]{0:T(128)} %bitcast.z_ref, s32[2]{0:T(128)} %len_any.1, bf16[2,256,256]{2,1,0:T(8,128)(2,1)} %x_any.1), custom_call_target="tpu_custom_call" | custom-call | flops 10000000000 | bytes 1 | tf_op jit(solution)/shard_map/pallas_call | solution.py:437
  1.8 4.0 %collective-permute-start.1 = (f32[256,256]{1,0:T(8,128)S(1)}, f32[256,256]{1,0:T(8,128)S(1)}, u32[]{:S(2)}, u32[]{:S(2)}) collective-permute-start(f32[256,256]{1,0:T(8,128)S(1)} %get-tuple-element.41), channel_id=1, source_target_pairs={{0,24},{4,28},{8,16},{12,20},{16,8},{20,12},{24,0},{28,4},{1,25},{... | collective-permute-start | bytes 786440 | tf_op jit(solution)/shard_map/ppermute | solution.py:428
  5.8 0.5 %collective-permute-start.7 = (f32[2,256,256]{2,1,0:T(8,128)S(1)}, f32[2,256,256]{2,1,0:T(8,128)S(1)}, u32[]{:S(2)}, u32[]{:S(2)}) collective-permute-start(f32[2,256,256]{2,1,0:T(8,128)S(1)} %get-tuple-element.38.refs_9_.pieces), channel_id=1, source_target_pairs={{0,8},{4,12},{8,0},{12,4},{16,24},{20,28},{24,16},{28,20},{1,9},{5... | collective-permute-start | bytes 1572872 | tf_op jit(solution)/shard_map/ppermute | solution.py:428
  6.3 0.1 collective-permute-start.6
  6.5 2.3 %shard_map.155 = (f32[8,128]{1,0:T(8,128)S(1)}, f32[2,3,256]{2,1,0:T(4,128)S(1)}, f32[2,3,256,256]{3,2,1,0:T(8,128)S(1)}, f32[16,128]{1,0:T(8,128)S(1)}) custom-call(s32[2]{0:T(128)} %refs_0_.1, s32[2]{0:T(128)} %refs_1_.1, s32[2]{0:T(128)} %refs_2_.1, f32[2]{0:T(128)} %refs_3_.1, f32[840]{0:T(1024)} %refs_4_.1, f32[40]{0:T(128)} %refs_5_.1, f32[8]{0:T(128)} %refs_6_.1, ...), custom_call_target="tpu_custom_call" | custom-call | flops 1 | bytes 1 | tf_op jit(solution)/shard_map/pallas_call | solution.py:437
  8.8 3.1 %collective-permute-start = (f32[8,128]{1,0:T(8,128)S(1)}, f32[8,128]{1,0:T(8,128)S(1)}, u32[]{:S(2)}, u32[]{:S(2)}) collective-permute-start(f32[8,128]{1,0:T(8,128)S(1)} %get-tuple-element.40), channel_id=1, source_target_pairs={{0,2},{1,3},{2,0},{3,1},{4,6},{5,7},{6,4},{7,5},{8,10},{9,11},{10,... | collective-permute-start | bytes 12296 | tf_op jit(solution)/shard_map/ppermute | solution.py:428
  11.9 0.9 %shard_map.156 = (f32[2,480,256]{2,1,0:T(8,128)S(1)}, f32[2,480,256]{2,1,0:T(8,128)S(1)}) custom-call(s32[1]{0:T(128)} %bitcast.1.d_ref, f32[2,256,256]{2,1,0:T(8,128)S(1)} %get-tuple-element.38.refs_9_.pieces, f32[2,3,256,256]{3,2,1,0:T(8,128)S(1)} %get-tuple-element.42.share_ref), custom_call_target="tpu_custom_call" | custom-call | flops 1 | bytes 1 | tf_op jit(solution)/shard_map/pallas_call | solution.py:437
  12.7 0.7 %collective-permute-done = f32[8,128]{1,0:T(8,128)S(1)} collective-permute-done((f32[8,128]{1,0:T(8,128)S(1)}, f32[8,128]{1,0:T(8,128)S(1)}, u32[]{:S(2)}, u32[]{:S(2)}) %collective-permute-start) | collective-permute-done | bytes 4128 | tf_op jit(solution)/shard_map/ppermute | solution.py:428
  13.5 1.9 %collective-permute-start.2 = (f32[8,128]{1,0:T(8,128)S(1)}, f32[8,128]{1,0:T(8,128)S(1)}, u32[]{:S(2)}, u32[]{:S(2)}) collective-permute-start(f32[8,128]{1,0:T(8,128)S(1)} %add.3.refs_0_), channel_id=1, source_target_pairs={{0,1},{1,0},{2,3},{3,2},{4,5},{5,4},{6,7},{7,6},{8,9},{9,8},{10,11... | collective-permute-start | bytes 12296 | tf_op jit(solution)/shard_map/ppermute | solution.py:428
  15.4 0.1 collective-permute-start.8
  15.5 1.2 %shard_map.157 = (f32[8,256]{1,0:T(8,128)S(1)}, f32[1,480,256]{2,1,0:T(8,128)S(1)}, f32[1,480,256]{2,1,0:T(8,128)S(1)}) custom-call(s32[1]{0:T(128)} %bitcast.1.d_ref, f32[256,256]{1,0:T(8,128)S(1)} %collective-permute-done.1.x_ref, bf16[3840,256]{1,0:T(8,128)(2,1)S(1)} %bitcast.9, bf16[3,256]{1,0:T(4,128)(2,1)S(1)} %copy-done.1), custom_call_target="tpu_custom_call" | custom-call | flops 4000000000 | bytes 1 | tf_op jit(solution)/shard_map/pallas_call | solution.py:437
  16.7 0.5 %collective-permute-done.2.refs_1_ = f32[8,128]{1,0:T(8,128)S(1)} collective-permute-done((f32[8,128]{1,0:T(8,128)S(1)}, f32[8,128]{1,0:T(8,128)S(1)}, u32[]{:S(2)}, u32[]{:S(2)}) %collective-permute-start.2) | collective-permute-done | bytes 4128 | tf_op jit(solution)/shard_map/ppermute | solution.py:428
  17.1 0.6 %shard_map.158 = (f32[16,128]{1,0:T(8,128)S(1)}, f32[2]{0:T(128)}) custom-call(f32[16,128]{1,0:T(8,128)S(1)} %get-tuple-element.39.base, f32[8,128]{1,0:T(8,128)S(1)} %add.3.refs_0_, f32[8,128]{1,0:T(8,128)S(1)} %collective-permute-done.2.refs_1_, f32[2,480,256]{2,1,0:T(8,128)S(1)} %get-tuple-element.52.refs_2_.refs_0_, ...), custom_call_target="tpu_custom_call" | custom-call | flops 1 | bytes 1 | tf_op jit(solution)/shard_map/pallas_call | solution.py:437
  17.7 2.8 %collective-permute-start.5 = (f32[16,128]{1,0:T(8,128)S(1)}, f32[16,128]{1,0:T(8,128)S(1)}, u32[]{:S(2)}, u32[]{:S(2)}) collective-permute-start(f32[16,128]{1,0:T(8,128)S(1)} %get-tuple-element.56.refs_0_.own_facts), channel_id=1, source_target_pairs={{0,24},{4,28},{8,16},{12,20},{16,8},{20,12},{24,0},{28,4},{1,25},{... | collective-permute-start | bytes 24584 | tf_op jit(solution)/shard_map/ppermute | solution.py:428
  20.5 0.5 %collective-permute-start.4 = (f32[16,128]{1,0:T(8,128)S(1)}, f32[16,128]{1,0:T(8,128)S(1)}, u32[]{:S(2)}, u32[]{:S(2)}) collective-permute-start(f32[16,128]{1,0:T(8,128)S(1)} %get-tuple-element.56.refs_0_.own_facts), channel_id=1, source_target_pairs={{0,8},{4,12},{8,0},{12,4},{16,24},{20,28},{24,16},{28,20},{1,9},{5... | collective-permute-start | bytes 24584 | tf_op jit(solution)/shard_map/ppermute | solution.py:428
  21.1 0.7 %collective-permute-done.8.x_ref = f32[256,256]{1,0:T(8,128)S(1)} collective-permute-done((f32[256,256]{1,0:T(8,128)S(1)}, f32[256,256]{1,0:T(8,128)S(1)}, u32[]{:S(2)}, u32[]{:S(2)}) %collective-permute-start.8) | collective-permute-done | bytes 262176 | tf_op jit(solution)/shard_map/ppermute | solution.py:428
  21.7 1.5 %collective-permute-start.3 = (f32[16,128]{1,0:T(8,128)S(1)}, f32[16,128]{1,0:T(8,128)S(1)}, u32[]{:S(2)}, u32[]{:S(2)}) collective-permute-start(f32[16,128]{1,0:T(8,128)S(1)} %get-tuple-element.56.refs_0_.own_facts), channel_id=1, source_target_pairs={{0,16},{4,20},{8,24},{12,28},{16,0},{20,4},{24,8},{28,12},{1,17},{... | collective-permute-start | bytes 24584 | tf_op jit(solution)/shard_map/ppermute | solution.py:428
  23.3 1.2 %shard_map.159 = (f32[8,256]{1,0:T(8,128)S(1)}, f32[1,480,256]{2,1,0:T(8,128)S(1)}, f32[1,480,256]{2,1,0:T(8,128)S(1)}) custom-call(s32[1]{0:T(128)} %bitcast.1.d_ref, f32[256,256]{1,0:T(8,128)S(1)} %collective-permute-done.8.x_ref, bf16[3840,256]{1,0:T(8,128)(2,1)S(1)} %bitcast.10, bf16[3,256]{1,0:T(4,128)(2,1)S(1)} %copy-done.1, ...), custom_call_target="tpu_custom_call" | custom-call | flops 1 | bytes 1 | tf_op jit(solution)/shard_map/pallas_call | solution.py:437
  24.4 0.9 %collective-permute-done.3.refs_1_ = f32[16,128]{1,0:T(8,128)S(1)} collective-permute-done((f32[16,128]{1,0:T(8,128)S(1)}, f32[16,128]{1,0:T(8,128)S(1)}, u32[]{:S(2)}, u32[]{:S(2)}) %collective-permute-start.3) | collective-permute-done | bytes 8224 | tf_op jit(solution)/shard_map/ppermute | solution.py:428
  25.4 3.4 %shard_map.160 = (f32[480,256]{1,0:T(8,128)S(1)}, f32[496,256]{1,0:T(8,128)S(1)}) custom-call(s32[1]{0:T(128)} %bitcast.1.d_ref, s32[1]{0:T(128)} %bitcast.z_ref, f32[16,128]{1,0:T(8,128)S(1)} %get-tuple-element.56.refs_0_.own_facts, f32[16,128]{1,0:T(8,128)S(1)} %collective-permute-done.3.refs_1_, f32[16,128]{1,0:T(8,128)S(1)} %collective-permute-done.4.refs_2_, ...), custom_call_target="tpu_custom_call" | custom-call | flops 1 | bytes 1 | tf_op jit(solution)/shard_map/pallas_call | solution.py:437
  28.8 0.1 collective-permute-start.9
  28.9 0.3 %shard_map.161.own_ref = f32[480,256]{1,0:T(8,128)S(1)} custom-call(s32[1]{0:T(128)} %bitcast.z_ref, f32[480,256]{1,0:T(8,128)S(1)} %get-tuple-element.61.acc, f32[16,128]{1,0:T(8,128)S(1)} %get-tuple-element.56.refs_0_.own_facts, f32[16,128]{1,0:T(8,128)S(1)} %collective-permute-done.5.refs_3_.far_facts, ...), custom_call_target="tpu_custom_call" | custom-call | flops 1 | bytes 1 | tf_op jit(solution)/shard_map/pallas_call | solution.py:437
  29.2 1.5 %collective-permute-done.9.came_ref = f32[496,256]{1,0:T(8,128)S(1)} collective-permute-done((f32[496,256]{1,0:T(8,128)S(1)}, f32[496,256]{1,0:T(8,128)S(1)}, u32[]{:S(2)}, u32[]{:S(2)}) %collective-permute-start.9) | collective-permute-done | bytes 507936 | tf_op jit(solution)/shard_map/ppermute | solution.py:428
  30.7 0.9 %shard_map.162 = (f32[480,256]{1,0:T(8,128)}, f32[3,256]{1,0:T(4,128)}, f32[840]{0:T(1024)}, f32[40]{0:T(128)}, f32[8]{0:T(128)}) custom-call(f32[480,256]{1,0:T(8,128)S(1)} %shard_map.161.own_ref, f32[496,256]{1,0:T(8,128)S(1)} %get-tuple-element.63.mine_ref, f32[496,256]{1,0:T(8,128)S(1)} %collective-permute-done.9.came_ref), custom_call_target="tpu_custom_call" | custom-call | flops 1 | bytes 1 | tf_op jit(solution)/shard_map/pallas_call | solution.py:437
  (10 shorter events, 0.0 us)
Async XLA Ops:
  0.6 5.8 %copy-start = (bf16[256,15,256]{2,0,1:T(8,128)(2,1)S(1)}, bf16[256,15,256]{2,0,1:T(8,128)(2,1)}, u32[]{:S(2)}) copy-start(bf16[256,15,256]{2,0,1:T(8,128)(2,1)} %param.13) | copy-start | bytes 5898244
  1.8 11.6 %collective-permute-start.1 = (f32[256,256]{1,0:T(8,128)S(1)}, f32[256,256]{1,0:T(8,128)S(1)}, u32[]{:S(2)}, u32[]{:S(2)}) collective-permute-start(f32[256,256]{1,0:T(8,128)S(1)} %get-tuple-element.41), channel_id=1, source_target_pairs={{0,24},{4,28},{8,16},{12,20},{16,8},{20,12},{24,0},{28,4},{1,25},{... | collective-permute-start | bytes 786440 | tf_op jit(solution)/shard_map/ppermute | solution.py:428
  5.8 19.6 %collective-permute-start.7 = (f32[2,256,256]{2,1,0:T(8,128)S(1)}, f32[2,256,256]{2,1,0:T(8,128)S(1)}, u32[]{:S(2)}, u32[]{:S(2)}) collective-permute-start(f32[2,256,256]{2,1,0:T(8,128)S(1)} %get-tuple-element.38.refs_9_.pieces), channel_id=1, source_target_pairs={{0,8},{4,12},{8,0},{12,4},{16,24},{20,28},{24,16},{28,20},{1,9},{5... | collective-permute-start | bytes 1572872 | tf_op jit(solution)/shard_map/ppermute | solution.py:428
  6.3 19.0 %collective-permute-start.6 = (f32[2,256,256]{2,1,0:T(8,128)S(1)}, f32[2,256,256]{2,1,0:T(8,128)S(1)}, u32[]{:S(2)}, u32[]{:S(2)}) collective-permute-start(f32[2,256,256]{2,1,0:T(8,128)S(1)} %get-tuple-element.38.refs_9_.pieces), channel_id=1, source_target_pairs={{0,16},{4,20},{8,24},{12,28},{16,0},{20,4},{24,8},{28,12},{1,17},{... | collective-permute-start | bytes 1572872 | tf_op jit(solution)/shard_map/ppermute | solution.py:428
  6.5 9.0 %copy-start.1 = (bf16[3,256]{1,0:T(4,128)(2,1)S(1)}, bf16[3,256]{1,0:T(4,128)(2,1)}, u32[]{:S(2)}) copy-start(bf16[3,256]{1,0:T(4,128)(2,1)} %refs_13_.1) | copy-start | bytes 4612
  8.8 4.6 %collective-permute-start = (f32[8,128]{1,0:T(8,128)S(1)}, f32[8,128]{1,0:T(8,128)S(1)}, u32[]{:S(2)}, u32[]{:S(2)}) collective-permute-start(f32[8,128]{1,0:T(8,128)S(1)} %get-tuple-element.40), channel_id=1, source_target_pairs={{0,2},{1,3},{2,0},{3,1},{4,6},{5,7},{6,4},{7,5},{8,10},{9,11},{10,... | collective-permute-start | bytes 12296 | tf_op jit(solution)/shard_map/ppermute | solution.py:428
  13.5 3.7 %collective-permute-start.2 = (f32[8,128]{1,0:T(8,128)S(1)}, f32[8,128]{1,0:T(8,128)S(1)}, u32[]{:S(2)}, u32[]{:S(2)}) collective-permute-start(f32[8,128]{1,0:T(8,128)S(1)} %add.3.refs_0_), channel_id=1, source_target_pairs={{0,1},{1,0},{2,3},{3,2},{4,5},{5,4},{6,7},{7,6},{8,9},{9,8},{10,11... | collective-permute-start | bytes 12296 | tf_op jit(solution)/shard_map/ppermute | solution.py:428
  15.4 6.4 %collective-permute-start.8 = (f32[256,256]{1,0:T(8,128)S(1)}, f32[256,256]{1,0:T(8,128)S(1)}, u32[]{:S(2)}, u32[]{:S(2)}) collective-permute-start(f32[256,256]{1,0:T(8,128)S(1)} %collective-permute-done.1.x_ref), channel_id=1, source_target_pairs={{0,1},{1,0},{2,3},{3,2},{4,5},{5,4},{6,7},{7,6},{8,9},{9,8},{10,11... | collective-permute-start | bytes 786440 | tf_op jit(solution)/shard_map/ppermute | solution.py:428
  17.7 6.7 %collective-permute-start.5 = (f32[16,128]{1,0:T(8,128)S(1)}, f32[16,128]{1,0:T(8,128)S(1)}, u32[]{:S(2)}, u32[]{:S(2)}) collective-permute-start(f32[16,128]{1,0:T(8,128)S(1)} %get-tuple-element.56.refs_0_.own_facts), channel_id=1, source_target_pairs={{0,24},{4,28},{8,16},{12,20},{16,8},{20,12},{24,0},{28,4},{1,25},{... | collective-permute-start | bytes 24584 | tf_op jit(solution)/shard_map/ppermute | solution.py:428
  20.5 3.9 %collective-permute-start.4 = (f32[16,128]{1,0:T(8,128)S(1)}, f32[16,128]{1,0:T(8,128)S(1)}, u32[]{:S(2)}, u32[]{:S(2)}) collective-permute-start(f32[16,128]{1,0:T(8,128)S(1)} %get-tuple-element.56.refs_0_.own_facts), channel_id=1, source_target_pairs={{0,8},{4,12},{8,0},{12,4},{16,24},{20,28},{24,16},{28,20},{1,9},{5... | collective-permute-start | bytes 24584 | tf_op jit(solution)/shard_map/ppermute | solution.py:428
  21.7 3.7 %collective-permute-start.3 = (f32[16,128]{1,0:T(8,128)S(1)}, f32[16,128]{1,0:T(8,128)S(1)}, u32[]{:S(2)}, u32[]{:S(2)}) collective-permute-start(f32[16,128]{1,0:T(8,128)S(1)} %get-tuple-element.56.refs_0_.own_facts), channel_id=1, source_target_pairs={{0,16},{4,20},{8,24},{12,28},{16,0},{20,4},{24,8},{28,12},{1,17},{... | collective-permute-start | bytes 24584 | tf_op jit(solution)/shard_map/ppermute | solution.py:428
  28.8 2.0 %collective-permute-start.9 = (f32[496,256]{1,0:T(8,128)S(1)}, f32[496,256]{1,0:T(8,128)S(1)}, u32[]{:S(2)}, u32[]{:S(2)}) collective-permute-start(f32[496,256]{1,0:T(8,128)S(1)} %get-tuple-element.63.mine_ref), channel_id=1, source_target_pairs={{0,4},{4,0},{8,12},{12,8},{16,20},{20,16},{24,28},{28,24},{1,5},{5... | collective-permute-start | bytes 1523720 | tf_op jit(solution)/shard_map/ppermute | solution.py:428

commit v7 on v6

--- a/solution.py
+++ b/solution.py
@@ -13,6 +13,7 @@
 TAPS = 15
 REACH = 3
 PAD = 8
+EARLY = 0
 OUTSIDE = np.float32(1024.0)
 BY_LAST = (((1,), (1,)), ((), ()))
 
@@ -255,21 +256,20 @@
         add_terms(at, slopes, own_ref.at[p], other_ref.at[p], slice_e, fresh=True)
 
 
-def facts_kernel(n_keep, base, *refs):
-    facts_ref, pred_ref = refs[-2:]
-    posts = pred_ref.shape[0]
+def facts_kernel(posts, n_keep, base, *refs):
+    facts_ref = refs[-1]
     facts_ref[...] = base[...]
-    total = tree_sum([part[...] for part in refs[: len(refs) - 2 - n_keep]])
+    total = tree_sum([part[...] for part in refs[: len(refs) - 1 - n_keep]])
     for p in range(posts):
         value = total[p : p + 1, :] + base[p : p + 1, :]
-        pred_ref[pl.ds(p, 1)] = value[0, 0:1]
         facts_ref[p : p + 1, :] = value - base[4 * posts + p : 4 * posts + p + 1, :]
-
-
-def far_kernel(n_keep, slice_e, d_ref, x_ref, w_ref, head_ref, *refs):
+        facts_ref[5 * posts + p : 5 * posts + p + 1, :] = value
+
+
+def one_kernel(n_keep, slice_e, d_ref, x_ref, w_ref, head_ref, *refs):
     feat_ref, own_ref, other_ref, xpads, counts, cols = refs[n_keep:]
     head = head_ref[...].astype(jnp.float32)
-    load_post(x_ref[...], xpads.at[0], counts.at[0])
+    load_post(x_ref[0], xpads.at[0], counts.at[0])
     make_cols(xpads.at[0], cols.at[0])
     slopes = []
     for index in range(3):
@@ -280,9 +280,9 @@
     add_terms(at, slopes, own_ref.at[0], other_ref.at[0], slice_e, fresh=True)
 
 
-def made_residuals(here, posts, own, far):
+def made_residuals(here, posts, own, far, near):
     rows = [own[p : p + 1, 0:1] for p in range(posts)]
-    return rows + [far[pl.ds(here, 1), 0:1], far[pl.ds(1 - here, 1), 0:1]]
+    return rows + [far[pl.ds(here, 1), 0:1], far[pl.ds(1 - here, 1), 0:1], near[0:1, 0:1]]
 
 
 def scaled_sum(residuals, terms):
@@ -296,28 +296,31 @@
 
 def last_kernel(sizes, slice_e, d_ref, z_ref, *refs):
     facts, near = refs[:4], refs[4:6]
-    (feat_own, *feat_far), terms = refs[6:9], refs[9:12]
-    w_ref, head_ref, acc_own, acc_other, xpads, counts, cols = refs[12:]
+    (feat_own, *feat_far, feat_near), terms = refs[6:10], refs[10:14]
+    w_ref, head_ref, acc_own, acc_other, xpads, counts, cols = refs[14:]
     posts = near[0].shape[0]
     n_rows, filters = acc_own.shape
     head = head_ref[...].astype(jnp.float32)
     here = z_ref[0]
-    pieces = [x[p] for x in near for p in range(posts)]
-    residuals = [fact[p : p + 1, 0:1] for fact in facts[1:3] for p in range(posts)]
+    left = [(k, p) for k in range(2) for p in range(posts) if (k, p) != (EARLY, 0)]
+    pieces = [near[k][p] for k, p in left]
+    residuals = [facts[1 + k][p : p + 1, 0:1] for k, p in left]
     for p, piece in enumerate(pieces):
         load_post(piece, xpads.at[p], counts.at[p])
         make_cols(xpads.at[p], cols.at[p])
     acc_own[...] = jnp.zeros_like(acc_own)
-    acc_other[0:n_rows, :] = scaled_sum(made_residuals(here, posts, facts[0], facts[3]), terms)
+    acc_other[0:n_rows, :] = scaled_sum(
+        made_residuals(here, posts, facts[0], facts[3], facts[1 + EARLY]), terms
+    )
     slopes = [[], [], []]
-    feat_last = []
+    feat_last = {}
     for p, residual in enumerate(residuals):
         features = []
         for index in range(3):
             feature, share = forward(index, cols.at[p], w_ref, head, counts.at[p])
             features.append(feature)
             slopes[index].append((residual * share).astype(jnp.bfloat16))
-        feat_last.append(jnp.concatenate(features, axis=0))
+        feat_last[left[p]] = jnp.concatenate(features, axis=0)
     at = jnp.concatenate(
         [pick_rows(d_ref, middle_of(cols.at[p]), slice_e) for p in range(len(pieces))], axis=1
     )
@@ -342,8 +345,7 @@
 
     features = [
         [feat_own[p] for p in range(posts)],
-        feat_last[:posts],
-        feat_last[posts:],
+        *[[feat_last.get((k, p), feat_near[0:3, :]) for p in range(posts)] for k in range(2)],
         [
             jnp.where(here == p, feat_far[0][0:3, :], feat_far[1][0:3, :])
             for p in range(posts)
@@ -355,9 +357,13 @@
     acc_other[n_rows + 3 : n_rows + 3 + n_codes, :] = tree_sum([total[1] for total in sums])
 
 
-def gather_kernel(z_ref, acc, own_facts, far_facts, *refs):
-    made = made_residuals(z_ref[0], refs[0].shape[0], own_facts, far_facts)
-    refs[-1][...] = acc[...] + scaled_sum(made, refs[:-1])
+def gather_kernel(z_ref, acc, own_facts, far_facts, near_facts, *refs):
+    *terms, total_ref, pred_ref = refs
+    posts = pred_ref.shape[0]
+    for p in range(posts):
+        pred_ref[pl.ds(p, 1)] = own_facts[5 * posts + p, 0:1]
+    made = made_residuals(z_ref[0], posts, own_facts, far_facts, near_facts)
+    total_ref[...] = acc[...] + scaled_sum(made, terms)
 
 
 def tree_sum(values):
@@ -450,7 +456,7 @@
         return run
 
     acc_shape = (TAPS * slice_e, filters)
-    n_facts = -(-5 * posts // 8) * 8
+    n_facts = -(-6 * posts // 8) * 8
     weights = jnp.transpose(conv_weight, (1, 0, 2)).reshape(TAPS * dims, filters)
     half = (lax.axis_index("filt").astype(i32) & 1).reshape(1)
     pieces, far_piece = call(
@@ -498,9 +504,9 @@
         pieces,
     )
 
-    def far_terms_of(x, keep, cost=1):
+    def terms_of(x, keep, cost=1):
         feat, *terms = call(
-            functools.partial(far_kernel, len(keep), slice_e),
+            functools.partial(one_kernel, len(keep), slice_e),
             [smem] + [vmem] * 3 + [anywhere] * len(keep),
             [(8, filters)] + [(1,) + acc_shape] * 2,
             posts_scratch(1),
@@ -520,24 +526,26 @@
         k //= 2
     parts = [part, swap(part, 1, "filt")]
     far_two = swap(far_one, 1, "filt")
-    far_feat, far_terms = far_terms_of(far_one, (), 4000000000)
+    far_feat, far_terms = terms_of(far_one[None], (), 4000000000)
     parts, far_feat, far_terms = lax.optimization_barrier((parts, far_feat, far_terms))
     keep = [*own_terms, *far_terms]
-    facts, prediction = call(
-        functools.partial(facts_kernel, len(keep)),
+    (facts,) = call(
+        functools.partial(facts_kernel, posts, len(keep)),
         [vmem] * (1 + len(parts)) + [anywhere] * len(keep),
-        [(n_facts, 128), (posts,)],
+        [(n_facts, 128)],
     )(base, *parts, *keep)
 
     all_facts = [facts] + [swap(facts, k) for k in near] + [swap(facts, far)]
-    far_feat_two, far_terms_two = far_terms_of(far_two, keep)
-    terms = list(zip(own_terms, far_terms, far_terms_two))
+    far_feat_two, far_terms_two = terms_of(far_two[None], keep)
+    keep += far_terms_two
+    near_feat, near_terms = terms_of(near_pieces[0], keep)
+    terms = list(zip(own_terms, far_terms, far_terms_two, near_terms))
     extra = -(-(3 + code_rows(sizes, filters)) // 8) * 8
     acc_own, acc_other = call(
         functools.partial(last_kernel, sizes, slice_e),
-        [smem] * 2 + [vmem] * 14,
+        [smem] * 2 + [vmem] * 16,
         [acc_shape, (acc_shape[0] + extra, filters)],
-        posts_scratch(2 * posts),
+        posts_scratch(2 * posts - 1),
     )(
         me,
         half,
@@ -546,14 +554,15 @@
         feat_own,
         far_feat,
         far_feat_two,
+        near_feat,
         *terms[1],
         weights,
         head_weight,
     )
 
     came = swap(acc_other, 1)
-    (total,) = call(gather_kernel, [smem] + [vmem] * 6, [acc_shape])(
-        half, acc_own, all_facts[0], all_facts[3], *terms[0]
+    total, prediction = call(gather_kernel, [smem] + [vmem] * 8, [acc_shape, (posts,)])(
+        half, acc_own, all_facts[0], all_facts[3], all_facts[1 + EARLY], *terms[0]
     )
     grad, head_grad, *codes = call(
         functools.partial(swap_kernel, sizes),

time: 31.8 us -> 31.2 us (0.981)
  waiting for transfers between devices: 4.36 us -> 3.66 us
    ppermute x10, waiting for transfers between devices: 4.36 us -> 3.66 us  [swap(): return lax.ppermute(x, axis, [(i, i ^ k) for i in range(size)])]
    pallas_call x9 -> x10, Pallas kernels: 11.9 us -> 12 us  [run(): return built(*operands)]
  transfers between devices with their start and end apart: 10 -> 10, of which waited for: 5 -> 4; matrix products, arithmetic and copies ran while one was open for 0% -> 0% of each run, Pallas kernels for 20% -> 24%
where the time goes in v7:
time: 31.2 us; the launch traced here: 31 us
  starting transfers between devices  14.6 us (47%)
  Pallas kernels  12 us (38%)
  waiting for transfers between devices  3.66 us (12%)
  between operations  0.74 us (2%)
    ppermute x10, starting transfers between devices, swap(): return lax.ppermute(x, axis, [(i, i ^ k) for i in range(size)])  14.6 us
    pallas_call x10, Pallas kernels, run(): return built(*operands)  12 us
    ppermute x10, waiting for transfers between devices, swap(): return lax.ppermute(x, axis, [(i, i ^ k) for i in range(size)])  3.66 us
  transfers between devices with their start and end apart: 10, of which 4 were waited for; matrix products, arithmetic and copies ran while one was open for 0% of the time, Pallas kernels for 24%

profile of v7, /device:TPU:0, one launch (start us, length us, event | category | flops | bytes accessed | tf_op | source)
XLA Modules:
  0.0 31.0 jit_solution(13310376257593631486)
XLA Ops:
  0.6 1.2 %shard_map.154 = (f32[2,256,256]{2,1,0:T(8,128)S(1)}, f32[256,256]{1,0:T(8,128)S(1)}) custom-call(s32[1]{0:T(128)} %bitcast.1.d_ref, s32[1]{0:T(128)} %bitcast.z_ref, s32[2]{0:T(128)} %len_any.1, bf16[2,256,256]{2,1,0:T(8,128)(2,1)} %x_any.1), custom_call_target="tpu_custom_call" | custom-call | flops 10000000000 | bytes 1 | tf_op jit(solution)/shard_map/pallas_call | solution.py:443
  1.8 4.0 %collective-permute-start.1 = (f32[256,256]{1,0:T(8,128)S(1)}, f32[256,256]{1,0:T(8,128)S(1)}, u32[]{:S(2)}, u32[]{:S(2)}) collective-permute-start(f32[256,256]{1,0:T(8,128)S(1)} %get-tuple-element.44), channel_id=1, source_target_pairs={{0,24},{4,28},{8,16},{12,20},{16,8},{20,12},{24,0},{28,4},{1,25},{... | collective-permute-start | bytes 786440 | tf_op jit(solution)/shard_map/ppermute | solution.py:434
  5.8 0.5 %collective-permute-start.6 = (f32[2,256,256]{2,1,0:T(8,128)S(1)}, f32[2,256,256]{2,1,0:T(8,128)S(1)}, u32[]{:S(2)}, u32[]{:S(2)}) collective-permute-start(f32[2,256,256]{2,1,0:T(8,128)S(1)} %get-tuple-element.41.refs_9_.pieces), channel_id=1, source_target_pairs={{0,16},{4,20},{8,24},{12,28},{16,0},{20,4},{24,8},{28,12},{1,17},{... | collective-permute-start | bytes 1572872 | tf_op jit(solution)/shard_map/ppermute | solution.py:434
  6.3 0.1 collective-permute-start.7
  6.5 2.3 %shard_map.155 = (f32[8,128]{1,0:T(8,128)S(1)}, f32[2,3,256]{2,1,0:T(4,128)S(1)}, f32[2,3,256,256]{3,2,1,0:T(8,128)S(1)}, f32[16,128]{1,0:T(8,128)S(1)}) custom-call(s32[2]{0:T(128)} %refs_0_.1, s32[2]{0:T(128)} %refs_1_.1, s32[2]{0:T(128)} %refs_2_.1, f32[2]{0:T(128)} %refs_3_.1, f32[840]{0:T(1024)} %refs_4_.1, f32[40]{0:T(128)} %refs_5_.1, f32[8]{0:T(128)} %refs_6_.1, ...), custom_call_target="tpu_custom_call" | custom-call | flops 1 | bytes 1 | tf_op jit(solution)/shard_map/pallas_call | solution.py:443
  8.8 3.1 %collective-permute-start = (f32[8,128]{1,0:T(8,128)S(1)}, f32[8,128]{1,0:T(8,128)S(1)}, u32[]{:S(2)}, u32[]{:S(2)}) collective-permute-start(f32[8,128]{1,0:T(8,128)S(1)} %get-tuple-element.43), channel_id=1, source_target_pairs={{0,2},{1,3},{2,0},{3,1},{4,6},{5,7},{6,4},{7,5},{8,10},{9,11},{10,... | collective-permute-start | bytes 12296 | tf_op jit(solution)/shard_map/ppermute | solution.py:434
  11.9 0.9 %shard_map.156 = (f32[2,480,256]{2,1,0:T(8,128)S(1)}, f32[2,480,256]{2,1,0:T(8,128)S(1)}) custom-call(s32[1]{0:T(128)} %bitcast.1.d_ref, f32[2,256,256]{2,1,0:T(8,128)S(1)} %get-tuple-element.41.refs_9_.pieces, f32[2,3,256,256]{3,2,1,0:T(8,128)S(1)} %get-tuple-element.45.share_ref), custom_call_target="tpu_custom_call" | custom-call | flops 1 | bytes 1 | tf_op jit(solution)/shard_map/pallas_call | solution.py:443
  12.7 0.7 %collective-permute-done = f32[8,128]{1,0:T(8,128)S(1)} collective-permute-done((f32[8,128]{1,0:T(8,128)S(1)}, f32[8,128]{1,0:T(8,128)S(1)}, u32[]{:S(2)}, u32[]{:S(2)}) %collective-permute-start) | collective-permute-done | bytes 4128 | tf_op jit(solution)/shard_map/ppermute | solution.py:434
  13.5 1.9 %collective-permute-start.2 = (f32[8,128]{1,0:T(8,128)S(1)}, f32[8,128]{1,0:T(8,128)S(1)}, u32[]{:S(2)}, u32[]{:S(2)}) collective-permute-start(f32[8,128]{1,0:T(8,128)S(1)} %add.3.refs_0_), channel_id=1, source_target_pairs={{0,1},{1,0},{2,3},{3,2},{4,5},{5,4},{6,7},{7,6},{8,9},{9,8},{10,11... | collective-permute-start | bytes 12296 | tf_op jit(solution)/shard_map/ppermute | solution.py:434
  15.4 0.1 collective-permute-start.8
  15.5 1.2 %shard_map.157 = (f32[8,256]{1,0:T(8,128)S(1)}, f32[1,480,256]{2,1,0:T(8,128)S(1)}, f32[1,480,256]{2,1,0:T(8,128)S(1)}) custom-call(s32[1]{0:T(128)} %bitcast.1.d_ref, f32[1,256,256]{2,1,0:T(8,128)S(1)} %bitcast.16, bf16[3840,256]{1,0:T(8,128)(2,1)S(1)} %bitcast.11, bf16[3,256]{1,0:T(4,128)(2,1)S(1)} %copy-done.1), custom_call_target="tpu_custom_call" | custom-call | flops 4000000000 | bytes 1 | tf_op jit(solution)/shard_map/pallas_call | solution.py:443
  16.7 0.5 %collective-permute-done.2.refs_1_ = f32[8,128]{1,0:T(8,128)S(1)} collective-permute-done((f32[8,128]{1,0:T(8,128)S(1)}, f32[8,128]{1,0:T(8,128)S(1)}, u32[]{:S(2)}, u32[]{:S(2)}) %collective-permute-start.2) | collective-permute-done | bytes 4128 | tf_op jit(solution)/shard_map/ppermute | solution.py:434
  17.1 2.8 %collective-permute-start.5 = (f32[16,128]{1,0:T(8,128)S(1)}, f32[16,128]{1,0:T(8,128)S(1)}, u32[]{:S(2)}, u32[]{:S(2)}) collective-permute-start(f32[16,128]{1,0:T(8,128)S(1)} %shard_map.158.refs_0_.own_facts), channel_id=1, source_target_pairs={{0,24},{4,28},{8,16},{12,20},{16,8},{20,12},{24,0},{28,4},{1,25},{... | collective-permute-start | bytes 24584 | tf_op jit(solution)/shard_map/ppermute | solution.py:434
  20.0 0.5 %collective-permute-start.4 = (f32[16,128]{1,0:T(8,128)S(1)}, f32[16,128]{1,0:T(8,128)S(1)}, u32[]{:S(2)}, u32[]{:S(2)}) collective-permute-start(f32[16,128]{1,0:T(8,128)S(1)} %shard_map.158.refs_0_.own_facts), channel_id=1, source_target_pairs={{0,8},{4,12},{8,0},{12,4},{16,24},{20,28},{24,16},{28,20},{1,9},{5... | collective-permute-start | bytes 24584 | tf_op jit(solution)/shard_map/ppermute | solution.py:434
  20.5 1.2 %collective-permute-done.8 = f32[256,256]{1,0:T(8,128)S(1)} collective-permute-done((f32[256,256]{1,0:T(8,128)S(1)}, f32[256,256]{1,0:T(8,128)S(1)}, u32[]{:S(2)}, u32[]{:S(2)}) %collective-permute-start.8) | collective-permute-done | bytes 262176 | tf_op jit(solution)/shard_map/ppermute | solution.py:434
  21.7 1.5 %collective-permute-start.3 = (f32[16,128]{1,0:T(8,128)S(1)}, f32[16,128]{1,0:T(8,128)S(1)}, u32[]{:S(2)}, u32[]{:S(2)}) collective-permute-start(f32[16,128]{1,0:T(8,128)S(1)} %shard_map.158.refs_0_.own_facts), channel_id=1, source_target_pairs={{0,16},{4,20},{8,24},{12,28},{16,0},{20,4},{24,8},{28,12},{1,17},{... | collective-permute-start | bytes 24584 | tf_op jit(solution)/shard_map/ppermute | solution.py:434
  23.3 1.2 %shard_map.159 = (f32[8,256]{1,0:T(8,128)S(1)}, f32[1,480,256]{2,1,0:T(8,128)S(1)}, f32[1,480,256]{2,1,0:T(8,128)S(1)}) custom-call(s32[1]{0:T(128)} %bitcast.1.d_ref, f32[1,256,256]{2,1,0:T(8,128)S(1)} %bitcast.15, bf16[3840,256]{1,0:T(8,128)(2,1)S(1)} %bitcast.12, bf16[3,256]{1,0:T(4,128)(2,1)S(1)} %copy-done.1, ...), custom_call_target="tpu_custom_call" | custom-call | flops 1 | bytes 1 | tf_op jit(solution)/shard_map/pallas_call | solution.py:443
  24.4 0.0 collective-permute-done.6.x_ref.refs_4_
  24.4 1.2 %shard_map.160 = (f32[8,256]{1,0:T(8,128)S(1)}, f32[1,480,256]{2,1,0:T(8,128)S(1)}, f32[1,480,256]{2,1,0:T(8,128)S(1)}) custom-call(s32[1]{0:T(128)} %bitcast.1.d_ref, f32[2,256,256]{2,1,0:T(8,128)S(1)} %collective-permute-done.6.x_ref.refs_4_, bf16[3840,256]{1,0:T(8,128)(2,1)S(1)} %bitcast.13, bf16[3,256]{1,0:T(4,128)(2,1)S(1)} %copy-done.1, ...), custom_call_target="tpu_custom_call" | custom-call | flops 1 | bytes 1 | tf_op jit(solution)/shard_map/pallas_call | solution.py:443
  25.7 2.6 %shard_map.161 = (f32[480,256]{1,0:T(8,128)S(1)}, f32[496,256]{1,0:T(8,128)S(1)}) custom-call(s32[1]{0:T(128)} %bitcast.1.d_ref, s32[1]{0:T(128)} %bitcast.z_ref, f32[16,128]{1,0:T(8,128)S(1)} %shard_map.158.refs_0_.own_facts, f32[16,128]{1,0:T(8,128)S(1)} %collective-permute-done.3.refs_1_.near_facts, f32[16,128]{1,0:T(8,128)S(1)} %collective-permute-done.4.refs_2_, ...), custom_call_target="tpu_custom_call" | custom-call | flops 1 | bytes 1 | tf_op jit(solution)/shard_map/pallas_call | solution.py:443
  28.2 0.1 collective-permute-start.9
  28.3 0.7 %shard_map.162 = (f32[480,256]{1,0:T(8,128)S(1)}, f32[2]{0:T(128)}) custom-call(s32[1]{0:T(128)} %bitcast.z_ref, f32[480,256]{1,0:T(8,128)S(1)} %get-tuple-element.66.acc, f32[16,128]{1,0:T(8,128)S(1)} %shard_map.158.refs_0_.own_facts, f32[16,128]{1,0:T(8,128)S(1)} %collective-permute-done.5.refs_3_.far_facts, ...), custom_call_target="tpu_custom_call" | custom-call | flops 1 | bytes 1 | tf_op jit(solution)/shard_map/pallas_call | solution.py:443
  29.0 1.2 %collective-permute-done.9.came_ref = f32[496,256]{1,0:T(8,128)S(1)} collective-permute-done((f32[496,256]{1,0:T(8,128)S(1)}, f32[496,256]{1,0:T(8,128)S(1)}, u32[]{:S(2)}, u32[]{:S(2)}) %collective-permute-start.9) | collective-permute-done | bytes 507936 | tf_op jit(solution)/shard_map/ppermute | solution.py:434
  30.2 0.8 %shard_map.163 = (f32[480,256]{1,0:T(8,128)}, f32[3,256]{1,0:T(4,128)}, f32[840]{0:T(1024)}, f32[40]{0:T(128)}, f32[8]{0:T(128)}) custom-call(f32[480,256]{1,0:T(8,128)S(1)} %get-tuple-element.68.own_ref, f32[496,256]{1,0:T(8,128)S(1)} %get-tuple-element.69.mine_ref, f32[496,256]{1,0:T(8,128)S(1)} %collective-permute-done.9.came_ref), custom_call_target="tpu_custom_call" | custom-call | flops 1 | bytes 1 | tf_op jit(solution)/shard_map/pallas_call | solution.py:443
  (11 shorter events, 0.0 us)
Async XLA Ops:
  0.6 5.8 %copy-start = (bf16[256,15,256]{2,0,1:T(8,128)(2,1)S(1)}, bf16[256,15,256]{2,0,1:T(8,128)(2,1)}, u32[]{:S(2)}) copy-start(bf16[256,15,256]{2,0,1:T(8,128)(2,1)} %param.13) | copy-start | bytes 5898244
  1.8 11.6 %collective-permute-start.1 = (f32[256,256]{1,0:T(8,128)S(1)}, f32[256,256]{1,0:T(8,128)S(1)}, u32[]{:S(2)}, u32[]{:S(2)}) collective-permute-start(f32[256,256]{1,0:T(8,128)S(1)} %get-tuple-element.44), channel_id=1, source_target_pairs={{0,24},{4,28},{8,16},{12,20},{16,8},{20,12},{24,0},{28,4},{1,25},{... | collective-permute-start | bytes 786440 | tf_op jit(solution)/shard_map/ppermute | solution.py:434
  5.8 18.6 %collective-permute-start.6 = (f32[2,256,256]{2,1,0:T(8,128)S(1)}, f32[2,256,256]{2,1,0:T(8,128)S(1)}, u32[]{:S(2)}, u32[]{:S(2)}) collective-permute-start(f32[2,256,256]{2,1,0:T(8,128)S(1)} %get-tuple-element.41.refs_9_.pieces), channel_id=1, source_target_pairs={{0,16},{4,20},{8,24},{12,28},{16,0},{20,4},{24,8},{28,12},{1,17},{... | collective-permute-start | bytes 1572872 | tf_op jit(solution)/shard_map/ppermute | solution.py:434
  6.3 19.3 %collective-permute-start.7 = (f32[2,256,256]{2,1,0:T(8,128)S(1)}, f32[2,256,256]{2,1,0:T(8,128)S(1)}, u32[]{:S(2)}, u32[]{:S(2)}) collective-permute-start(f32[2,256,256]{2,1,0:T(8,128)S(1)} %get-tuple-element.41.refs_9_.pieces), channel_id=1, source_target_pairs={{0,8},{4,12},{8,0},{12,4},{16,24},{20,28},{24,16},{28,20},{1,9},{5... | collective-permute-start | bytes 1572872 | tf_op jit(solution)/shard_map/ppermute | solution.py:434
  6.5 9.0 %copy-start.1 = (bf16[3,256]{1,0:T(4,128)(2,1)S(1)}, bf16[3,256]{1,0:T(4,128)(2,1)}, u32[]{:S(2)}) copy-start(bf16[3,256]{1,0:T(4,128)(2,1)} %refs_15_.1) | copy-start | bytes 4612
  8.8 4.6 %collective-permute-start = (f32[8,128]{1,0:T(8,128)S(1)}, f32[8,128]{1,0:T(8,128)S(1)}, u32[]{:S(2)}, u32[]{:S(2)}) collective-permute-start(f32[8,128]{1,0:T(8,128)S(1)} %get-tuple-element.43), channel_id=1, source_target_pairs={{0,2},{1,3},{2,0},{3,1},{4,6},{5,7},{6,4},{7,5},{8,10},{9,11},{10,... | collective-permute-start | bytes 12296 | tf_op jit(solution)/shard_map/ppermute | solution.py:434
  13.5 3.7 %collective-permute-start.2 = (f32[8,128]{1,0:T(8,128)S(1)}, f32[8,128]{1,0:T(8,128)S(1)}, u32[]{:S(2)}, u32[]{:S(2)}) collective-permute-start(f32[8,128]{1,0:T(8,128)S(1)} %add.3.refs_0_), channel_id=1, source_target_pairs={{0,1},{1,0},{2,3},{3,2},{4,5},{5,4},{6,7},{7,6},{8,9},{9,8},{10,11... | collective-permute-start | bytes 12296 | tf_op jit(solution)/shard_map/ppermute | solution.py:434
  15.4 6.4 %collective-permute-start.8 = (f32[256,256]{1,0:T(8,128)S(1)}, f32[256,256]{1,0:T(8,128)S(1)}, u32[]{:S(2)}, u32[]{:S(2)}) collective-permute-start(f32[256,256]{1,0:T(8,128)S(1)} %collective-permute-done.1), channel_id=1, source_target_pairs={{0,1},{1,0},{2,3},{3,2},{4,5},{5,4},{6,7},{7,6},{8,9},{9,8},{10,11... | collective-permute-start | bytes 786440 | tf_op jit(solution)/shard_map/ppermute | solution.py:434
  17.1 8.5 %collective-permute-start.5 = (f32[16,128]{1,0:T(8,128)S(1)}, f32[16,128]{1,0:T(8,128)S(1)}, u32[]{:S(2)}, u32[]{:S(2)}) collective-permute-start(f32[16,128]{1,0:T(8,128)S(1)} %shard_map.158.refs_0_.own_facts), channel_id=1, source_target_pairs={{0,24},{4,28},{8,16},{12,20},{16,8},{20,12},{24,0},{28,4},{1,25},{... | collective-permute-start | bytes 24584 | tf_op jit(solution)/shard_map/ppermute | solution.py:434
  20.0 5.7 %collective-permute-start.4 = (f32[16,128]{1,0:T(8,128)S(1)}, f32[16,128]{1,0:T(8,128)S(1)}, u32[]{:S(2)}, u32[]{:S(2)}) collective-permute-start(f32[16,128]{1,0:T(8,128)S(1)} %shard_map.158.refs_0_.own_facts), channel_id=1, source_target_pairs={{0,8},{4,12},{8,0},{12,4},{16,24},{20,28},{24,16},{28,20},{1,9},{5... | collective-permute-start | bytes 24584 | tf_op jit(solution)/shard_map/ppermute | solution.py:434
  21.7 3.9 %collective-permute-start.3 = (f32[16,128]{1,0:T(8,128)S(1)}, f32[16,128]{1,0:T(8,128)S(1)}, u32[]{:S(2)}, u32[]{:S(2)}) collective-permute-start(f32[16,128]{1,0:T(8,128)S(1)} %shard_map.158.refs_0_.own_facts), channel_id=1, source_target_pairs={{0,16},{4,20},{8,24},{12,28},{16,0},{20,4},{24,8},{28,12},{1,17},{... | collective-permute-start | bytes 24584 | tf_op jit(solution)/shard_map/ppermute | solution.py:434
  28.2 2.0 %collective-permute-start.9 = (f32[496,256]{1,0:T(8,128)S(1)}, f32[496,256]{1,0:T(8,128)S(1)}, u32[]{:S(2)}, u32[]{:S(2)}) collective-permute-start(f32[496,256]{1,0:T(8,128)S(1)} %get-tuple-element.69.mine_ref), channel_id=1, source_target_pairs={{0,4},{4,0},{8,12},{12,8},{16,20},{20,16},{24,28},{28,24},{1,5},{5... | collective-permute-start | bytes 1523720 | tf_op jit(solution)/shard_map/ppermute | solution.py:434

commit v8 on v7

--- a/solution.py
+++ b/solution.py
@@ -177,7 +177,7 @@
 
 def add_terms(at, slopes, acc_own, acc_other, slice_e, fresh=False):
     step = 2 * slice_e
-    for index, (taps, first) in enumerate(WIDTH_LIST):
+    for index, (taps, first) in list(enumerate(WIDTH_LIST))[::-1]:
         half = taps // 2
         term = jnp.dot(
             at[(REACH - half) * step : (REACH + half + 1) * step],
@@ -211,19 +211,18 @@
 
 
 def own_kernel(*refs):
-    small = refs[:8]
-    w_ref, pieces, part_ref, feat_ref, share_ref, base_ref = refs[8:14]
-    held = refs[14:22]
-    xpad, cols, counts, small_sems = refs[22:]
+    small = refs[:7]
+    w_ref, pieces, head_ref, part_ref, feat_ref, share_ref, base_ref = refs[7:14]
+    held = refs[14:21]
+    xpad, cols, counts, small_sems = refs[21:]
     posts = pieces.shape[0]
-    copies = [pltpu.make_async_copy(small[i], held[i], small_sems.at[i]) for i in range(8)]
+    copies = [pltpu.make_async_copy(small[i], held[i], small_sems.at[i]) for i in range(7)]
     for copy in copies:
         copy.start()
     for p in range(posts):
         load_post(pieces[p], xpad.at[p], counts.at[p])
         make_cols(xpad.at[p], cols.at[p])
-    copies[7].wait()
-    head = held[7][...].astype(jnp.float32)
+    head = head_ref[...].astype(jnp.float32)
     parts = [jnp.zeros((1, head.shape[1]), jnp.float32) for _ in range(posts)]
     for index in (2, 1, 0):
         for p in range(posts):
@@ -236,9 +235,9 @@
     for p in range(posts):
         total = jnp.sum(parts[p], axis=1, keepdims=True)
         part_ref[p : p + 1, :] = jnp.broadcast_to(total, (1, lanes))
-    for copy in copies[:7]:
+    for copy in copies:
         copy.wait()
-    codes, wage_ref, tables = held[:3], held[3], held[4:7]
+    codes, wage_ref, tables = held[:3], held[3], held[4:]
     base_ref[...] = jnp.zeros_like(base_ref)
     for p in range(posts):
         offset = sum(table[code[p]] for code, table in zip(codes, tables))
@@ -271,12 +270,12 @@
     head = head_ref[...].astype(jnp.float32)
     load_post(x_ref[0], xpads.at[0], counts.at[0])
     make_cols(xpads.at[0], cols.at[0])
-    slopes = []
-    for index in range(3):
+    at = pick_rows(d_ref, middle_of(cols.at[0]), slice_e)
+    slopes = [None] * 3
+    for index in (2, 1, 0):
         feature, share = forward(index, cols.at[0], w_ref, head, counts.at[0])
         feat_ref[index : index + 1, :] = feature
-        slopes.append(share.astype(jnp.bfloat16))
-    at = pick_rows(d_ref, middle_of(cols.at[0]), slice_e)
+        slopes[index] = share.astype(jnp.bfloat16)
     add_terms(at, slopes, own_ref.at[0], other_ref.at[0], slice_e, fresh=True)
 
 
@@ -478,7 +477,7 @@
 
     part, feat_own, share_own, base = call(
         own_kernel,
-        [hbm] * 8 + [vmem] * 2,
+        [hbm] * 7 + [vmem] * 3,
         [
             (8, 128),
             (posts, 3, filters),
@@ -488,9 +487,8 @@
         [pltpu.SMEM((posts,), i32)] * 3
         + [pltpu.SMEM((posts,), f32)]
         + [pltpu.SMEM((size,), f32) for size in sizes]
-        + [pltpu.VMEM(head_weight.shape, head_weight.dtype)]
         + [posts_scratch(posts)[i] for i in (0, 2, 1)]
-        + [pltpu.SemaphoreType.DMA((8,))],
+        + [pltpu.SemaphoreType.DMA((7,))],
     )(
         occupation,
         cohort,
@@ -499,9 +497,9 @@
         occ_table,
         cohort_table,
         edu_table,
-        head_weight,
         weights,
         pieces,
+        head_weight,
     )
 
     def terms_of(x, keep, cost=1):
@@ -518,16 +516,17 @@
         functools.partial(own_terms_kernel, slice_e),
         [smem, vmem, vmem],
         [(posts,) + acc_shape] * 2,
+        cost=1,
     )(me, pieces, share_own)
-    k = n_filt // 2
-    while k > 1:
-        part = part + swap(part, k, "filt")
-        part, far_one, own_terms = lax.optimization_barrier((part, far_one, own_terms))
-        k //= 2
-    parts = [part, swap(part, 1, "filt")]
+    parts = [part] + [swap(part, k, "filt") for k in range(2, n_filt)]
+    first_part, far_one = lax.optimization_barrier((part, far_one))
+    parts.insert(1, swap(first_part, 1, "filt"))
+    parts[-1], share_held = lax.optimization_barrier((parts[-1], share_own))
     far_two = swap(far_one, 1, "filt")
     far_feat, far_terms = terms_of(far_one[None], (), 4000000000)
-    parts, far_feat, far_terms = lax.optimization_barrier((parts, far_feat, far_terms))
+    parts, far_feat, far_terms, own_terms = lax.optimization_barrier(
+        (parts, far_feat, far_terms, own_terms)
+    )
     keep = [*own_terms, *far_terms]
     (facts,) = call(
         functools.partial(facts_kernel, posts, len(keep)),

time: 31.2 us -> 30.9 us (level)
  starting transfers between devices: 14.6 us -> 15.5 us
  Pallas kernels: 12 us -> 11.2 us
  waiting for transfers between devices: 3.66 us -> 3.32 us
    ppermute x10 -> x11, starting transfers between devices: 14.6 us -> 15.5 us  [swap(): return lax.ppermute(x, axis, [(i, i ^ k) for i in range(size)])]
    pallas_call x10, Pallas kernels: 12 us -> 11.2 us  [run(): return built(*operands)]
    ppermute x10 -> x11, waiting for transfers between devices: 3.66 us -> 3.32 us  [swap(): return lax.ppermute(x, axis, [(i, i ^ k) for i in range(size)])]
  transfers between devices with their start and end apart: 10 -> 11, of which waited for: 4 -> 4; matrix products, arithmetic and copies ran while one was open for 0% -> 0% of each run, Pallas kernels for 24% -> 21%
where the time goes in v8:
time: 30.9 us; the launch traced here: 30.7 us
  starting transfers between devices  15.5 us (50%)
  Pallas kernels  11.2 us (36%)
  waiting for transfers between devices  3.32 us (11%)
  between operations  0.76 us (2%)
    ppermute x11, starting transfers between devices, swap(): return lax.ppermute(x, axis, [(i, i ^ k) for i in range(size)])  15.5 us
    pallas_call x10, Pallas kernels, run(): return built(*operands)  11.2 us
    ppermute x11, waiting for transfers between devices, swap(): return lax.ppermute(x, axis, [(i, i ^ k) for i in range(size)])  3.32 us
  transfers between devices with their start and end apart: 11, of which 4 were waited for; matrix products, arithmetic and copies ran while one was open for 0% of the time, Pallas kernels for 21%

profile of v8, /device:TPU:0, one launch (start us, length us, event | category | flops | bytes accessed | tf_op | source)
XLA Modules:
  0.0 30.7 jit_solution(16504437585494227171)
XLA Ops:
  0.7 1.2 %shard_map.154 = (f32[2,256,256]{2,1,0:T(8,128)S(1)}, f32[256,256]{1,0:T(8,128)S(1)}) custom-call(s32[1]{0:T(128)} %bitcast.1.d_ref, s32[1]{0:T(128)} %bitcast.z_ref, s32[2]{0:T(128)} %len_any.1, bf16[2,256,256]{2,1,0:T(8,128)(2,1)} %x_any.1), custom_call_target="tpu_custom_call" | custom-call | flops 10000000000 | bytes 1 | tf_op jit(solution)/shard_map/pallas_call | solution.py:442
  1.9 4.0 %collective-permute-start = (f32[256,256]{1,0:T(8,128)S(1)}, f32[256,256]{1,0:T(8,128)S(1)}, u32[]{:S(2)}, u32[]{:S(2)}) collective-permute-start(f32[256,256]{1,0:T(8,128)S(1)} %get-tuple-element.47), channel_id=1, source_target_pairs={{0,24},{4,28},{8,16},{12,20},{16,8},{20,12},{24,0},{28,4},{1,25},{... | collective-permute-start | bytes 786440 | tf_op jit(solution)/shard_map/ppermute | solution.py:433
  5.8 0.5 %collective-permute-start.7 = (f32[2,256,256]{2,1,0:T(8,128)S(1)}, f32[2,256,256]{2,1,0:T(8,128)S(1)}, u32[]{:S(2)}, u32[]{:S(2)}) collective-permute-start(f32[2,256,256]{2,1,0:T(8,128)S(1)} %get-tuple-element.44.refs_8_.pieces), channel_id=1, source_target_pairs={{0,16},{4,20},{8,24},{12,28},{16,0},{20,4},{24,8},{28,12},{1,17},{... | collective-permute-start | bytes 1572872 | tf_op jit(solution)/shard_map/ppermute | solution.py:433
  6.3 0.1 collective-permute-start.8
  6.5 1.6 %shard_map.155 = (f32[8,128]{1,0:T(8,128)S(1)}, f32[2,3,256]{2,1,0:T(4,128)S(1)}, f32[2,3,256,256]{3,2,1,0:T(8,128)S(1)}, f32[16,128]{1,0:T(8,128)S(1)}) custom-call(s32[2]{0:T(128)} %refs_0_.1, s32[2]{0:T(128)} %refs_1_.1, s32[2]{0:T(128)} %refs_2_.1, f32[2]{0:T(128)} %refs_3_.1, f32[840]{0:T(1024)} %refs_4_.1, f32[40]{0:T(128)} %refs_5_.1, f32[8]{0:T(128)} %refs_6_.1, ...), custom_call_target="tpu_custom_call" | custom-call | flops 1 | bytes 1 | tf_op jit(solution)/shard_map/pallas_call | solution.py:442
  8.1 4.1 %collective-permute-start.3 = (f32[8,128]{1,0:T(8,128)S(1)}, f32[8,128]{1,0:T(8,128)S(1)}, u32[]{:S(2)}, u32[]{:S(2)}) collective-permute-start(f32[8,128]{1,0:T(8,128)S(1)} %get-tuple-element.57.refs_0_), channel_id=1, source_target_pairs={{0,3},{1,2},{2,1},{3,0},{4,7},{5,6},{6,5},{7,4},{8,11},{9,10},{10,... | collective-permute-start | bytes 12296 | tf_op jit(solution)/shard_map/ppermute | solution.py:433
  12.2 0.8 %shard_map.157 = (f32[2,480,256]{2,1,0:T(8,128)S(1)}, f32[2,480,256]{2,1,0:T(8,128)S(1)}) custom-call(s32[1]{0:T(128)} %bitcast.1.d_ref, f32[2,256,256]{2,1,0:T(8,128)S(1)} %get-tuple-element.44.refs_8_.pieces, f32[2,3,256,256]{3,2,1,0:T(8,128)S(1)} %get-tuple-element.49.share_ref), custom_call_target="tpu_custom_call" | custom-call | flops 1 | bytes 1 | tf_op jit(solution)/shard_map/pallas_call | solution.py:442
  13.0 0.8 %collective-permute-done.3.refs_3_ = f32[8,128]{1,0:T(8,128)S(1)} collective-permute-done((f32[8,128]{1,0:T(8,128)S(1)}, f32[8,128]{1,0:T(8,128)S(1)}, u32[]{:S(2)}, u32[]{:S(2)}) %collective-permute-start.3) | collective-permute-done | bytes 4128 | tf_op jit(solution)/shard_map/ppermute | solution.py:433
  13.8 0.0 collective-permute-done
  13.8 1.3 %collective-permute-start.1 = (f32[8,128]{1,0:T(8,128)S(1)}, f32[8,128]{1,0:T(8,128)S(1)}, u32[]{:S(2)}, u32[]{:S(2)}) collective-permute-start(f32[8,128]{1,0:T(8,128)S(1)} %get-tuple-element.57.refs_0_), channel_id=1, source_target_pairs={{0,1},{1,0},{2,3},{3,2},{4,5},{5,4},{6,7},{7,6},{8,9},{9,8},{10,11... | collective-permute-start | bytes 12296 | tf_op jit(solution)/shard_map/ppermute | solution.py:433
  15.1 0.7 %collective-permute-start.9 = (f32[256,256]{1,0:T(8,128)S(1)}, f32[256,256]{1,0:T(8,128)S(1)}, u32[]{:S(2)}, u32[]{:S(2)}) collective-permute-start(f32[256,256]{1,0:T(8,128)S(1)} %collective-permute-done), channel_id=1, source_target_pairs={{0,1},{1,0},{2,3},{3,2},{4,5},{5,4},{6,7},{7,6},{8,9},{9,8},{10,11... | collective-permute-start | bytes 786440 | tf_op jit(solution)/shard_map/ppermute | solution.py:433
  15.8 1.1 %shard_map.156 = (f32[8,256]{1,0:T(8,128)S(1)}, f32[1,480,256]{2,1,0:T(8,128)S(1)}, f32[1,480,256]{2,1,0:T(8,128)S(1)}) custom-call(s32[1]{0:T(128)} %bitcast.1.d_ref, f32[1,256,256]{2,1,0:T(8,128)S(1)} %bitcast.16, bf16[3840,256]{1,0:T(8,128)(2,1)S(1)} %bitcast.11, bf16[3,256]{1,0:T(4,128)(2,1)S(1)} %copy-done.1), custom_call_target="tpu_custom_call" | custom-call | flops 4000000000 | bytes 1 | tf_op jit(solution)/shard_map/pallas_call | solution.py:442
  16.9 0.6 %collective-permute-done.1.refs_1_ = f32[8,128]{1,0:T(8,128)S(1)} collective-permute-done((f32[8,128]{1,0:T(8,128)S(1)}, f32[8,128]{1,0:T(8,128)S(1)}, u32[]{:S(2)}, u32[]{:S(2)}) %collective-permute-start.1) | collective-permute-done | bytes 4128 | tf_op jit(solution)/shard_map/ppermute | solution.py:433
  17.5 2.7 %collective-permute-start.6 = (f32[16,128]{1,0:T(8,128)S(1)}, f32[16,128]{1,0:T(8,128)S(1)}, u32[]{:S(2)}, u32[]{:S(2)}) collective-permute-start(f32[16,128]{1,0:T(8,128)S(1)} %shard_map.158.refs_0_.own_facts), channel_id=1, source_target_pairs={{0,24},{4,28},{8,16},{12,20},{16,8},{20,12},{24,0},{28,4},{1,25},{... | collective-permute-start | bytes 24584 | tf_op jit(solution)/shard_map/ppermute | solution.py:433
  20.1 0.5 %collective-permute-start.5 = (f32[16,128]{1,0:T(8,128)S(1)}, f32[16,128]{1,0:T(8,128)S(1)}, u32[]{:S(2)}, u32[]{:S(2)}) collective-permute-start(f32[16,128]{1,0:T(8,128)S(1)} %shard_map.158.refs_0_.own_facts), channel_id=1, source_target_pairs={{0,8},{4,12},{8,0},{12,4},{16,24},{20,28},{24,16},{28,20},{1,9},{5... | collective-permute-start | bytes 24584 | tf_op jit(solution)/shard_map/ppermute | solution.py:433
  20.7 0.8 %collective-permute-done.9 = f32[256,256]{1,0:T(8,128)S(1)} collective-permute-done((f32[256,256]{1,0:T(8,128)S(1)}, f32[256,256]{1,0:T(8,128)S(1)}, u32[]{:S(2)}, u32[]{:S(2)}) %collective-permute-start.9) | collective-permute-done | bytes 262176 | tf_op jit(solution)/shard_map/ppermute | solution.py:433
  21.5 1.5 %collective-permute-start.4 = (f32[16,128]{1,0:T(8,128)S(1)}, f32[16,128]{1,0:T(8,128)S(1)}, u32[]{:S(2)}, u32[]{:S(2)}) collective-permute-start(f32[16,128]{1,0:T(8,128)S(1)} %shard_map.158.refs_0_.own_facts), channel_id=1, source_target_pairs={{0,16},{4,20},{8,24},{12,28},{16,0},{20,4},{24,8},{28,12},{1,17},{... | collective-permute-start | bytes 24584 | tf_op jit(solution)/shard_map/ppermute | solution.py:433
  23.0 1.1 %shard_map.159 = (f32[8,256]{1,0:T(8,128)S(1)}, f32[1,480,256]{2,1,0:T(8,128)S(1)}, f32[1,480,256]{2,1,0:T(8,128)S(1)}) custom-call(s32[1]{0:T(128)} %bitcast.1.d_ref, f32[1,256,256]{2,1,0:T(8,128)S(1)} %bitcast.15, bf16[3840,256]{1,0:T(8,128)(2,1)S(1)} %bitcast.12, bf16[3,256]{1,0:T(4,128)(2,1)S(1)} %copy-done.1, ...), custom_call_target="tpu_custom_call" | custom-call | flops 1 | bytes 1 | tf_op jit(solution)/shard_map/pallas_call | solution.py:442
  24.1 1.1 %shard_map.160 = (f32[8,256]{1,0:T(8,128)S(1)}, f32[1,480,256]{2,1,0:T(8,128)S(1)}, f32[1,480,256]{2,1,0:T(8,128)S(1)}) custom-call(s32[1]{0:T(128)} %bitcast.1.d_ref, f32[2,256,256]{2,1,0:T(8,128)S(1)} %collective-permute-done.7.x_ref.refs_4_, bf16[3840,256]{1,0:T(8,128)(2,1)S(1)} %bitcast.13, bf16[3,256]{1,0:T(4,128)(2,1)S(1)} %copy-done.1, ...), custom_call_target="tpu_custom_call" | custom-call | flops 1 | bytes 1 | tf_op jit(solution)/shard_map/pallas_call | solution.py:442
  25.3 2.7 %shard_map.161 = (f32[480,256]{1,0:T(8,128)S(1)}, f32[496,256]{1,0:T(8,128)S(1)}) custom-call(s32[1]{0:T(128)} %bitcast.1.d_ref, s32[1]{0:T(128)} %bitcast.z_ref, f32[16,128]{1,0:T(8,128)S(1)} %shard_map.158.refs_0_.own_facts, f32[16,128]{1,0:T(8,128)S(1)} %collective-permute-done.4.refs_1_.near_facts, f32[16,128]{1,0:T(8,128)S(1)} %collective-permute-done.5.refs_2_, ...), custom_call_target="tpu_custom_call" | custom-call | flops 1 | bytes 1 | tf_op jit(solution)/shard_map/pallas_call | solution.py:442
  27.9 0.1 collective-permute-start.10
  28.0 0.7 %shard_map.162 = (f32[480,256]{1,0:T(8,128)S(1)}, f32[2]{0:T(128)}) custom-call(s32[1]{0:T(128)} %bitcast.z_ref, f32[480,256]{1,0:T(8,128)S(1)} %get-tuple-element.72.acc, f32[16,128]{1,0:T(8,128)S(1)} %shard_map.158.refs_0_.own_facts, f32[16,128]{1,0:T(8,128)S(1)} %collective-permute-done.6.refs_3_.far_facts, ...), custom_call_target="tpu_custom_call" | custom-call | flops 1 | bytes 1 | tf_op jit(solution)/shard_map/pallas_call | solution.py:442
  28.7 1.2 %collective-permute-done.10.came_ref = f32[496,256]{1,0:T(8,128)S(1)} collective-permute-done((f32[496,256]{1,0:T(8,128)S(1)}, f32[496,256]{1,0:T(8,128)S(1)}, u32[]{:S(2)}, u32[]{:S(2)}) %collective-permute-start.10) | collective-permute-done | bytes 507936 | tf_op jit(solution)/shard_map/ppermute | solution.py:433
  29.9 0.8 %shard_map.163 = (f32[480,256]{1,0:T(8,128)}, f32[3,256]{1,0:T(4,128)}, f32[840]{0:T(1024)}, f32[40]{0:T(128)}, f32[8]{0:T(128)}) custom-call(f32[480,256]{1,0:T(8,128)S(1)} %get-tuple-element.74.own_ref, f32[496,256]{1,0:T(8,128)S(1)} %get-tuple-element.75.mine_ref, f32[496,256]{1,0:T(8,128)S(1)} %collective-permute-done.10.came_ref), custom_call_target="tpu_custom_call" | custom-call | flops 1 | bytes 1 | tf_op jit(solution)/shard_map/pallas_call | solution.py:442
  (12 shorter events, 0.0 us)
Async XLA Ops:
  0.6 5.8 %copy-start = (bf16[256,15,256]{2,0,1:T(8,128)(2,1)S(1)}, bf16[256,15,256]{2,0,1:T(8,128)(2,1)}, u32[]{:S(2)}) copy-start(bf16[256,15,256]{2,0,1:T(8,128)(2,1)} %param.13) | copy-start | bytes 5898244
  0.6 5.8 %copy-start.1 = (bf16[3,256]{1,0:T(4,128)(2,1)S(1)}, bf16[3,256]{1,0:T(4,128)(2,1)}, u32[]{:S(2)}) copy-start(bf16[3,256]{1,0:T(4,128)(2,1)} %refs_15_.1) | copy-start | bytes 4612
  1.9 11.9 %collective-permute-start = (f32[256,256]{1,0:T(8,128)S(1)}, f32[256,256]{1,0:T(8,128)S(1)}, u32[]{:S(2)}, u32[]{:S(2)}) collective-permute-start(f32[256,256]{1,0:T(8,128)S(1)} %get-tuple-element.47), channel_id=1, source_target_pairs={{0,24},{4,28},{8,16},{12,20},{16,8},{20,12},{24,0},{28,4},{1,25},{... | collective-permute-start | bytes 786440 | tf_op jit(solution)/shard_map/ppermute | solution.py:433
  5.8 18.3 %collective-permute-start.7 = (f32[2,256,256]{2,1,0:T(8,128)S(1)}, f32[2,256,256]{2,1,0:T(8,128)S(1)}, u32[]{:S(2)}, u32[]{:S(2)}) collective-permute-start(f32[2,256,256]{2,1,0:T(8,128)S(1)} %get-tuple-element.44.refs_8_.pieces), channel_id=1, source_target_pairs={{0,16},{4,20},{8,24},{12,28},{16,0},{20,4},{24,8},{28,12},{1,17},{... | collective-permute-start | bytes 1572872 | tf_op jit(solution)/shard_map/ppermute | solution.py:433
  6.3 18.9 %collective-permute-start.8 = (f32[2,256,256]{2,1,0:T(8,128)S(1)}, f32[2,256,256]{2,1,0:T(8,128)S(1)}, u32[]{:S(2)}, u32[]{:S(2)}) collective-permute-start(f32[2,256,256]{2,1,0:T(8,128)S(1)} %get-tuple-element.44.refs_8_.pieces), channel_id=1, source_target_pairs={{0,8},{4,12},{8,0},{12,4},{16,24},{20,28},{24,16},{28,20},{1,9},{5... | collective-permute-start | bytes 1572872 | tf_op jit(solution)/shard_map/ppermute | solution.py:433
  8.1 5.7 %collective-permute-start.3 = (f32[8,128]{1,0:T(8,128)S(1)}, f32[8,128]{1,0:T(8,128)S(1)}, u32[]{:S(2)}, u32[]{:S(2)}) collective-permute-start(f32[8,128]{1,0:T(8,128)S(1)} %get-tuple-element.57.refs_0_), channel_id=1, source_target_pairs={{0,3},{1,2},{2,1},{3,0},{4,7},{5,6},{6,5},{7,4},{8,11},{9,10},{10,... | collective-permute-start | bytes 12296 | tf_op jit(solution)/shard_map/ppermute | solution.py:433
  12.2 4.7 %collective-permute-start.2 = (f32[8,128]{1,0:T(8,128)S(1)}, f32[8,128]{1,0:T(8,128)S(1)}, u32[]{:S(2)}, u32[]{:S(2)}) collective-permute-start(f32[8,128]{1,0:T(8,128)S(1)} %get-tuple-element.57.refs_0_), channel_id=1, source_target_pairs={{0,2},{1,3},{2,0},{3,1},{4,6},{5,7},{6,4},{7,5},{8,10},{9,11},{10,... | collective-permute-start | bytes 12296 | tf_op jit(solution)/shard_map/ppermute | solution.py:433
  13.8 3.7 %collective-permute-start.1 = (f32[8,128]{1,0:T(8,128)S(1)}, f32[8,128]{1,0:T(8,128)S(1)}, u32[]{:S(2)}, u32[]{:S(2)}) collective-permute-start(f32[8,128]{1,0:T(8,128)S(1)} %get-tuple-element.57.refs_0_), channel_id=1, source_target_pairs={{0,1},{1,0},{2,3},{3,2},{4,5},{5,4},{6,7},{7,6},{8,9},{9,8},{10,11... | collective-permute-start | bytes 12296 | tf_op jit(solution)/shard_map/ppermute | solution.py:433
  15.1 6.4 %collective-permute-start.9 = (f32[256,256]{1,0:T(8,128)S(1)}, f32[256,256]{1,0:T(8,128)S(1)}, u32[]{:S(2)}, u32[]{:S(2)}) collective-permute-start(f32[256,256]{1,0:T(8,128)S(1)} %collective-permute-done), channel_id=1, source_target_pairs={{0,1},{1,0},{2,3},{3,2},{4,5},{5,4},{6,7},{7,6},{8,9},{9,8},{10,11... | collective-permute-start | bytes 786440 | tf_op jit(solution)/shard_map/ppermute | solution.py:433
  17.5 7.7 %collective-permute-start.6 = (f32[16,128]{1,0:T(8,128)S(1)}, f32[16,128]{1,0:T(8,128)S(1)}, u32[]{:S(2)}, u32[]{:S(2)}) collective-permute-start(f32[16,128]{1,0:T(8,128)S(1)} %shard_map.158.refs_0_.own_facts), channel_id=1, source_target_pairs={{0,24},{4,28},{8,16},{12,20},{16,8},{20,12},{24,0},{28,4},{1,25},{... | collective-permute-start | bytes 24584 | tf_op jit(solution)/shard_map/ppermute | solution.py:433
  20.1 5.1 %collective-permute-start.5 = (f32[16,128]{1,0:T(8,128)S(1)}, f32[16,128]{1,0:T(8,128)S(1)}, u32[]{:S(2)}, u32[]{:S(2)}) collective-permute-start(f32[16,128]{1,0:T(8,128)S(1)} %shard_map.158.refs_0_.own_facts), channel_id=1, source_target_pairs={{0,8},{4,12},{8,0},{12,4},{16,24},{20,28},{24,16},{28,20},{1,9},{5... | collective-permute-start | bytes 24584 | tf_op jit(solution)/shard_map/ppermute | solution.py:433
  21.5 3.8 %collective-permute-start.4 = (f32[16,128]{1,0:T(8,128)S(1)}, f32[16,128]{1,0:T(8,128)S(1)}, u32[]{:S(2)}, u32[]{:S(2)}) collective-permute-start(f32[16,128]{1,0:T(8,128)S(1)} %shard_map.158.refs_0_.own_facts), channel_id=1, source_target_pairs={{0,16},{4,20},{8,24},{12,28},{16,0},{20,4},{24,8},{28,12},{1,17},{... | collective-permute-start | bytes 24584 | tf_op jit(solution)/shard_map/ppermute | solution.py:433
  27.9 2.0 %collective-permute-start.10 = (f32[496,256]{1,0:T(8,128)S(1)}, f32[496,256]{1,0:T(8,128)S(1)}, u32[]{:S(2)}, u32[]{:S(2)}) collective-permute-start(f32[496,256]{1,0:T(8,128)S(1)} %get-tuple-element.75.mine_ref), channel_id=1, source_target_pairs={{0,4},{4,0},{8,12},{12,8},{16,20},{20,16},{24,28},{28,24},{1,5},{5... | collective-permute-start | bytes 1523720 | tf_op jit(solution)/shard_map/ppermute | solution.py:433

commit v9 on v8

--- a/solution.py
+++ b/solution.py
@@ -432,7 +432,6 @@
         size = n_doc if axis == "doc" else n_filt
         return lax.ppermute(x, axis, [(i, i ^ k) for i in range(size)])
 
-
     def call(kernel, specs, out, scratch=(), cost=1):
         def run(*operands):
             operands = [
@@ -467,7 +466,7 @@
             pltpu.SMEM((posts,), i32),
             pltpu.SemaphoreType.DMA((posts + 1,)),
         ],
-        cost=10000000000,
+        cost=10**10,
     )(me, half, lengths, embedded)
 
     near = [k for k in range(2, n_doc, 2) if bin(k).count("1") == 1][::-1]
@@ -512,18 +511,16 @@
         )(me, x, weights, head_weight, *keep)
         return feat, terms
 
+    parts = [part] + [swap(part, k, "filt") for k in range(2, n_filt)]
+    first_part, far_one = lax.optimization_barrier((part, far_one))
+    parts.insert(1, swap(first_part, 1, "filt"))
     own_terms = call(
         functools.partial(own_terms_kernel, slice_e),
         [smem, vmem, vmem],
         [(posts,) + acc_shape] * 2,
-        cost=1,
     )(me, pieces, share_own)
-    parts = [part] + [swap(part, k, "filt") for k in range(2, n_filt)]
-    first_part, far_one = lax.optimization_barrier((part, far_one))
-    parts.insert(1, swap(first_part, 1, "filt"))
-    parts[-1], share_held = lax.optimization_barrier((parts[-1], share_own))
     far_two = swap(far_one, 1, "filt")
-    far_feat, far_terms = terms_of(far_one[None], (), 4000000000)
+    far_feat, far_terms = terms_of(far_one[None], (), 4 * 10**9)
     parts, far_feat, far_terms, own_terms = lax.optimization_barrier(
         (parts, far_feat, far_terms, own_terms)
     )
@@ -574,10 +571,12 @@
 
 def solution(mesh):
     n_doc, n_filt = mesh.shape["doc"], mesh.shape["filt"]
-    if n_doc == 8 and n_filt == 4:
-        local = functools.partial(local_gather, n_doc, n_filt)
-    else:
-        local = local_scatter
+
+    def local(*args):
+        if (n_doc, n_filt, args[0].shape[0]) == (8, 4, 2):
+            return local_gather(n_doc, n_filt, *args)
+        return local_scatter(*args)
+
     return jax.shard_map(
         local,
         mesh=mesh,

time: 30.9 us -> 30.9 us (level)
  transfers between devices with their start and end apart: 11 -> 11, of which waited for: 4 -> 3; matrix products, arithmetic and copies ran while one was open for 0% -> 0% of each run, Pallas kernels for 21% -> 21%
where the time goes in v9:
time: 30.9 us; the launch traced here: 30.7 us
  starting transfers between devices  15.8 us (51%)
  Pallas kernels  11.2 us (36%)
  waiting for transfers between devices  3.06 us (10%)
  between operations  0.75 us (2%)
    ppermute x11, starting transfers between devices, swap(): return lax.ppermute(x, axis, [(i, i ^ k) for i in range(size)])  15.8 us
    pallas_call x10, Pallas kernels, run(): return built(*operands)  11.2 us
    ppermute x11, waiting for transfers between devices, swap(): return lax.ppermute(x, axis, [(i, i ^ k) for i in range(size)])  3.06 us
  transfers between devices with their start and end apart: 11, of which 3 were waited for; matrix products, arithmetic and copies ran while one was open for 0% of the time, Pallas kernels for 21%

profile of v9, /device:TPU:0, one launch (start us, length us, event | category | flops | bytes accessed | tf_op | source)
XLA Modules:
  0.0 30.7 jit_solution(15510919832229017658)
XLA Ops:
  0.7 1.2 %shard_map.154 = (f32[2,256,256]{2,1,0:T(8,128)S(1)}, f32[256,256]{1,0:T(8,128)S(1)}) custom-call(s32[1]{0:T(128)} %bitcast.1.d_ref, s32[1]{0:T(128)} %bitcast.z_ref, s32[2]{0:T(128)} %len_any.1, bf16[2,256,256]{2,1,0:T(8,128)(2,1)} %x_any.1), custom_call_target="tpu_custom_call" | custom-call | flops 10000000000 | bytes 1 | tf_op jit(solution)/shard_map/pallas_call | solution.py:441
  1.9 4.0 %collective-permute-start = (f32[256,256]{1,0:T(8,128)S(1)}, f32[256,256]{1,0:T(8,128)S(1)}, u32[]{:S(2)}, u32[]{:S(2)}) collective-permute-start(f32[256,256]{1,0:T(8,128)S(1)} %get-tuple-element.46), channel_id=1, source_target_pairs={{0,24},{4,28},{8,16},{12,20},{16,8},{20,12},{24,0},{28,4},{1,25},{... | collective-permute-start | bytes 786440 | tf_op jit(solution)/shard_map/ppermute | solution.py:433
  5.8 0.5 %collective-permute-start.7 = (f32[2,256,256]{2,1,0:T(8,128)S(1)}, f32[2,256,256]{2,1,0:T(8,128)S(1)}, u32[]{:S(2)}, u32[]{:S(2)}) collective-permute-start(f32[2,256,256]{2,1,0:T(8,128)S(1)} %get-tuple-element.43.refs_8_.pieces), channel_id=1, source_target_pairs={{0,16},{4,20},{8,24},{12,28},{16,0},{20,4},{24,8},{28,12},{1,17},{... | collective-permute-start | bytes 1572872 | tf_op jit(solution)/shard_map/ppermute | solution.py:433
  6.3 0.1 collective-permute-start.8
  6.5 1.6 %shard_map.155 = (f32[8,128]{1,0:T(8,128)S(1)}, f32[2,3,256]{2,1,0:T(4,128)S(1)}, f32[2,3,256,256]{3,2,1,0:T(8,128)S(1)}, f32[16,128]{1,0:T(8,128)S(1)}) custom-call(s32[2]{0:T(128)} %refs_0_.1, s32[2]{0:T(128)} %refs_1_.1, s32[2]{0:T(128)} %refs_2_.1, f32[2]{0:T(128)} %refs_3_.1, f32[840]{0:T(1024)} %refs_4_.1, f32[40]{0:T(128)} %refs_5_.1, f32[8]{0:T(128)} %refs_6_.1, ...), custom_call_target="tpu_custom_call" | custom-call | flops 1 | bytes 1 | tf_op jit(solution)/shard_map/pallas_call | solution.py:441
  8.1 4.1 %collective-permute-start.3 = (f32[8,128]{1,0:T(8,128)S(1)}, f32[8,128]{1,0:T(8,128)S(1)}, u32[]{:S(2)}, u32[]{:S(2)}) collective-permute-start(f32[8,128]{1,0:T(8,128)S(1)} %get-tuple-element.55.refs_0_), channel_id=1, source_target_pairs={{0,3},{1,2},{2,1},{3,0},{4,7},{5,6},{6,5},{7,4},{8,11},{9,10},{10,... | collective-permute-start | bytes 12296 | tf_op jit(solution)/shard_map/ppermute | solution.py:433
  12.2 0.8 %shard_map.157 = (f32[2,480,256]{2,1,0:T(8,128)S(1)}, f32[2,480,256]{2,1,0:T(8,128)S(1)}) custom-call(s32[1]{0:T(128)} %bitcast.1.d_ref, f32[2,256,256]{2,1,0:T(8,128)S(1)} %get-tuple-element.43.refs_8_.pieces, f32[2,3,256,256]{3,2,1,0:T(8,128)S(1)} %get-tuple-element.52.share_ref), custom_call_target="tpu_custom_call" | custom-call | flops 1 | bytes 1 | tf_op jit(solution)/shard_map/pallas_call | solution.py:441
  13.0 0.0 collective-permute-done
  13.0 2.1 %collective-permute-start.1 = (f32[8,128]{1,0:T(8,128)S(1)}, f32[8,128]{1,0:T(8,128)S(1)}, u32[]{:S(2)}, u32[]{:S(2)}) collective-permute-start(f32[8,128]{1,0:T(8,128)S(1)} %get-tuple-element.55.refs_0_), channel_id=1, source_target_pairs={{0,1},{1,0},{2,3},{3,2},{4,5},{5,4},{6,7},{7,6},{8,9},{9,8},{10,11... | collective-permute-start | bytes 12296 | tf_op jit(solution)/shard_map/ppermute | solution.py:433
  15.1 0.0 collective-permute-start.9
  15.1 1.1 %shard_map.156 = (f32[8,256]{1,0:T(8,128)S(1)}, f32[1,480,256]{2,1,0:T(8,128)S(1)}, f32[1,480,256]{2,1,0:T(8,128)S(1)}) custom-call(s32[1]{0:T(128)} %bitcast.1.d_ref, f32[1,256,256]{2,1,0:T(8,128)S(1)} %bitcast.16, bf16[3840,256]{1,0:T(8,128)(2,1)S(1)} %bitcast.11, bf16[3,256]{1,0:T(4,128)(2,1)S(1)} %copy-done.1), custom_call_target="tpu_custom_call" | custom-call | flops 4000000000 | bytes 1 | tf_op jit(solution)/shard_map/pallas_call | solution.py:441
  16.2 0.5 %collective-permute-done.2.refs_2_ = f32[8,128]{1,0:T(8,128)S(1)} collective-permute-done((f32[8,128]{1,0:T(8,128)S(1)}, f32[8,128]{1,0:T(8,128)S(1)}, u32[]{:S(2)}, u32[]{:S(2)}) %collective-permute-start.2) | collective-permute-done | bytes 4128 | tf_op jit(solution)/shard_map/ppermute | solution.py:433
  16.8 0.0 collective-permute-done.1.refs_1_
  16.8 2.8 %collective-permute-start.6 = (f32[16,128]{1,0:T(8,128)S(1)}, f32[16,128]{1,0:T(8,128)S(1)}, u32[]{:S(2)}, u32[]{:S(2)}) collective-permute-start(f32[16,128]{1,0:T(8,128)S(1)} %shard_map.158.refs_0_.own_facts), channel_id=1, source_target_pairs={{0,24},{4,28},{8,16},{12,20},{16,8},{20,12},{24,0},{28,4},{1,25},{... | collective-permute-start | bytes 24584 | tf_op jit(solution)/shard_map/ppermute | solution.py:433
  19.6 0.6 %collective-permute-start.5 = (f32[16,128]{1,0:T(8,128)S(1)}, f32[16,128]{1,0:T(8,128)S(1)}, u32[]{:S(2)}, u32[]{:S(2)}) collective-permute-start(f32[16,128]{1,0:T(8,128)S(1)} %shard_map.158.refs_0_.own_facts), channel_id=1, source_target_pairs={{0,8},{4,12},{8,0},{12,4},{16,24},{20,28},{24,16},{28,20},{1,9},{5... | collective-permute-start | bytes 24584 | tf_op jit(solution)/shard_map/ppermute | solution.py:433
  20.2 1.2 %collective-permute-done.9 = f32[256,256]{1,0:T(8,128)S(1)} collective-permute-done((f32[256,256]{1,0:T(8,128)S(1)}, f32[256,256]{1,0:T(8,128)S(1)}, u32[]{:S(2)}, u32[]{:S(2)}) %collective-permute-start.9) | collective-permute-done | bytes 262176 | tf_op jit(solution)/shard_map/ppermute | solution.py:433
  21.5 1.5 %collective-permute-start.4 = (f32[16,128]{1,0:T(8,128)S(1)}, f32[16,128]{1,0:T(8,128)S(1)}, u32[]{:S(2)}, u32[]{:S(2)}) collective-permute-start(f32[16,128]{1,0:T(8,128)S(1)} %shard_map.158.refs_0_.own_facts), channel_id=1, source_target_pairs={{0,16},{4,20},{8,24},{12,28},{16,0},{20,4},{24,8},{28,12},{1,17},{... | collective-permute-start | bytes 24584 | tf_op jit(solution)/shard_map/ppermute | solution.py:433
  23.0 1.1 %shard_map.159 = (f32[8,256]{1,0:T(8,128)S(1)}, f32[1,480,256]{2,1,0:T(8,128)S(1)}, f32[1,480,256]{2,1,0:T(8,128)S(1)}) custom-call(s32[1]{0:T(128)} %bitcast.1.d_ref, f32[1,256,256]{2,1,0:T(8,128)S(1)} %bitcast.15, bf16[3840,256]{1,0:T(8,128)(2,1)S(1)} %bitcast.12, bf16[3,256]{1,0:T(4,128)(2,1)S(1)} %copy-done.1, ...), custom_call_target="tpu_custom_call" | custom-call | flops 1 | bytes 1 | tf_op jit(solution)/shard_map/pallas_call | solution.py:441
  24.1 1.1 %shard_map.160 = (f32[8,256]{1,0:T(8,128)S(1)}, f32[1,480,256]{2,1,0:T(8,128)S(1)}, f32[1,480,256]{2,1,0:T(8,128)S(1)}) custom-call(s32[1]{0:T(128)} %bitcast.1.d_ref, f32[2,256,256]{2,1,0:T(8,128)S(1)} %collective-permute-done.7.x_ref.refs_4_, bf16[3840,256]{1,0:T(8,128)(2,1)S(1)} %bitcast.13, bf16[3,256]{1,0:T(4,128)(2,1)S(1)} %copy-done.1, ...), custom_call_target="tpu_custom_call" | custom-call | flops 1 | bytes 1 | tf_op jit(solution)/shard_map/pallas_call | solution.py:441
  25.3 2.7 %shard_map.161 = (f32[480,256]{1,0:T(8,128)S(1)}, f32[496,256]{1,0:T(8,128)S(1)}) custom-call(s32[1]{0:T(128)} %bitcast.1.d_ref, s32[1]{0:T(128)} %bitcast.z_ref, f32[16,128]{1,0:T(8,128)S(1)} %shard_map.158.refs_0_.own_facts, f32[16,128]{1,0:T(8,128)S(1)} %collective-permute-done.4.refs_1_.near_facts, f32[16,128]{1,0:T(8,128)S(1)} %collective-permute-done.5.refs_2_, ...), custom_call_target="tpu_custom_call" | custom-call | flops 1 | bytes 1 | tf_op jit(solution)/shard_map/pallas_call | solution.py:441
  27.9 0.1 collective-permute-start.10
  28.0 0.7 %shard_map.162 = (f32[480,256]{1,0:T(8,128)S(1)}, f32[2]{0:T(128)}) custom-call(s32[1]{0:T(128)} %bitcast.z_ref, f32[480,256]{1,0:T(8,128)S(1)} %get-tuple-element.70.acc, f32[16,128]{1,0:T(8,128)S(1)} %shard_map.158.refs_0_.own_facts, f32[16,128]{1,0:T(8,128)S(1)} %collective-permute-done.6.refs_3_.far_facts, ...), custom_call_target="tpu_custom_call" | custom-call | flops 1 | bytes 1 | tf_op jit(solution)/shard_map/pallas_call | solution.py:441
  28.7 1.2 %collective-permute-done.10.came_ref = f32[496,256]{1,0:T(8,128)S(1)} collective-permute-done((f32[496,256]{1,0:T(8,128)S(1)}, f32[496,256]{1,0:T(8,128)S(1)}, u32[]{:S(2)}, u32[]{:S(2)}) %collective-permute-start.10) | collective-permute-done | bytes 507936 | tf_op jit(solution)/shard_map/ppermute | solution.py:433
  29.9 0.8 %shard_map.163 = (f32[480,256]{1,0:T(8,128)}, f32[3,256]{1,0:T(4,128)}, f32[840]{0:T(1024)}, f32[40]{0:T(128)}, f32[8]{0:T(128)}) custom-call(f32[480,256]{1,0:T(8,128)S(1)} %get-tuple-element.72.own_ref, f32[496,256]{1,0:T(8,128)S(1)} %get-tuple-element.73.mine_ref, f32[496,256]{1,0:T(8,128)S(1)} %collective-permute-done.10.came_ref), custom_call_target="tpu_custom_call" | custom-call | flops 1 | bytes 1 | tf_op jit(solution)/shard_map/pallas_call | solution.py:441
  (12 shorter events, 0.0 us)
Async XLA Ops:
  0.6 5.8 %copy-start = (bf16[256,15,256]{2,0,1:T(8,128)(2,1)S(1)}, bf16[256,15,256]{2,0,1:T(8,128)(2,1)}, u32[]{:S(2)}) copy-start(bf16[256,15,256]{2,0,1:T(8,128)(2,1)} %param.13) | copy-start | bytes 5898244
  0.6 5.8 %copy-start.1 = (bf16[3,256]{1,0:T(4,128)(2,1)S(1)}, bf16[3,256]{1,0:T(4,128)(2,1)}, u32[]{:S(2)}) copy-start(bf16[3,256]{1,0:T(4,128)(2,1)} %refs_15_.1) | copy-start | bytes 4612
  1.9 11.1 %collective-permute-start = (f32[256,256]{1,0:T(8,128)S(1)}, f32[256,256]{1,0:T(8,128)S(1)}, u32[]{:S(2)}, u32[]{:S(2)}) collective-permute-start(f32[256,256]{1,0:T(8,128)S(1)} %get-tuple-element.46), channel_id=1, source_target_pairs={{0,24},{4,28},{8,16},{12,20},{16,8},{20,12},{24,0},{28,4},{1,25},{... | collective-permute-start | bytes 786440 | tf_op jit(solution)/shard_map/ppermute | solution.py:433
  5.8 18.3 %collective-permute-start.7 = (f32[2,256,256]{2,1,0:T(8,128)S(1)}, f32[2,256,256]{2,1,0:T(8,128)S(1)}, u32[]{:S(2)}, u32[]{:S(2)}) collective-permute-start(f32[2,256,256]{2,1,0:T(8,128)S(1)} %get-tuple-element.43.refs_8_.pieces), channel_id=1, source_target_pairs={{0,16},{4,20},{8,24},{12,28},{16,0},{20,4},{24,8},{28,12},{1,17},{... | collective-permute-start | bytes 1572872 | tf_op jit(solution)/shard_map/ppermute | solution.py:433
  6.3 18.9 %collective-permute-start.8 = (f32[2,256,256]{2,1,0:T(8,128)S(1)}, f32[2,256,256]{2,1,0:T(8,128)S(1)}, u32[]{:S(2)}, u32[]{:S(2)}) collective-permute-start(f32[2,256,256]{2,1,0:T(8,128)S(1)} %get-tuple-element.43.refs_8_.pieces), channel_id=1, source_target_pairs={{0,8},{4,12},{8,0},{12,4},{16,24},{20,28},{24,16},{28,20},{1,9},{5... | collective-permute-start | bytes 1572872 | tf_op jit(solution)/shard_map/ppermute | solution.py:433
  8.1 7.0 %collective-permute-start.3 = (f32[8,128]{1,0:T(8,128)S(1)}, f32[8,128]{1,0:T(8,128)S(1)}, u32[]{:S(2)}, u32[]{:S(2)}) collective-permute-start(f32[8,128]{1,0:T(8,128)S(1)} %get-tuple-element.55.refs_0_), channel_id=1, source_target_pairs={{0,3},{1,2},{2,1},{3,0},{4,7},{5,6},{6,5},{7,4},{8,11},{9,10},{10,... | collective-permute-start | bytes 12296 | tf_op jit(solution)/shard_map/ppermute | solution.py:433
  12.2 4.6 %collective-permute-start.2 = (f32[8,128]{1,0:T(8,128)S(1)}, f32[8,128]{1,0:T(8,128)S(1)}, u32[]{:S(2)}, u32[]{:S(2)}) collective-permute-start(f32[8,128]{1,0:T(8,128)S(1)} %get-tuple-element.55.refs_0_), channel_id=1, source_target_pairs={{0,2},{1,3},{2,0},{3,1},{4,6},{5,7},{6,4},{7,5},{8,10},{9,11},{10,... | collective-permute-start | bytes 12296 | tf_op jit(solution)/shard_map/ppermute | solution.py:433
  13.0 3.8 %collective-permute-start.1 = (f32[8,128]{1,0:T(8,128)S(1)}, f32[8,128]{1,0:T(8,128)S(1)}, u32[]{:S(2)}, u32[]{:S(2)}) collective-permute-start(f32[8,128]{1,0:T(8,128)S(1)} %get-tuple-element.55.refs_0_), channel_id=1, source_target_pairs={{0,1},{1,0},{2,3},{3,2},{4,5},{5,4},{6,7},{7,6},{8,9},{9,8},{10,11... | collective-permute-start | bytes 12296 | tf_op jit(solution)/shard_map/ppermute | solution.py:433
  15.1 6.4 %collective-permute-start.9 = (f32[256,256]{1,0:T(8,128)S(1)}, f32[256,256]{1,0:T(8,128)S(1)}, u32[]{:S(2)}, u32[]{:S(2)}) collective-permute-start(f32[256,256]{1,0:T(8,128)S(1)} %collective-permute-done), channel_id=1, source_target_pairs={{0,1},{1,0},{2,3},{3,2},{4,5},{5,4},{6,7},{7,6},{8,9},{9,8},{10,11... | collective-permute-start | bytes 786440 | tf_op jit(solution)/shard_map/ppermute | solution.py:433
  16.8 8.4 %collective-permute-start.6 = (f32[16,128]{1,0:T(8,128)S(1)}, f32[16,128]{1,0:T(8,128)S(1)}, u32[]{:S(2)}, u32[]{:S(2)}) collective-permute-start(f32[16,128]{1,0:T(8,128)S(1)} %shard_map.158.refs_0_.own_facts), channel_id=1, source_target_pairs={{0,24},{4,28},{8,16},{12,20},{16,8},{20,12},{24,0},{28,4},{1,25},{... | collective-permute-start | bytes 24584 | tf_op jit(solution)/shard_map/ppermute | solution.py:433
  19.6 5.6 %collective-permute-start.5 = (f32[16,128]{1,0:T(8,128)S(1)}, f32[16,128]{1,0:T(8,128)S(1)}, u32[]{:S(2)}, u32[]{:S(2)}) collective-permute-start(f32[16,128]{1,0:T(8,128)S(1)} %shard_map.158.refs_0_.own_facts), channel_id=1, source_target_pairs={{0,8},{4,12},{8,0},{12,4},{16,24},{20,28},{24,16},{28,20},{1,9},{5... | collective-permute-start | bytes 24584 | tf_op jit(solution)/shard_map/ppermute | solution.py:433
  21.5 3.8 %collective-permute-start.4 = (f32[16,128]{1,0:T(8,128)S(1)}, f32[16,128]{1,0:T(8,128)S(1)}, u32[]{:S(2)}, u32[]{:S(2)}) collective-permute-start(f32[16,128]{1,0:T(8,128)S(1)} %shard_map.158.refs_0_.own_facts), channel_id=1, source_target_pairs={{0,16},{4,20},{8,24},{12,28},{16,0},{20,4},{24,8},{28,12},{1,17},{... | collective-permute-start | bytes 24584 | tf_op jit(solution)/shard_map/ppermute | solution.py:433
  27.9 2.0 %collective-permute-start.10 = (f32[496,256]{1,0:T(8,128)S(1)}, f32[496,256]{1,0:T(8,128)S(1)}, u32[]{:S(2)}, u32[]{:S(2)}) collective-permute-start(f32[496,256]{1,0:T(8,128)S(1)} %get-tuple-element.73.mine_ref), channel_id=1, source_target_pairs={{0,4},{4,0},{8,12},{12,8},{16,20},{20,16},{24,28},{28,24},{1,5},{5... | collective-permute-start | bytes 1523720 | tf_op jit(solution)/shard_map/ppermute | solution.py:433

commit v10 on v9

--- a/solution.py
+++ b/solution.py
@@ -177,7 +177,8 @@
 
 def add_terms(at, slopes, acc_own, acc_other, slice_e, fresh=False):
     step = 2 * slice_e
-    for index, (taps, first) in list(enumerate(WIDTH_LIST))[::-1]:
+    for index in (2, 1, 0) if fresh else (0, 1, 2):
+        taps, first = WIDTH_LIST[index]
         half = taps // 2
         term = jnp.dot(
             at[(REACH - half) * step : (REACH + half + 1) * step],

time: 30.9 us -> 30.8 us (level)
  no operation moved by 1% of the time
where the time goes in v10:
time: 30.8 us; the launch traced here: 30.6 us
  starting transfers between devices  15.8 us (51%)
  Pallas kernels  11.1 us (36%)
  waiting for transfers between devices  3.06 us (10%)
  between operations  0.75 us (2%)
    ppermute x11, starting transfers between devices, swap(): return lax.ppermute(x, axis, [(i, i ^ k) for i in range(size)])  15.8 us
    pallas_call x10, Pallas kernels, run(): return built(*operands)  11.1 us
    ppermute x11, waiting for transfers between devices, swap(): return lax.ppermute(x, axis, [(i, i ^ k) for i in range(size)])  3.06 us
  transfers between devices with their start and end apart: 11, of which 3 were waited for; matrix products, arithmetic and copies ran while one was open for 0% of the time, Pallas kernels for 21%

profile of v10, /device:TPU:0, one launch (start us, length us, event | category | flops | bytes accessed | tf_op | source)
XLA Modules:
  0.0 30.6 jit_solution(16139733141051496344)
XLA Ops:
  0.7 1.2 %shard_map.154 = (f32[2,256,256]{2,1,0:T(8,128)S(1)}, f32[256,256]{1,0:T(8,128)S(1)}) custom-call(s32[1]{0:T(128)} %bitcast.1.d_ref, s32[1]{0:T(128)} %bitcast.z_ref, s32[2]{0:T(128)} %len_any.1, bf16[2,256,256]{2,1,0:T(8,128)(2,1)} %x_any.1), custom_call_target="tpu_custom_call" | custom-call | flops 10000000000 | bytes 1 | tf_op jit(solution)/shard_map/pallas_call | solution.py:442
  1.9 4.0 %collective-permute-start = (f32[256,256]{1,0:T(8,128)S(1)}, f32[256,256]{1,0:T(8,128)S(1)}, u32[]{:S(2)}, u32[]{:S(2)}) collective-permute-start(f32[256,256]{1,0:T(8,128)S(1)} %get-tuple-element.46), channel_id=1, source_target_pairs={{0,24},{4,28},{8,16},{12,20},{16,8},{20,12},{24,0},{28,4},{1,25},{... | collective-permute-start | bytes 786440 | tf_op jit(solution)/shard_map/ppermute | solution.py:434
  5.8 0.5 %collective-permute-start.7 = (f32[2,256,256]{2,1,0:T(8,128)S(1)}, f32[2,256,256]{2,1,0:T(8,128)S(1)}, u32[]{:S(2)}, u32[]{:S(2)}) collective-permute-start(f32[2,256,256]{2,1,0:T(8,128)S(1)} %get-tuple-element.43.refs_8_.pieces), channel_id=1, source_target_pairs={{0,16},{4,20},{8,24},{12,28},{16,0},{20,4},{24,8},{28,12},{1,17},{... | collective-permute-start | bytes 1572872 | tf_op jit(solution)/shard_map/ppermute | solution.py:434
  6.3 0.1 collective-permute-start.8
  6.5 1.6 %shard_map.155 = (f32[8,128]{1,0:T(8,128)S(1)}, f32[2,3,256]{2,1,0:T(4,128)S(1)}, f32[2,3,256,256]{3,2,1,0:T(8,128)S(1)}, f32[16,128]{1,0:T(8,128)S(1)}) custom-call(s32[2]{0:T(128)} %refs_0_.1, s32[2]{0:T(128)} %refs_1_.1, s32[2]{0:T(128)} %refs_2_.1, f32[2]{0:T(128)} %refs_3_.1, f32[840]{0:T(1024)} %refs_4_.1, f32[40]{0:T(128)} %refs_5_.1, f32[8]{0:T(128)} %refs_6_.1, ...), custom_call_target="tpu_custom_call" | custom-call | flops 1 | bytes 1 | tf_op jit(solution)/shard_map/pallas_call | solution.py:442
  8.1 4.1 %collective-permute-start.3 = (f32[8,128]{1,0:T(8,128)S(1)}, f32[8,128]{1,0:T(8,128)S(1)}, u32[]{:S(2)}, u32[]{:S(2)}) collective-permute-start(f32[8,128]{1,0:T(8,128)S(1)} %get-tuple-element.55.refs_0_), channel_id=1, source_target_pairs={{0,3},{1,2},{2,1},{3,0},{4,7},{5,6},{6,5},{7,4},{8,11},{9,10},{10,... | collective-permute-start | bytes 12296 | tf_op jit(solution)/shard_map/ppermute | solution.py:434
  12.2 0.8 %shard_map.157 = (f32[2,480,256]{2,1,0:T(8,128)S(1)}, f32[2,480,256]{2,1,0:T(8,128)S(1)}) custom-call(s32[1]{0:T(128)} %bitcast.1.d_ref, f32[2,256,256]{2,1,0:T(8,128)S(1)} %get-tuple-element.43.refs_8_.pieces, f32[2,3,256,256]{3,2,1,0:T(8,128)S(1)} %get-tuple-element.52.share_ref), custom_call_target="tpu_custom_call" | custom-call | flops 1 | bytes 1 | tf_op jit(solution)/shard_map/pallas_call | solution.py:442
  13.0 0.0 collective-permute-done
  13.0 2.1 %collective-permute-start.1 = (f32[8,128]{1,0:T(8,128)S(1)}, f32[8,128]{1,0:T(8,128)S(1)}, u32[]{:S(2)}, u32[]{:S(2)}) collective-permute-start(f32[8,128]{1,0:T(8,128)S(1)} %get-tuple-element.55.refs_0_), channel_id=1, source_target_pairs={{0,1},{1,0},{2,3},{3,2},{4,5},{5,4},{6,7},{7,6},{8,9},{9,8},{10,11... | collective-permute-start | bytes 12296 | tf_op jit(solution)/shard_map/ppermute | solution.py:434
  15.1 0.0 collective-permute-start.9
  15.1 1.1 %shard_map.156 = (f32[8,256]{1,0:T(8,128)S(1)}, f32[1,480,256]{2,1,0:T(8,128)S(1)}, f32[1,480,256]{2,1,0:T(8,128)S(1)}) custom-call(s32[1]{0:T(128)} %bitcast.1.d_ref, f32[1,256,256]{2,1,0:T(8,128)S(1)} %bitcast.16, bf16[3840,256]{1,0:T(8,128)(2,1)S(1)} %bitcast.11, bf16[3,256]{1,0:T(4,128)(2,1)S(1)} %copy-done.1), custom_call_target="tpu_custom_call" | custom-call | flops 4000000000 | bytes 1 | tf_op jit(solution)/shard_map/pallas_call | solution.py:442
  16.2 0.5 %collective-permute-done.2.refs_2_ = f32[8,128]{1,0:T(8,128)S(1)} collective-permute-done((f32[8,128]{1,0:T(8,128)S(1)}, f32[8,128]{1,0:T(8,128)S(1)}, u32[]{:S(2)}, u32[]{:S(2)}) %collective-permute-start.2) | collective-permute-done | bytes 4128 | tf_op jit(solution)/shard_map/ppermute | solution.py:434
  16.8 0.0 collective-permute-done.1.refs_1_
  16.8 2.8 %collective-permute-start.6 = (f32[16,128]{1,0:T(8,128)S(1)}, f32[16,128]{1,0:T(8,128)S(1)}, u32[]{:S(2)}, u32[]{:S(2)}) collective-permute-start(f32[16,128]{1,0:T(8,128)S(1)} %shard_map.158.refs_0_.own_facts), channel_id=1, source_target_pairs={{0,24},{4,28},{8,16},{12,20},{16,8},{20,12},{24,0},{28,4},{1,25},{... | collective-permute-start | bytes 24584 | tf_op jit(solution)/shard_map/ppermute | solution.py:434
  19.6 0.6 %collective-permute-start.5 = (f32[16,128]{1,0:T(8,128)S(1)}, f32[16,128]{1,0:T(8,128)S(1)}, u32[]{:S(2)}, u32[]{:S(2)}) collective-permute-start(f32[16,128]{1,0:T(8,128)S(1)} %shard_map.158.refs_0_.own_facts), channel_id=1, source_target_pairs={{0,8},{4,12},{8,0},{12,4},{16,24},{20,28},{24,16},{28,20},{1,9},{5... | collective-permute-start | bytes 24584 | tf_op jit(solution)/shard_map/ppermute | solution.py:434
  20.2 1.2 %collective-permute-done.9 = f32[256,256]{1,0:T(8,128)S(1)} collective-permute-done((f32[256,256]{1,0:T(8,128)S(1)}, f32[256,256]{1,0:T(8,128)S(1)}, u32[]{:S(2)}, u32[]{:S(2)}) %collective-permute-start.9) | collective-permute-done | bytes 262176 | tf_op jit(solution)/shard_map/ppermute | solution.py:434
  21.5 1.5 %collective-permute-start.4 = (f32[16,128]{1,0:T(8,128)S(1)}, f32[16,128]{1,0:T(8,128)S(1)}, u32[]{:S(2)}, u32[]{:S(2)}) collective-permute-start(f32[16,128]{1,0:T(8,128)S(1)} %shard_map.158.refs_0_.own_facts), channel_id=1, source_target_pairs={{0,16},{4,20},{8,24},{12,28},{16,0},{20,4},{24,8},{28,12},{1,17},{... | collective-permute-start | bytes 24584 | tf_op jit(solution)/shard_map/ppermute | solution.py:434
  23.0 1.1 %shard_map.159 = (f32[8,256]{1,0:T(8,128)S(1)}, f32[1,480,256]{2,1,0:T(8,128)S(1)}, f32[1,480,256]{2,1,0:T(8,128)S(1)}) custom-call(s32[1]{0:T(128)} %bitcast.1.d_ref, f32[1,256,256]{2,1,0:T(8,128)S(1)} %bitcast.15, bf16[3840,256]{1,0:T(8,128)(2,1)S(1)} %bitcast.12, bf16[3,256]{1,0:T(4,128)(2,1)S(1)} %copy-done.1, ...), custom_call_target="tpu_custom_call" | custom-call | flops 1 | bytes 1 | tf_op jit(solution)/shard_map/pallas_call | solution.py:442
  24.1 1.1 %shard_map.160 = (f32[8,256]{1,0:T(8,128)S(1)}, f32[1,480,256]{2,1,0:T(8,128)S(1)}, f32[1,480,256]{2,1,0:T(8,128)S(1)}) custom-call(s32[1]{0:T(128)} %bitcast.1.d_ref, f32[2,256,256]{2,1,0:T(8,128)S(1)} %collective-permute-done.7.x_ref.refs_4_, bf16[3840,256]{1,0:T(8,128)(2,1)S(1)} %bitcast.13, bf16[3,256]{1,0:T(4,128)(2,1)S(1)} %copy-done.1, ...), custom_call_target="tpu_custom_call" | custom-call | flops 1 | bytes 1 | tf_op jit(solution)/shard_map/pallas_call | solution.py:442
  25.3 2.6 %shard_map.161 = (f32[480,256]{1,0:T(8,128)S(1)}, f32[496,256]{1,0:T(8,128)S(1)}) custom-call(s32[1]{0:T(128)} %bitcast.1.d_ref, s32[1]{0:T(128)} %bitcast.z_ref, f32[16,128]{1,0:T(8,128)S(1)} %shard_map.158.refs_0_.own_facts, f32[16,128]{1,0:T(8,128)S(1)} %collective-permute-done.4.refs_1_.near_facts, f32[16,128]{1,0:T(8,128)S(1)} %collective-permute-done.5.refs_2_, ...), custom_call_target="tpu_custom_call" | custom-call | flops 1 | bytes 1 | tf_op jit(solution)/shard_map/pallas_call | solution.py:442
  27.8 0.1 collective-permute-start.10
  27.9 0.7 %shard_map.162 = (f32[480,256]{1,0:T(8,128)S(1)}, f32[2]{0:T(128)}) custom-call(s32[1]{0:T(128)} %bitcast.z_ref, f32[480,256]{1,0:T(8,128)S(1)} %get-tuple-element.70.acc, f32[16,128]{1,0:T(8,128)S(1)} %shard_map.158.refs_0_.own_facts, f32[16,128]{1,0:T(8,128)S(1)} %collective-permute-done.6.refs_3_.far_facts, ...), custom_call_target="tpu_custom_call" | custom-call | flops 1 | bytes 1 | tf_op jit(solution)/shard_map/pallas_call | solution.py:442
  28.6 1.2 %collective-permute-done.10.came_ref = f32[496,256]{1,0:T(8,128)S(1)} collective-permute-done((f32[496,256]{1,0:T(8,128)S(1)}, f32[496,256]{1,0:T(8,128)S(1)}, u32[]{:S(2)}, u32[]{:S(2)}) %collective-permute-start.10) | collective-permute-done | bytes 507936 | tf_op jit(solution)/shard_map/ppermute | solution.py:434
  29.8 0.8 %shard_map.163 = (f32[480,256]{1,0:T(8,128)}, f32[3,256]{1,0:T(4,128)}, f32[840]{0:T(1024)}, f32[40]{0:T(128)}, f32[8]{0:T(128)}) custom-call(f32[480,256]{1,0:T(8,128)S(1)} %get-tuple-element.72.own_ref, f32[496,256]{1,0:T(8,128)S(1)} %get-tuple-element.73.mine_ref, f32[496,256]{1,0:T(8,128)S(1)} %collective-permute-done.10.came_ref), custom_call_target="tpu_custom_call" | custom-call | flops 1 | bytes 1 | tf_op jit(solution)/shard_map/pallas_call | solution.py:442
  (12 shorter events, 0.0 us)
Async XLA Ops:
  0.6 5.8 %copy-start = (bf16[256,15,256]{2,0,1:T(8,128)(2,1)S(1)}, bf16[256,15,256]{2,0,1:T(8,128)(2,1)}, u32[]{:S(2)}) copy-start(bf16[256,15,256]{2,0,1:T(8,128)(2,1)} %param.13) | copy-start | bytes 5898244
  0.6 5.8 %copy-start.1 = (bf16[3,256]{1,0:T(4,128)(2,1)S(1)}, bf16[3,256]{1,0:T(4,128)(2,1)}, u32[]{:S(2)}) copy-start(bf16[3,256]{1,0:T(4,128)(2,1)} %refs_15_.1) | copy-start | bytes 4612
  1.9 11.1 %collective-permute-start = (f32[256,256]{1,0:T(8,128)S(1)}, f32[256,256]{1,0:T(8,128)S(1)}, u32[]{:S(2)}, u32[]{:S(2)}) collective-permute-start(f32[256,256]{1,0:T(8,128)S(1)} %get-tuple-element.46), channel_id=1, source_target_pairs={{0,24},{4,28},{8,16},{12,20},{16,8},{20,12},{24,0},{28,4},{1,25},{... | collective-permute-start | bytes 786440 | tf_op jit(solution)/shard_map/ppermute | solution.py:434
  5.8 18.3 %collective-permute-start.7 = (f32[2,256,256]{2,1,0:T(8,128)S(1)}, f32[2,256,256]{2,1,0:T(8,128)S(1)}, u32[]{:S(2)}, u32[]{:S(2)}) collective-permute-start(f32[2,256,256]{2,1,0:T(8,128)S(1)} %get-tuple-element.43.refs_8_.pieces), channel_id=1, source_target_pairs={{0,16},{4,20},{8,24},{12,28},{16,0},{20,4},{24,8},{28,12},{1,17},{... | collective-permute-start | bytes 1572872 | tf_op jit(solution)/shard_map/ppermute | solution.py:434
  6.3 18.9 %collective-permute-start.8 = (f32[2,256,256]{2,1,0:T(8,128)S(1)}, f32[2,256,256]{2,1,0:T(8,128)S(1)}, u32[]{:S(2)}, u32[]{:S(2)}) collective-permute-start(f32[2,256,256]{2,1,0:T(8,128)S(1)} %get-tuple-element.43.refs_8_.pieces), channel_id=1, source_target_pairs={{0,8},{4,12},{8,0},{12,4},{16,24},{20,28},{24,16},{28,20},{1,9},{5... | collective-permute-start | bytes 1572872 | tf_op jit(solution)/shard_map/ppermute | solution.py:434
  8.1 7.0 %collective-permute-start.3 = (f32[8,128]{1,0:T(8,128)S(1)}, f32[8,128]{1,0:T(8,128)S(1)}, u32[]{:S(2)}, u32[]{:S(2)}) collective-permute-start(f32[8,128]{1,0:T(8,128)S(1)} %get-tuple-element.55.refs_0_), channel_id=1, source_target_pairs={{0,3},{1,2},{2,1},{3,0},{4,7},{5,6},{6,5},{7,4},{8,11},{9,10},{10,... | collective-permute-start | bytes 12296 | tf_op jit(solution)/shard_map/ppermute | solution.py:434
  12.2 4.6 %collective-permute-start.2 = (f32[8,128]{1,0:T(8,128)S(1)}, f32[8,128]{1,0:T(8,128)S(1)}, u32[]{:S(2)}, u32[]{:S(2)}) collective-permute-start(f32[8,128]{1,0:T(8,128)S(1)} %get-tuple-element.55.refs_0_), channel_id=1, source_target_pairs={{0,2},{1,3},{2,0},{3,1},{4,6},{5,7},{6,4},{7,5},{8,10},{9,11},{10,... | collective-permute-start | bytes 12296 | tf_op jit(solution)/shard_map/ppermute | solution.py:434
  13.0 3.8 %collective-permute-start.1 = (f32[8,128]{1,0:T(8,128)S(1)}, f32[8,128]{1,0:T(8,128)S(1)}, u32[]{:S(2)}, u32[]{:S(2)}) collective-permute-start(f32[8,128]{1,0:T(8,128)S(1)} %get-tuple-element.55.refs_0_), channel_id=1, source_target_pairs={{0,1},{1,0},{2,3},{3,2},{4,5},{5,4},{6,7},{7,6},{8,9},{9,8},{10,11... | collective-permute-start | bytes 12296 | tf_op jit(solution)/shard_map/ppermute | solution.py:434
  15.1 6.4 %collective-permute-start.9 = (f32[256,256]{1,0:T(8,128)S(1)}, f32[256,256]{1,0:T(8,128)S(1)}, u32[]{:S(2)}, u32[]{:S(2)}) collective-permute-start(f32[256,256]{1,0:T(8,128)S(1)} %collective-permute-done), channel_id=1, source_target_pairs={{0,1},{1,0},{2,3},{3,2},{4,5},{5,4},{6,7},{7,6},{8,9},{9,8},{10,11... | collective-permute-start | bytes 786440 | tf_op jit(solution)/shard_map/ppermute | solution.py:434
  16.8 8.4 %collective-permute-start.6 = (f32[16,128]{1,0:T(8,128)S(1)}, f32[16,128]{1,0:T(8,128)S(1)}, u32[]{:S(2)}, u32[]{:S(2)}) collective-permute-start(f32[16,128]{1,0:T(8,128)S(1)} %shard_map.158.refs_0_.own_facts), channel_id=1, source_target_pairs={{0,24},{4,28},{8,16},{12,20},{16,8},{20,12},{24,0},{28,4},{1,25},{... | collective-permute-start | bytes 24584 | tf_op jit(solution)/shard_map/ppermute | solution.py:434
  19.6 5.6 %collective-permute-start.5 = (f32[16,128]{1,0:T(8,128)S(1)}, f32[16,128]{1,0:T(8,128)S(1)}, u32[]{:S(2)}, u32[]{:S(2)}) collective-permute-start(f32[16,128]{1,0:T(8,128)S(1)} %shard_map.158.refs_0_.own_facts), channel_id=1, source_target_pairs={{0,8},{4,12},{8,0},{12,4},{16,24},{20,28},{24,16},{28,20},{1,9},{5... | collective-permute-start | bytes 24584 | tf_op jit(solution)/shard_map/ppermute | solution.py:434
  21.5 3.8 %collective-permute-start.4 = (f32[16,128]{1,0:T(8,128)S(1)}, f32[16,128]{1,0:T(8,128)S(1)}, u32[]{:S(2)}, u32[]{:S(2)}) collective-permute-start(f32[16,128]{1,0:T(8,128)S(1)} %shard_map.158.refs_0_.own_facts), channel_id=1, source_target_pairs={{0,16},{4,20},{8,24},{12,28},{16,0},{20,4},{24,8},{28,12},{1,17},{... | collective-permute-start | bytes 24584 | tf_op jit(solution)/shard_map/ppermute | solution.py:434
  27.8 2.0 %collective-permute-start.10 = (f32[496,256]{1,0:T(8,128)S(1)}, f32[496,256]{1,0:T(8,128)S(1)}, u32[]{:S(2)}, u32[]{:S(2)}) collective-permute-start(f32[496,256]{1,0:T(8,128)S(1)} %get-tuple-element.73.mine_ref), channel_id=1, source_target_pairs={{0,4},{4,0},{8,12},{12,8},{16,20},{20,16},{24,28},{28,24},{1,5},{5... | collective-permute-start | bytes 1523720 | tf_op jit(solution)/shard_map/ppermute | solution.py:434
